TPU v7x, 32 devices: a whole 2x2x4 slice. The times are simulated.
32 devices in a mesh: row: 4 (over x, core), col: 8 (over z, y).
Axes of the slice: x: 2, y: 2, z: 4, core: 2. Of those that a mesh axis runs over, the one named last changes fastest.
Arguments:
- tokens: bfloat16 [8, 768, 1024], P('col', 'row'), may hold values from -6 to 6
- gain_one: float32 [768], replicated, may hold values from 0.5 to 1.5
- gain_two: float32 [768], replicated, may hold values from 0.5 to 1.5
- w_query: bfloat16 [768, 768], P('row', 'col'), may hold values from -0.21875 to 0.21875
- w_key: bfloat16 [768, 768], P('row', 'col'), may hold values from -0.21875 to 0.21875
- w_value: bfloat16 [768, 768], P('row', 'col'), may hold values from -0.21875 to 0.21875
- w_out: bfloat16 [768, 768], P('row', 'col'), may hold values from -3.5 to 3.5
- w_router: bfloat16 [768, 32], P('row', 'col'), may hold values from -0.15625 to 0.15625
- w_in: bfloat16 [768, 98304], P('row', 'col'), may hold values from -0.21875 to 0.21875
- w_expert_out: bfloat16 [3072, 24576], P('row', 'col'), may hold values from -3.5 to 3.5
- bias_table: float32 [32, 12], replicated, may hold values from -4 to 4
- segment: int32 [8, 1024], P('col'), may hold values from 0 to 3, never falling along the last dimension, each value on 1 to 768 neighbouring positions
- expert: int32 [8, 1024, 1], P('col'), may hold values from 0 to 31; in each aligned block of 1024 rows (0 to 1023, 1024 to 2047, ..., all dimensions but the last counted through in order) at most 48 rows name the same one
- bucket: int32 [8, 1024, 1024], P('col', 'row'), may hold values from 0 to 31
- cotangent: bfloat16 [8, 768, 1024], P('col', 'row'), may hold values from -6 to 6
Outputs:
- layer_out: bfloat16 [8, 768, 1024], P('col', 'row')
- grad_tokens: bfloat16 [8, 768, 1024], P('col', 'row')
- grad_gain_one: float32 [768], replicated
- grad_gain_two: float32 [768], replicated
- grad_query: float32 [768, 768], P('row', 'col')
- grad_key: float32 [768, 768], P('row', 'col')
- grad_value: float32 [768, 768], P('row', 'col')
- grad_out: float32 [768, 768], P('row', 'col')
- grad_router: float32 [768, 32], P('row', 'col')
- grad_in: float32 [768, 98304], P('row', 'col')
- grad_expert_out: float32 [3072, 24576], P('row', 'col')
- grad_table: float32 [32, 12], replicated
Inputs may be any that keep to these rules, and one draw needn't show every extreme that they name: Within a sequence at most 48 tokens name the same expert. `segment`: never falls along a sequence.
All inputs are finite; a program needn't handle non-finite values.
Results may differ from a plain program's by a relative error of at most 0.014.
Values may be sent and summed in bfloat16 or wider, within the bound.
No kernel may reach another device: no remote copies, remote signals or barrier semaphores. Data moves between devices by JAX's collectives and lax.ppermute only.
A program may use at most 448 MiB of HBM per device.

v0:
```python
import jax
import jax.numpy as jnp
from jax import lax
from jax.sharding import PartitionSpec as P

EXPERTS = 32
CAPACITY = 48


NORM_EPS = 1e-06
NEG_FILL = -1e30


def row_totals(partial_values):
    return lax.psum(partial_values, "row")


def feature_split(partial_rows):
    return lax.psum_scatter(partial_rows, "row", scatter_dimension=1, tiled=True)


def feature_join(rows_low):
    return lax.all_gather(rows_low, "row", axis=1, tiled=True)


def norm_back(grad_normed, inputs_f, inverse_rms, gain_part, model_width):
    inner_sum = row_totals(jnp.sum(gain_part * grad_normed * inputs_f, axis=1))
    return (
        inverse_rms[:, None] * gain_part * grad_normed
        - inputs_f * (inverse_rms**3 / model_width * inner_sum)[:, None]
    )


def block_scores(
    query_heads, keys_all, bucket_rows, query_docs, doc_ids, bias_table, number, key_block
):
    head_count = bias_table.shape[1]
    head_dim = query_heads.shape[2]
    offset = number * key_block
    key_rows = lax.dynamic_slice_in_dim(keys_all, offset, key_block, 0).reshape(
        key_block, head_count, head_dim
    )
    bucket_cols = lax.dynamic_slice_in_dim(bucket_rows, offset, key_block, 1)
    key_docs = lax.dynamic_slice_in_dim(doc_ids, offset, key_block, 0)
    raw_scores = jnp.einsum(
        "ihd,jhd->hij", query_heads, key_rows, preferred_element_type=jnp.float32
    ) * head_dim ** (-0.5)
    one_hot = (bucket_cols[:, :, None] == jnp.arange(bias_table.shape[0], dtype=jnp.int32)).astype(
        jnp.float32
    )
    pair_bias = jnp.einsum("ijb,bh->hij", one_hot, bias_table, precision=lax.Precision.HIGHEST)
    allowed = (query_docs[:, None] == key_docs[None, :])[None]
    return (raw_scores + pair_bias, allowed, one_hot)


def attend(query_heads, keys_all, values_all, bucket_rows, query_docs, doc_ids, bias_table):
    tok_rows, head_count, head_dim = query_heads.shape
    seq_len = keys_all.shape[0]
    key_block = min(seq_len, 512)
    blocks = seq_len // key_block

    def first_pass(status, number):
        row_peak, row_total = status
        scores, allowed, one_hot = block_scores(
            query_heads, keys_all, bucket_rows, query_docs, doc_ids, bias_table, number, key_block
        )
        masked = jnp.where(allowed, scores, NEG_FILL)
        new_peak = jnp.maximum(row_peak, jnp.max(masked, axis=2))
        weights = jnp.where(allowed, jnp.exp(masked - new_peak[:, :, None]), 0.0)
        row_total = row_total * jnp.exp(row_peak - new_peak) + jnp.sum(weights, axis=2)
        return ((new_peak, row_total), None)

    start_status = (
        jnp.full((head_count, tok_rows), NEG_FILL, jnp.float32),
        jnp.zeros((head_count, tok_rows), jnp.float32),
    )
    (row_peak, row_total), unused = lax.scan(first_pass, start_status, jnp.arange(blocks))
    log_total = row_peak + jnp.log(row_total)

    def second_pass(running, number):
        scores, allowed, one_hot = block_scores(
            query_heads, keys_all, bucket_rows, query_docs, doc_ids, bias_table, number, key_block
        )
        soft_weights = jnp.where(allowed, jnp.exp(scores - log_total[:, :, None]), 0.0).astype(
            jnp.bfloat16
        )
        value_rows = lax.dynamic_slice_in_dim(values_all, number * key_block, key_block, 0).reshape(
            key_block, head_count, head_dim
        )
        return (
            running
            + jnp.einsum(
                "hij,jhd->ihd", soft_weights, value_rows, preferred_element_type=jnp.float32
            ),
            None,
        )

    start_acc = jnp.zeros((tok_rows, head_count, head_dim), jnp.float32)
    attended, unused = lax.scan(second_pass, start_acc, jnp.arange(blocks))
    return (attended, log_total)


def attend_back(
    query_heads,
    keys_all,
    values_all,
    bucket_rows,
    query_docs,
    doc_ids,
    bias_table,
    log_total,
    grad_heads,
    grad_dot,
):
    tok_rows, head_count, head_dim = query_heads.shape
    seq_len = keys_all.shape[0]
    model_width = head_count * head_dim
    key_block = min(seq_len, 512)
    blocks = seq_len // key_block
    scaling = head_dim ** (-0.5)

    def step_back(status, number):
        grad_query, grad_table = status
        scores, allowed, one_hot = block_scores(
            query_heads, keys_all, bucket_rows, query_docs, doc_ids, bias_table, number, key_block
        )
        key_rows = lax.dynamic_slice_in_dim(keys_all, number * key_block, key_block, 0).reshape(
            key_block, head_count, head_dim
        )
        value_rows = lax.dynamic_slice_in_dim(values_all, number * key_block, key_block, 0).reshape(
            key_block, head_count, head_dim
        )
        soft_weights = jnp.where(allowed, jnp.exp(scores - log_total[:, :, None]), 0.0)
        weights_low = soft_weights.astype(jnp.bfloat16)
        grad_soft = jnp.einsum(
            "ihd,jhd->hij", grad_heads, value_rows, preferred_element_type=jnp.float32
        )
        grad_scores = soft_weights * (grad_soft - grad_dot[:, :, None])
        grad_table = grad_table + jnp.einsum(
            "ijb,hij->bh", one_hot, grad_scores, precision=lax.Precision.HIGHEST
        )
        scores_low = grad_scores.astype(jnp.bfloat16)
        grad_query = grad_query + scaling * jnp.einsum(
            "hij,jhd->ihd", scores_low, key_rows, preferred_element_type=jnp.float32
        )
        grad_key = scaling * jnp.einsum(
            "hij,ihd->jhd", scores_low, query_heads, preferred_element_type=jnp.float32
        )
        grad_value = jnp.einsum(
            "hij,ihd->jhd", weights_low, grad_heads, preferred_element_type=jnp.float32
        )
        stacked = jnp.concatenate(
            [grad_key.reshape(key_block, model_width), grad_value.reshape(key_block, model_width)],
            axis=1,
        )
        return ((grad_query, grad_table), stacked)

    start_status = (
        jnp.zeros((tok_rows, head_count, head_dim), jnp.float32),
        jnp.zeros(bias_table.shape, jnp.float32),
    )
    (grad_query, grad_table), kv_terms = lax.scan(step_back, start_status, jnp.arange(blocks))
    return (grad_query, grad_table, kv_terms.reshape(seq_len, 2 * model_width))


def on_device(
    tokens,
    gain_one,
    gain_two,
    w_query,
    w_key,
    w_value,
    w_out,
    w_router,
    w_in,
    w_expert_out,
    bias_table,
    segment,
    expert,
    bucket,
    cotangent,
):
    seq_len = tokens.shape[2]
    dim_rows = tokens.shape[1]
    row_count = lax.axis_size("row")
    model_width = dim_rows * row_count
    tok_rows = seq_len // row_count
    experts = EXPERTS
    hid_rows = w_expert_out.shape[0]
    ffn_width = hid_rows * row_count
    head_count = bias_table.shape[1]
    head_dim = model_width // head_count
    row_index = lax.axis_index("row")
    gathered = (
        lax.all_gather(w_query, "col", axis=1, tiled=True),
        lax.all_gather(w_key, "col", axis=1, tiled=True),
        lax.all_gather(w_value, "col", axis=1, tiled=True),
        lax.all_gather(w_out, "col", axis=1, tiled=True),
        lax.all_gather(w_router, "col", axis=1, tiled=True),
        lax.all_gather(w_in, "col", axis=1, tiled=True),
        lax.all_gather(w_expert_out, "col", axis=1, tiled=True),
    )
    query_full, key_full, value_full, out_proj_full, router_full, in_flat, out_flat = gathered
    in_full = in_flat.reshape(dim_rows, experts, ffn_width)
    out_full = out_flat.reshape(hid_rows, experts, model_width)
    stacked_weights = jnp.concatenate([query_full, key_full, value_full], axis=1)
    tok_float = jnp.transpose(tokens[0].astype(jnp.float32))
    doc_ids = segment[0]
    query_docs = lax.dynamic_slice_in_dim(doc_ids, row_index * tok_rows, tok_rows, 0)
    bucket_rows = bucket[0]
    expert_ids = expert[0, :, 0]
    gain_part_one = lax.dynamic_slice_in_dim(gain_one, row_index * dim_rows, dim_rows, 0)
    gain_part_two = lax.dynamic_slice_in_dim(gain_two, row_index * dim_rows, dim_rows, 0)
    inverse_one = lax.rsqrt(
        row_totals(jnp.sum(tok_float * tok_float, axis=1)) / model_width + NORM_EPS
    )
    normed_one = (tok_float * inverse_one[:, None] * gain_part_one).astype(jnp.bfloat16)
    projected = lax.psum_scatter(
        jnp.dot(normed_one, stacked_weights, preferred_element_type=jnp.float32),
        "row",
        scatter_dimension=0,
        tiled=True,
    ).astype(jnp.bfloat16)
    queries_low = projected[:, :model_width]
    keys_low = projected[:, model_width : 2 * model_width]
    values_low = projected[:, 2 * model_width :]
    keys_all, values_all = (
        lax.all_gather(keys_low, "row", axis=0, tiled=True),
        lax.all_gather(values_low, "row", axis=0, tiled=True),
    )
    query_heads = queries_low.reshape(tok_rows, head_count, head_dim)
    attended, log_total = attend(
        query_heads, keys_all, values_all, bucket_rows, query_docs, doc_ids, bias_table
    )
    attn_low = attended.reshape(tok_rows, model_width).astype(jnp.bfloat16)
    heads_home = lax.all_to_all(attn_low, "row", split_axis=1, concat_axis=0, tiled=True)
    attn_rows = feature_split(
        jnp.dot(heads_home, out_proj_full, preferred_element_type=jnp.float32)
    )
    residual = tok_float + attn_rows
    inverse_two = lax.rsqrt(
        row_totals(jnp.sum(residual * residual, axis=1)) / model_width + NORM_EPS
    )
    normed_two = (residual * inverse_two[:, None] * gain_part_two).astype(jnp.bfloat16)
    logits = row_totals(jnp.dot(normed_two, router_full, preferred_element_type=jnp.float32))
    gate_probs = jax.nn.softmax(logits, axis=1)
    picked = (expert_ids[:, None] == jnp.arange(experts, dtype=jnp.int32)[None, :]).astype(
        jnp.int32
    )
    picked_float = picked.astype(jnp.float32)
    slot_rank = jnp.sum((jnp.cumsum(picked, axis=0) - 1) * picked, axis=1)
    slot_index = expert_ids * CAPACITY + slot_rank
    token_gate = jnp.sum(gate_probs * picked_float, axis=1)
    slots_in = (
        jnp.zeros((experts * CAPACITY, dim_rows), jnp.bfloat16).at[slot_index].set(normed_two)
    )
    slots_own = slots_in.reshape(experts, CAPACITY, dim_rows)
    lead_count = slots_own.shape[0]
    slot_count = slots_own.shape[1]
    pre_partial = jnp.einsum("ecd,def->ecf", slots_own, in_full, preferred_element_type=jnp.float32)
    pre_act = feature_split(pre_partial.reshape(lead_count * slot_count, ffn_width))
    hidden = jax.nn.gelu(pre_act).astype(jnp.bfloat16)
    hidden_three = hidden.reshape(lead_count, slot_count, hid_rows)
    out_partial = jnp.einsum(
        "ecf,fed->ecd", hidden_three, out_full, preferred_element_type=jnp.float32
    )
    expert_local = feature_split(out_partial.reshape(lead_count * slot_count, model_width))
    expert_tok = expert_local[slot_index]
    layer_out = (residual + token_gate[:, None] * expert_tok).astype(jnp.bfloat16)
    grad_final = jnp.transpose(cotangent[0].astype(jnp.float32))
    grad_gate = row_totals(jnp.sum(grad_final * expert_tok, axis=1))
    grad_expert_tok = (token_gate[:, None] * grad_final).astype(jnp.bfloat16)
    grad_slots = (
        jnp.zeros((experts * CAPACITY, dim_rows), jnp.bfloat16).at[slot_index].set(grad_expert_tok)
    )
    grad_slots_local = grad_slots.reshape(experts, CAPACITY, dim_rows)
    grad_slots_full = feature_join(
        grad_slots_local.reshape(lead_count * slot_count, dim_rows)
    ).reshape(lead_count, slot_count, model_width)
    grad_hidden = jnp.einsum(
        "ecd,fed->ecf", grad_slots_full, out_full, preferred_element_type=jnp.float32
    )
    grad_out_weight = jnp.einsum(
        "ecf,ecd->fed", hidden_three, grad_slots_full, preferred_element_type=jnp.float32
    )
    unused, gelu_back = jax.vjp(jax.nn.gelu, pre_act)
    grad_pre = gelu_back(grad_hidden.reshape(lead_count * slot_count, hid_rows))[0].astype(
        jnp.bfloat16
    )
    grad_pre_full = feature_join(grad_pre).reshape(lead_count, slot_count, ffn_width)
    grad_slots_in = jnp.einsum(
        "ecf,def->ecd", grad_pre_full, in_full, preferred_element_type=jnp.float32
    )
    grad_in_weight = jnp.einsum(
        "ecd,ecf->def", slots_own, grad_pre_full, preferred_element_type=jnp.float32
    )
    grad_logits = ((grad_gate * token_gate)[:, None] * (picked_float - gate_probs)).astype(
        jnp.bfloat16
    )
    router_back = lax.dot_general(
        grad_logits, router_full, (((1,), (1,)), ((), ())), preferred_element_type=jnp.float32
    )
    grad_normed_two = grad_slots_in.reshape(experts * CAPACITY, dim_rows)[slot_index] + router_back
    grad_router = lax.dot_general(
        normed_two, grad_logits, (((0,), (0,)), ((), ())), preferred_element_type=jnp.float32
    )
    grad_res = grad_final + norm_back(
        grad_normed_two, residual, inverse_two, gain_part_two, model_width
    )
    grad_gain_two = jnp.sum(grad_normed_two * residual * inverse_two[:, None], axis=0)
    grad_attn_full = feature_join(grad_res.astype(jnp.bfloat16))
    grad_heads_home = lax.dot_general(
        grad_attn_full, out_proj_full, (((1,), (1,)), ((), ())), preferred_element_type=jnp.float32
    ).astype(jnp.bfloat16)
    grad_out_proj = lax.dot_general(
        heads_home, grad_attn_full, (((0,), (0,)), ((), ())), preferred_element_type=jnp.float32
    )
    grad_attn = lax.all_to_all(grad_heads_home, "row", split_axis=0, concat_axis=1, tiled=True)
    grad_heads = grad_attn.reshape(tok_rows, head_count, head_dim)
    grad_dot = jnp.einsum("ihd,ihd->hi", grad_heads.astype(jnp.float32), attended)
    grad_query, grad_table, kv_terms = attend_back(
        query_heads,
        keys_all,
        values_all,
        bucket_rows,
        query_docs,
        doc_ids,
        bias_table,
        log_total,
        grad_heads,
        grad_dot,
    )
    key_value_grads = lax.psum_scatter(kv_terms, "row", scatter_dimension=0, tiled=True)
    grad_qkv = jnp.concatenate(
        [
            grad_query.reshape(tok_rows, model_width).astype(jnp.bfloat16),
            key_value_grads.astype(jnp.bfloat16),
        ],
        axis=1,
    )
    portion = lax.all_gather(grad_qkv, "row", axis=0, tiled=True)
    grad_part = lax.dot_general(
        portion, stacked_weights, (((1,), (1,)), ((), ())), preferred_element_type=jnp.float32
    )
    grad_weights = lax.dot_general(
        normed_one, portion, (((0,), (0,)), ((), ())), preferred_element_type=jnp.float32
    )
    grad_input = grad_res + norm_back(grad_part, tok_float, inverse_one, gain_part_one, model_width)
    grad_gain_one = jnp.sum(grad_part * tok_float * inverse_one[:, None], axis=0)
    summed = (
        lax.psum_scatter(grad_weights[:, :model_width], "col", scatter_dimension=1, tiled=True),
        lax.psum_scatter(
            grad_weights[:, model_width : 2 * model_width], "col", scatter_dimension=1, tiled=True
        ),
        lax.psum_scatter(
            grad_weights[:, 2 * model_width :], "col", scatter_dimension=1, tiled=True
        ),
        lax.psum_scatter(grad_out_proj, "col", scatter_dimension=1, tiled=True),
        lax.psum_scatter(grad_router, "col", scatter_dimension=1, tiled=True),
        lax.psum_scatter(
            grad_in_weight.reshape(dim_rows, experts * ffn_width),
            "col",
            scatter_dimension=1,
            tiled=True,
        ),
        lax.psum_scatter(
            grad_out_weight.reshape(hid_rows, experts * model_width),
            "col",
            scatter_dimension=1,
            tiled=True,
        ),
    )
    grad_query_w, grad_key_w, grad_value_w, grad_out_w, grad_router_w, grad_in_w, grad_expert_w = (
        summed
    )
    place_one = lax.dynamic_update_slice_in_dim(
        jnp.zeros((model_width,), jnp.float32), grad_gain_one, row_index * dim_rows, 0
    )
    place_two = lax.dynamic_update_slice_in_dim(
        jnp.zeros((model_width,), jnp.float32), grad_gain_two, row_index * dim_rows, 0
    )
    gain_one_grad, gain_two_grad, table_grad = lax.psum(
        (place_one, place_two, grad_table), ("row", "col")
    )
    layer_out_t = jnp.transpose(layer_out)[None]
    grad_input_t = jnp.transpose(grad_input.astype(jnp.bfloat16))[None]
    return (
        layer_out_t,
        grad_input_t,
        gain_one_grad,
        gain_two_grad,
        grad_query_w,
        grad_key_w,
        grad_value_w,
        grad_out_w,
        grad_router_w,
        grad_in_w,
        grad_expert_w,
        table_grad,
    )


def solution(mesh):
    return jax.shard_map(
        on_device,
        mesh=mesh,
        in_specs=(
            P("col", "row", None),
            P(),
            P(),
            P("row", "col"),
            P("row", "col"),
            P("row", "col"),
            P("row", "col"),
            P("row", "col"),
            P("row", "col"),
            P("row", "col"),
            P(),
            P("col", None),
            P("col", None, None),
            P("col", "row", None),
            P("col", "row", None),
        ),
        out_specs=(
            P("col", "row", None),
            P("col", "row", None),
            P(),
            P(),
            P("row", "col"),
            P("row", "col"),
            P("row", "col"),
            P("row", "col"),
            P("row", "col"),
            P("row", "col"),
            P("row", "col"),
            P(),
        ),
        check_vma=False,
    )
```

profile of v0, /device:TPU:25, one launch (start us, length us, event | category | flops | bytes accessed | tf_op | source)
XLA Modules:
  0.0 4934.9 jit_solution(7491941516581088649)
XLA Ops:
  18.2 22.1 all_gather.41
  40.3 25.3 all_gather.40
  65.6 25.2 all_gather.39
  97.5 100.5 %reduce-scatter.22.cloned.1.call-done = f32[256,2304]{1,0:T(8,128)} async-done(((f32[1024,2304]{1,0:T(8,128)}), f32[256,2304]{1,0:T(8,128)}) %reduce-scatter.22.cloned.1.call-update) | async-done | bytes 2359312 | tf_op jit(solution)/shard_map/reduce_scatter | solution.py:218
  223.8 53.8 %while.39 = (s32[]{:T(128)}, f32[12,256]{1,0:T(8,128)S(1)}, f32[12,256]{1,0:T(8,128)S(1)}, s32[256]{0:T(256)}, s32[2]{0:T(128)S(1)}, /*index=5*/s32[1024]{0:T(10...) while((s32[]{:T(128)}, f32[12,256]{1,0:T(8,128)S(1)}, ...), condition=%wide.region_6.7_spmd.clone, body=%wide.region_3.6_spmd.clone.sunk | while | flops 820657152 | bytes 42635992 | solution.py:77
  280.8 53.7 %while.40 = (s32[]{:T(128)}, f32[256,12,64]{0,2,1:T(8,128)S(1)}, s32[2]{0:T(128)S(1)}, bf16[1024,768]{0,1:T(8,128)(2,1)}, s32[256]{0:T(256)}, /*index=5*/s32[102...) while((s32[]{:T(128)}, f32[256,12,64]{0,2,1:T(8,128)S(1)}, ...), condition=%wide.region_8.9_spmd.clone, body=%wide.region_7.8_spmd.clone.sunk | while | flops 1019215872 | bytes 33706724 | solution.py:99
  339.4 22.4 all_gather.44
  386.4 26.1 reduce-scatter.24.cloned.1.call-done
  475.3 665.5 %all-gather.14.cloned.1.call-done = bf16[192,98304]{1,0:T(8,128)(2,1)} async-done(((bf16[192,12288]{1,0:T(8,128)(2,1)}), bf16[192,98304]{1,0:T(8,128)(2,1)}) %all-gather.14.cloned.1.call-update) | async-done | bytes 37748752 | tf_op jit(solution)/shard_map/all_gather | solution.py:200
  1140.7 21.7 fusion.55
  1170.5 714.7 %all-gather.16.cloned.1.call-done = bf16[768,24576]{0,1:T(8,128)(2,1)} async-done(((bf16[768,3072]{0,1:T(8,128)(2,1)}), bf16[768,24576]{0,1:T(8,128)(2,1)}) %all-gather.16.cloned.1.call-update) | async-done | bytes 37748752 | tf_op jit(solution)/shard_map/all_gather | solution.py:201
  1935.1 46.9 reduce-scatter.34.cloned.1.call-done
  1996.4 51.9 %all-gather.20.cloned.1.call-done = bf16[1536,3072]{1,0:T(8,128)(2,1)} async-done(((bf16[1536,768]{1,0:T(8,128)(2,1)}), bf16[1536,3072]{1,0:T(8,128)(2,1)}) %all-gather.20.cloned.1.call-update) | async-done | bytes 9437200 | tf_op jit(solution)/shard_map/all_gather | solution.py:23
  2119.7 124.5 %while.41 = (s32[]{:T(128)}, f32[256,12,64]{0,2,1:T(8,128)}, f32[32,12]{0,1:T(8,128)S(1)}, f32[2,512,1536]{2,1,0:T(8,128)}, s32[2]{0:T(128)}, /*index=5*/bf16[10...) while((s32[]{:T(128)}, f32[256,12,64]{0,2,1:T(8,128)}, ...), condition=%wide.region_28.29_spmd.clone, body=%wide.region_27.28_spmd.clone.sunk | while | flops 2239038208 | bytes 142118736 | solution.py:162
  2245.8 57.1 %reduce-scatter.28.cloned.1.call-done = f32[256,1536]{1,0:T(8,128)} async-done(((f32[1024,1536]{1,0:T(8,128)}), f32[256,1536]{1,0:T(8,128)}) %reduce-scatter.28.cloned.1.call-update) | async-done | bytes 1572880 | tf_op jit(solution)/shard_map/reduce_scatter | solution.py:333
  2307.1 36.4 all-gather.24.cloned.1.call-done
  2352.8 28.8 fusion.117
  2381.6 73.2 %copy.146 = f32[768,24576]{1,0:T(8,128)} copy(f32[768,24576]{0,1:T(8,128)} %bitcast.44) | data formatting | bytes 150994944 | tf_op jit(solution)/shard_map/reshape | solution.py:367
  2455.9 29.5 convolution_bitcast_fusion
  2485.5 49.6 %copy.184 = f32[32,24,8,3072]{3,2,0,1:T(8,128)} copy(f32[32,24,8,3072]{3,2,1,0:T(8,128)} %convolution_bitcast_fusion) | data formatting | bytes 150994944 | tf_op jit(solution)/shard_map/reshape | solution.py:361
  2537.2 26.8 all-reduce
  2572.2 51.1 %all-reduce.1 = (f32[768]{0:T(1024)}, f32[768]{0:T(1024)}, f32[32,12]{0,1:T(8,128)}) all-reduce(f32[768]{0:T(1024)S(1)} %dynamic_update_slice.10, f32[768]{0:T(1024)S(1)} %dynamic_update_slice.11, f32[32,12]{0,1:T(8,128)S(1)} %copy-done.31), channel_id=1, replica_groups=mesh['row'=4,'col'=8] {'row','col'}, use_global_device_ids=true, to_apply=%region_33.34 | all-reduce | flops 1920 | bytes 15360 | tf_op jit(solution)/shard_map/psum | solution.py:382
  2636.4 1111.2 %reduce-scatter.32.cloned.1.call-done = f32[768,3072]{1,0:T(8,128)} async-done(((f32[768,24576]{1,0:T(8,128)}), f32[768,3072]{1,0:T(8,128)}) %reduce-scatter.32.cloned.1.call-update) | async-done | bytes 9437200 | tf_op jit(solution)/shard_map/reduce_scatter | solution.py:366
  3747.6 1179.7 %reduce-scatter.30.cloned.1.call-done = f32[192,12288]{1,0:T(8,128)} async-done(((f32[192,98304]{1,0:T(8,128)}), f32[192,12288]{1,0:T(8,128)}) %reduce-scatter.30.cloned.1.call-update) | async-done | bytes 9437200 | tf_op jit(solution)/shard_map/reduce_scatter | solution.py:360
  (366 shorter events, 546.7 us)
Async XLA Ops:
  8.0 190.0 %reduce-scatter.22.cloned.1.call-start = ((), (), s32[]{:S(2)}) async-start(), calls=%async_computation.13 | async-start | bytes 11796480 | tf_op jit(solution)/shard_map/reduce_scatter | solution.py:218
  97.5 123.6 %all-gather.12.cloned.1.call-start = ((), (), s32[]{:S(2)}) async-start(), calls=%async_computation.15 | async-start | bytes 1966080 | tf_op jit(solution)/shard_map/all_gather | solution.py:228
  200.8 77.4 %all-gather.10.cloned.1.call-start = ((), (), s32[]{:S(2)}) async-start(), calls=%async_computation.14 | async-start | bytes 1966080 | tf_op jit(solution)/shard_map/all_gather | solution.py:229
  335.4 26.4 all-to-all-start
  339.3 73.1 %reduce-scatter.24.cloned.1.call-start = ((), (), s32[]{:S(2)}) async-start(), calls=%async_computation.16 | async-start | bytes 3932160 | tf_op jit(solution)/shard_map/reduce_scatter | solution.py:19
  365.0 87.8 %all-reduce.4.cloned.1.call-start = ((), (), s32[]{:S(2)}) async-start(), calls=%async_computation.17 | async-start | bytes 262144 | tf_op jit(solution)/shard_map/psum | solution.py:15
  413.7 1668.5 %copy-start.5 = (f32[1024,192]{0,1:T(8,128)}, f32[1024,192]{0,1:T(8,128)S(1)}, u32[]{:S(2)}) copy-start(f32[1024,192]{0,1:T(8,128)S(1)} %get-tuple-element.548) | copy-start | bytes 2359300
  420.0 1662.2 %copy-start.36 = (f32[1024]{0:T(1024)}, f32[1024]{0:T(1024)S(1)}, u32[]{:S(2)}) copy-start(f32[1024]{0:T(1024)S(1)} %add_rsqrt_fusion) | copy-start | bytes 12292
  421.0 719.7 %all-gather.14.cloned.1.call-start = ((), (), s32[]{:S(2)}) async-start(), calls=%async_computation.18 | async-start | bytes 42467328 | tf_op jit(solution)/shard_map/all_gather | solution.py:200
  421.6 745.4 %all-gather.18.cloned.1.call-start = ((), (), s32[]{:S(2)}) async-start(), calls=%async_computation.21 | async-start | bytes 2949120 | tf_op jit(solution)/shard_map/all_gather | solution.py:23
  463.1 1422.1 %all-gather.16.cloned.1.call-start = ((), (), s32[]{:S(2)}) async-start(), calls=%async_computation.20 | async-start | bytes 42467328 | tf_op jit(solution)/shard_map/all_gather | solution.py:201
  469.8 1431.8 %reduce-scatter.26.cloned.1.call-start = ((), (), s32[]{:S(2)}) async-start(), calls=%async_computation.19 | async-start | bytes 23592960 | tf_op jit(solution)/shard_map/reduce_scatter | solution.py:19
  1162.5 819.5 %reduce-scatter.34.cloned.1.call-start = ((), (), s32[]{:S(2)}) async-start(), calls=%async_computation.28 | async-start | bytes 5898240
  1934.3 114.1 %all-gather.20.cloned.1.call-start = ((), (), s32[]{:S(2)}) async-start(), calls=%async_computation.22 | async-start | bytes 11796480 | tf_op jit(solution)/shard_map/all_gather | solution.py:23
  1935.0 170.4 %all-gather.22.cloned.1.call-start = ((), (), s32[]{:S(2)}) async-start(), calls=%async_computation.23 | async-start | bytes 1966080 | tf_op jit(solution)/shard_map/all_gather | solution.py:23
  2108.2 10.3 all-to-all-start.1
  2111.9 191.0 %reduce-scatter.28.cloned.1.call-start = ((), (), s32[]{:S(2)}) async-start(), calls=%async_computation.24 | async-start | bytes 7864320 | tf_op jit(solution)/shard_map/reduce_scatter | solution.py:333
  2244.2 99.3 %all-gather.24.cloned.1.call-start = ((), (), s32[]{:S(2)}) async-start(), calls=%async_computation.25 | async-start | bytes 5898240 | tf_op jit(solution)/shard_map/all_gather | solution.py:341
  2305.5 259.3 %reduce-scatter.42.cloned.1.call-start = ((), (), s32[]{:S(2)}) async-start(), calls=%async_computation.32 | async-start | bytes 884736
  2307.1 324.4 %reduce-scatter.40.cloned.1.call-start = ((), (), s32[]{:S(2)}) async-start(), calls=%async_computation.31 | async-start | bytes 884736
  2350.3 282.9 %reduce-scatter.38.cloned.1.call-start = ((), (), s32[]{:S(2)}) async-start(), calls=%async_computation.30 | async-start | bytes 884736
  2351.5 283.3 %reduce-scatter.36.cloned.1.call-start = ((), (), s32[]{:S(2)}) async-start(), calls=%async_computation.29 | async-start | bytes 884736
  2352.8 1394.9 %reduce-scatter.32.cloned.1.call-start = ((), (), s32[]{:S(2)}) async-start(), calls=%async_computation.27 | async-start | bytes 84934656 | tf_op jit(solution)/shard_map/reduce_scatter | solution.py:366
  2454.8 2472.5 %reduce-scatter.30.cloned.1.call-start = ((), (), s32[]{:S(2)}) async-start(), calls=%async_computation.26 | async-start | bytes 84934656 | tf_op jit(solution)/shard_map/reduce_scatter | solution.py:360
  (64 other events, 3629.5 us)
Sparse Core Ops, SparseCore 0:
  97.6 100.4 reduce-scatter.21
  200.9 20.0 all-gather.11
  223.2 19.6 all-gather.9
  365.1 47.2 reduce-scatter.23
  421.1 31.5 all-reduce.3
  1162.6 139.1 reduce-scatter.25
  1934.4 47.5 reduce-scatter.33
  1983.6 64.7 all-gather.19
  2084.0 21.3 all-gather.21
  2244.3 58.5 reduce-scatter.27
  2305.6 37.8 all-gather.23
Sparse Core Ops, SparseCore 1:
  423.0 717.7 all-gather.13
  1142.8 24.1 all-gather.17
  1169.0 716.1 all-gather.15
  2309.9 59.7 reduce-scatter.41
  2373.0 61.6 reduce-scatter.39
  2438.3 61.6 reduce-scatter.37
  2503.1 61.6 reduce-scatter.35
  2569.6 1178.0 reduce-scatter.31
  3751.9 1175.3 reduce-scatter.29
where the time goes:
time: 4940 us; the launch traced here: 4930 us
  waiting for transfers between devices  4060 us (82%)
  local copies, waits for them, and re-layouts  305 us (6%)
  matrix products  268 us (5%)
  blocking collectives  222 us (4%)
    reduce_scatter x1, waiting for transfers between devices, on_device(): lax.psum_scatter(grad_in_weight.reshape(dim_rows, experts * ffn_width), '...  1180 us
    reduce_scatter x1, waiting for transfers between devices, on_device(): lax.psum_scatter(grad_out_weight.reshape(hid_rows, experts * model_width)...  1110 us
    all_gather x1, waiting for transfers between devices, on_device(): lax.all_gather(w_expert_out, 'col', axis=1, tiled=True)  715 us
    all_gather x1, waiting for transfers between devices, on_device(): lax.all_gather(w_in, 'col', axis=1, tiled=True)  665 us
    reduce_scatter x1, waiting for transfers between devices, on_device(): lax.psum_scatter(jnp.dot(normed_one, stacked_weights, preferred_element_t...  101 us
  transfers between devices with their start and end apart: 22, of which 15 were waited for; matrix products, arithmetic and copies ran while one was open for 7% of the time, Pallas kernels for 0%

commit v1 on v0

--- a/solution.py
+++ b/solution.py
@@ -1,6 +1,10 @@
+import functools
+
 import jax
 import jax.numpy as jnp
 from jax import lax
+from jax.experimental import pallas as pl
+from jax.experimental.pallas import tpu as pltpu
 from jax.sharding import PartitionSpec as P
 
 EXPERTS = 32
@@ -53,7 +57,7 @@
     return (raw_scores + pair_bias, allowed, one_hot)
 
 
-def attend(query_heads, keys_all, values_all, bucket_rows, query_docs, doc_ids, bias_table):
+def attend_blocks(query_heads, keys_all, values_all, bucket_rows, query_docs, doc_ids, bias_table):
     tok_rows, head_count, head_dim = query_heads.shape
     seq_len = keys_all.shape[0]
     key_block = min(seq_len, 512)
@@ -100,7 +104,7 @@
     return (attended, log_total)
 
 
-def attend_back(
+def attend_blocks_back(
     query_heads,
     keys_all,
     values_all,
@@ -163,7 +167,7 @@
     return (grad_query, grad_table, kv_terms.reshape(seq_len, 2 * model_width))
 
 
-def on_device(
+def general_plan(
     tokens,
     gain_one,
     gain_two,
@@ -229,7 +233,7 @@
         lax.all_gather(values_low, "row", axis=0, tiled=True),
     )
     query_heads = queries_low.reshape(tok_rows, head_count, head_dim)
-    attended, log_total = attend(
+    attended, log_total = attend_blocks(
         query_heads, keys_all, values_all, bucket_rows, query_docs, doc_ids, bias_table
     )
     attn_low = attended.reshape(tok_rows, model_width).astype(jnp.bfloat16)
@@ -318,7 +322,7 @@
     grad_attn = lax.all_to_all(grad_heads_home, "row", split_axis=0, concat_axis=1, tiled=True)
     grad_heads = grad_attn.reshape(tok_rows, head_count, head_dim)
     grad_dot = jnp.einsum("ihd,ihd->hi", grad_heads.astype(jnp.float32), attended)
-    grad_query, grad_table, kv_terms = attend_back(
+    grad_query, grad_table, kv_terms = attend_blocks_back(
         query_heads,
         keys_all,
         values_all,
@@ -400,9 +404,756 @@
     )
 
 
+BF16 = jnp.bfloat16
+F32 = jnp.float32
+I32 = jnp.int32
+NT = (((1,), (1,)), ((), ()))
+NN = (((1,), (0,)), ((), ()))
+TN = (((0,), (0,)), ((), ()))
+LANES = 128
+PAIR_ROWS = 16
+LOW_BINS = 8
+GELU_SCALE = 0.7978845608028654
+GELU_CUBE = 0.044715
+QUICK = pl.CostEstimate(flops=0, bytes_accessed=0, transcendentals=0)
+
+
+def mm(left, right, dims):
+    return lax.dot_general(left, right, dims, preferred_element_type=F32)
+
+
+def two_parts(values):
+    high = values.astype(BF16)
+    return high, (values - high.astype(F32)).astype(BF16)
+
+
+def attend_kernel(heads, head_dim, q_ref, k_ref, v_ref, idx_ref, tab_ref, o_ref, p_ref):
+    rows, keys = idx_ref.shape
+    idx = idx_ref[...].astype(F32).astype(I32)
+    for h in range(heads):
+        span = slice(h * head_dim, (h + 1) * head_dim)
+        table = jnp.broadcast_to(tab_ref[h : h + 1, :], (rows, LANES))
+        bias = jnp.concatenate(
+            [
+                jnp.take_along_axis(table, idx[:, c : c + LANES], axis=1)
+                for c in range(0, keys, LANES)
+            ],
+            axis=1,
+        )
+        scores = mm(q_ref[span, :], k_ref[span, :], TN) * head_dim**-0.5 + bias
+        weights = jnp.exp(scores - jnp.max(scores, axis=1, keepdims=True))
+        soft = (weights * (1.0 / jnp.sum(weights, axis=1, keepdims=True))).astype(BF16)
+        p_ref[h] = soft
+        o_ref[span, :] = mm(v_ref[span, :], soft, NT)
+
+
+def attend(q, k, v, idx, tab, heads, tile):
+    width, keys = q.shape
+    whole = lambda a: pl.BlockSpec(a.shape, lambda i: (0, 0))
+    return pl.pallas_call(
+        functools.partial(attend_kernel, heads, width // heads),
+        grid=(keys // tile,),
+        in_specs=[
+            pl.BlockSpec((width, tile), lambda i: (0, i)),
+            whole(k),
+            whole(v),
+            pl.BlockSpec((tile, keys), lambda i: (i, 0)),
+            whole(tab),
+        ],
+        out_specs=[
+            pl.BlockSpec((width, tile), lambda i: (0, i)),
+            pl.BlockSpec((heads, tile, keys), lambda i: (0, i, 0)),
+        ],
+        out_shape=[
+            jax.ShapeDtypeStruct((width, keys), F32),
+            jax.ShapeDtypeStruct((heads, keys, keys), BF16),
+        ],
+        compiler_params=pltpu.CompilerParams(vmem_limit_bytes=48 * 2**20),
+        cost_estimate=QUICK,
+    )(q, k, v, idx, tab)
+
+
+def back_kernel(
+    heads,
+    count,
+    experts,
+    cols,
+    place_ref,
+    q_ref,
+    k_ref,
+    v_ref,
+    idx_ref,
+    p_ref,
+    o_ref,
+    slot_ref,
+    h1_ref,
+    row_ref,
+    col_ref,
+    x_ref,
+    n1_ref,
+    ofull_ref,
+    w_ref,
+    gain_two_ref,
+    *refs,
+):
+    pieces = refs[:count]
+    layer_ref, da_ref, proj_ref = refs[count : count + 3]
+    dn1_refs = refs[count + 3 : 2 * count + 3]
+    g_aug, v_aug, dqkv, dk_acc, dv_acc, hist, router_acc, dn1_acc = refs[2 * count + 3 :]
+    step, steps = pl.program_id(0), pl.num_programs(0)
+    me = place_ref[0]
+    part, tile = q_ref.shape
+    keys = k_ref.shape[1]
+    head_dim = part // heads
+    aug = g_aug.shape[0] // heads
+    width = x_ref.shape[0]
+    slots = pieces[0].shape[0]
+    scale = head_dim**-0.5
+
+    @pl.when(step == 0)
+    def _():
+        dk_acc[...] = jnp.zeros_like(dk_acc)
+        dv_acc[...] = jnp.zeros_like(dv_acc)
+        hist[...] = jnp.zeros_like(hist)
+        placed = jnp.zeros((3 * part, keys), F32)
+        router = jnp.zeros((part, 2 * experts), F32)
+        slot_row = lax.broadcasted_iota(I32, (slots, keys), 0)
+        for k in range(count):
+            spread = jnp.where(slot_row + (me ^ k) * slots == slot_ref[...], 1.0, 0.0).astype(BF16)
+            placed = placed + mm(pieces[k][:, : 3 * part], spread, TN)
+            router = router + pieces[k][:part, 3 * part :].astype(F32)
+        router_acc[...] = router[:, :experts] + router[:, experts:]
+        layer_ref[...] = (h1_ref[...] + row_ref[1:2, :] * placed[:part]).astype(BF16)
+        da_ref[...] = placed[part : 2 * part].astype(BF16)
+        fill = jnp.zeros((PAIR_ROWS - 2, keys), F32)
+        ones = jnp.concatenate([jnp.ones((2, keys), F32), fill], axis=0).astype(BF16)
+        for h in range(heads):
+            span = slice(h * head_dim, (h + 1) * head_dim)
+            do = placed[2 * part + h * head_dim : 2 * part + (h + 1) * head_dim]
+            delta = jnp.sum(do * o_ref[span, :], axis=0, keepdims=True)
+            high = delta.astype(BF16).astype(F32)
+            rest = jnp.concatenate([-high, high - delta, fill], axis=0).astype(BF16)
+            g_aug[h * aug : h * aug + head_dim, :] = do.astype(BF16)
+            g_aug[h * aug + head_dim : (h + 1) * aug, :] = rest
+            v_aug[h * aug : h * aug + head_dim, :] = v_ref[span, :]
+            v_aug[h * aug + head_dim : (h + 1) * aug, :] = ones
+
+    lanes = pl.ds(pl.multiple_of(step * tile, tile), tile)
+    slopes = []
+    for h in range(heads):
+        span = slice(h * head_dim, (h + 1) * head_dim)
+        soft = p_ref[h]
+        g_part = g_aug[h * aug : (h + 1) * aug, lanes]
+        diff = mm(g_part, v_aug[h * aug : (h + 1) * aug, :], TN)
+        slope = (soft.astype(F32) * diff).astype(BF16)
+        slopes.append(slope)
+        dqkv[span, lanes] = (mm(k_ref[span, :], slope, NT) * scale).astype(BF16)
+        dk_acc[span, :] += mm(q_ref[span, :], slope, NN) * scale
+        dv_acc[span, :] += mm(g_part[:head_dim], soft, NN)
+    idx = idx_ref[...].astype(F32).astype(I32)
+    high = (idx // LOW_BINS).astype(F32).astype(BF16)
+    low = (idx % LOW_BINS).astype(F32).astype(BF16)
+    high_bins = hist.shape[1] // (heads * PAIR_ROWS)
+    one = jnp.ones((), BF16)
+    zero = jnp.zeros((), BF16)
+    total = hist[...]
+    for s in range(0, tile, PAIR_ROWS):
+        rows = slice(s, s + PAIR_ROWS)
+        left = jnp.concatenate(
+            [jnp.where(low[rows] == n, one, zero) for n in range(LOW_BINS)], axis=0
+        )
+        right = jnp.concatenate(
+            [
+                jnp.where(high[rows] == n, slopes[h][rows], zero)
+                for h in range(heads)
+                for n in range(high_bins)
+            ],
+            axis=0,
+        )
+        total = total + mm(left, right, NT)
+    hist[...] = total
+
+    @pl.when(step == steps - 1)
+    def _():
+        dqkv[part : 2 * part, :] = dk_acc[...].astype(BF16)
+        dqkv[2 * part :, :] = dv_acc[...].astype(BF16)
+        r1 = row_ref[0:1, :]
+        inner = jnp.zeros((1, keys), F32)
+        gain_rows = []
+        for d in range(count):
+            rows = slice(d * part, (d + 1) * part)
+            dn1 = mm(w_ref[rows, :], dqkv[...], NN)
+            dn1_acc[d] = dn1.astype(BF16)
+            dn1_x = dn1 * x_ref[rows, :].astype(F32)
+            inner = inner + jnp.sum(dn1_x * col_ref[rows, :], axis=0, keepdims=True)
+            gain_rows.append(
+                lax.dot_general(
+                    jnp.broadcast_to(r1, (8, keys)),
+                    dn1_x,
+                    NT,
+                    precision=lax.Precision.HIGHEST,
+                    preferred_element_type=F32,
+                )[:1]
+            )
+        cells = hist[...]
+        same = lax.broadcasted_iota(I32, cells.shape, 0) % PAIR_ROWS == (
+            lax.broadcasted_iota(I32, cells.shape, 1) % PAIR_ROWS
+        )
+        cells = jnp.where(same, cells, 0.0)
+        low_rows = (LOW_BINS, cells.shape[0])
+        sum_rows = jnp.where(
+            lax.broadcasted_iota(I32, low_rows, 1) // PAIR_ROWS
+            == lax.broadcasted_iota(I32, low_rows, 0),
+            1.0,
+            0.0,
+        )
+        lane_cols = (cells.shape[1], LANES)
+        bins = heads * high_bins
+        sum_cols = jnp.where(
+            lax.broadcasted_iota(I32, lane_cols, 0) // PAIR_ROWS + me * bins
+            == lax.broadcasted_iota(I32, lane_cols, 1),
+            1.0,
+            0.0,
+        )
+        exact = functools.partial(
+            lax.dot_general,
+            dimension_numbers=NN,
+            precision=lax.Precision.HIGHEST,
+            preferred_element_type=F32,
+        )
+        table = exact(exact(sum_rows, cells), sum_cols)
+        table_row = jnp.concatenate([table[n : n + 1] for n in range(LOW_BINS)], axis=1)
+        pad = jnp.zeros((1, keys - width), F32)
+        gain_row = jnp.concatenate(gain_rows + [pad], axis=1)
+        gain_two_row = jnp.concatenate([gain_two_ref[...], pad], axis=1)
+        extra = jnp.concatenate([inner, gain_row, gain_two_row, table_row], axis=0)
+        extra_high = extra.astype(BF16).astype(F32)
+        extra = jnp.concatenate(
+            [extra_high, extra - extra_high, jnp.zeros((PAIR_ROWS - 8, keys), F32)], axis=0
+        ).astype(BF16)
+        for k in range(count):
+            dn1_refs[k][:part, :] = dn1_acc[me ^ k]
+            dn1_refs[k][part:, :] = extra
+        router = jnp.transpose(router_acc[...])
+        router_high = router.astype(BF16).astype(F32)
+        router_low = router - router_high
+        band = width // cols
+        share = experts // cols
+        blank = jnp.zeros((PAIR_ROWS - 2 * share, width), F32)
+        pad = jnp.zeros((share, width - part), F32)
+        dqkv_all, da_all = dqkv[...], da_ref[...]
+        for c in range(cols):
+            rows = slice(c * band, (c + 1) * band)
+            proj_ref[c, :band, : 3 * part] = mm(n1_ref[rows, :], dqkv_all, NT).astype(BF16)
+            proj_ref[c, :band, 3 * part :] = mm(ofull_ref[rows, :], da_all, NT).astype(BF16)
+            own = slice(c * share, (c + 1) * share)
+            proj_ref[c, band:, :] = jnp.concatenate(
+                [
+                    jnp.concatenate([router_high[own], pad], axis=1),
+                    jnp.concatenate([router_low[own], pad], axis=1),
+                    blank,
+                ],
+                axis=0,
+            ).astype(BF16)
+
+
+def attend_back(
+    place, q, k, v, idx, p, o, slot, h1, row_facts, gain, x, n1, o_full, w, gain_two, pieces, cols, buckets, tile
+):
+    part, keys = q.shape
+    width = x.shape[0]
+    count = len(pieces)
+    heads = p.shape[0]
+    experts = (pieces[0].shape[1] - 3 * part) // 2
+    aug_width = part + heads * PAIR_ROWS
+    hist_shape = (LOW_BINS * PAIR_ROWS, heads * (buckets // LOW_BINS) * PAIR_ROWS)
+    fixed = lambda a: pl.BlockSpec(a.shape, lambda i, m: (0,) * len(a.shape))
+    outs = [
+        jax.ShapeDtypeStruct((part, keys), BF16),
+        jax.ShapeDtypeStruct((part, keys), BF16),
+        jax.ShapeDtypeStruct((cols, width // cols + PAIR_ROWS, width), BF16),
+    ] + [jax.ShapeDtypeStruct((part + PAIR_ROWS, keys), BF16)] * count
+    rest = (o, slot, h1, row_facts, gain, x, n1, o_full, w, gain_two, *pieces)
+    out = pl.pallas_call(
+        functools.partial(back_kernel, heads, count, experts, cols),
+        grid_spec=pltpu.PrefetchScalarGridSpec(
+            num_scalar_prefetch=1,
+            grid=(keys // tile,),
+            in_specs=[
+                pl.BlockSpec((part, tile), lambda i, m: (0, i)),
+                fixed(k),
+                fixed(v),
+                pl.BlockSpec((tile, keys), lambda i, m: (i, 0)),
+                pl.BlockSpec((heads, tile, keys), lambda i, m: (0, i, 0)),
+            ]
+            + [fixed(a) for a in rest],
+            out_specs=[fixed(a) for a in outs],
+            scratch_shapes=[
+                pltpu.VMEM((aug_width, keys), BF16),
+                pltpu.VMEM((aug_width, keys), BF16),
+                pltpu.VMEM((3 * part, keys), BF16),
+                pltpu.VMEM((part, keys), F32),
+                pltpu.VMEM((part, keys), F32),
+                pltpu.VMEM(hist_shape, F32),
+                pltpu.VMEM((part, experts), F32),
+                pltpu.VMEM((count, part, keys), BF16),
+            ],
+        ),
+        out_shape=outs,
+        compiler_params=pltpu.CompilerParams(vmem_limit_bytes=56 * 2**20),
+        cost_estimate=QUICK,
+    )(place, q, k, v, idx, p, *rest)
+    return out[0], out[1], out[2], out[3:]
+
+
+def expert_kernel(count, place_ref, x_ref, dy_ref, router_ref, *refs):
+    in_refs, eout_refs = refs[:count], refs[count : 2 * count]
+    back_ref = refs[2 * count]
+    gi_refs = refs[2 * count + 1 : 3 * count + 1]
+    ge_refs = refs[3 * count + 1 : 4 * count + 1]
+    win, eout, dys, y_acc, dx_acc, gi = refs[4 * count + 1 :]
+    step = pl.program_id(0)
+    me = place_ref[0]
+    part = in_refs[0].shape[0]
+
+    @pl.when(step == 0)
+    def _():
+        logits = mm(x_ref[...], router_ref[...], NN)
+        probs = jnp.exp(logits - jnp.max(logits, axis=1, keepdims=True))
+        own = lax.broadcasted_iota(I32, logits.shape, 1) == place_ref[1]
+        gate = jnp.sum(jnp.where(own, probs, 0.0), axis=1, keepdims=True)
+        gate = gate / jnp.sum(probs, axis=1, keepdims=True)
+        dys[...] = (gate * dy_ref[...].astype(F32)).astype(BF16)
+        y_acc[...] = jnp.zeros_like(y_acc)
+        dx_acc[...] = jnp.zeros_like(dx_acc)
+
+    for k in range(count):
+        win[pl.ds(pl.multiple_of((me ^ k) * part, part), part), :] = in_refs[k][...]
+
+        @pl.when(step == k)
+        def _(k=k):
+            eout[...] = eout_refs[k][...]
+
+    pre = mm(x_ref[...], win[...], NN)
+    square = pre * pre
+    curve = jnp.tanh(GELU_SCALE * pre * (1.0 + GELU_CUBE * square))
+    half = 0.5 * (1.0 + curve)
+    hidden = (pre * half).astype(BF16)
+    slope = half + 0.5 * pre * (1.0 - curve * curve) * (
+        GELU_SCALE * (1.0 + 3.0 * GELU_CUBE * square)
+    )
+    dpre = (mm(dys[...], eout[...], NT) * slope).astype(BF16)
+    y_acc[...] += mm(hidden, eout[...], NN)
+    dx_acc[...] += mm(dpre, win[...], NT)
+    ge = mm(hidden, dys[...], TN).astype(BF16)
+    gi[...] = mm(x_ref[...], dpre, TN).astype(BF16)
+    for k in range(count):
+        gi_refs[k][...] = gi[pl.ds(pl.multiple_of((me ^ k) * part, part), part), :]
+
+        @pl.when(step == k)
+        def _(k=k):
+            ge_refs[k][...] = ge
+
+    @pl.when(step == count - 1)
+    def _():
+        width = y_acc.shape[1]
+        back_ref[:, :width] = y_acc[...].astype(BF16)
+        back_ref[:, width:] = dx_acc[...].astype(BF16)
+
+
+def expert_work(place, x, dy, router, in_held, eout_held):
+    count = len(in_held)
+    slots, width = x.shape
+    part, hidden_width = in_held[0].shape
+    chunk = hidden_width // count
+    fixed = lambda a: pl.BlockSpec(a.shape, lambda i, m: (0, 0))
+    lanes = pl.BlockSpec((part, chunk), lambda i, m: (0, m[0] ^ i))
+    shape = lambda s: jax.ShapeDtypeStruct(s, BF16)
+    out = pl.pallas_call(
+        functools.partial(expert_kernel, count),
+        grid_spec=pltpu.PrefetchScalarGridSpec(
+            num_scalar_prefetch=1,
+            grid=(count,),
+            in_specs=[fixed(x), fixed(dy), fixed(router)]
+            + [lanes] * count
+            + [fixed(eout_held[0])] * count,
+            out_specs=[pl.BlockSpec((slots, 2 * width), lambda i, m: (0, 0))] + [lanes] * count + [fixed(eout_held[0])] * count,
+            scratch_shapes=[
+                pltpu.VMEM((width, chunk), BF16),
+                pltpu.VMEM((chunk, width), BF16),
+                pltpu.VMEM((slots, width), BF16),
+                pltpu.VMEM((slots, width), F32),
+                pltpu.VMEM((slots, width), F32),
+                pltpu.VMEM((width, chunk), BF16),
+            ],
+        ),
+        out_shape=[shape((slots, 2 * width))]
+        + [shape((part, hidden_width))] * count
+        + [shape((chunk, width))] * count,
+        compiler_params=pltpu.CompilerParams(vmem_limit_bytes=56 * 2**20),
+        cost_estimate=QUICK,
+    )(place, x, dy, router, *in_held, *eout_held)
+    return out[0], out[1 : 1 + count], out[1 + count :]
+
+
+def slot_kernel(
+    count,
+    experts,
+    place_ref,
+    home_ref,
+    dy_ref,
+    n2_ref,
+    h1_ref,
+    scalar_ref,
+    router_ref,
+    out_ref,
+    gain_ref,
+    parcel_ref,
+    gain_part_ref,
+):
+    me = place_ref[0]
+    slots, width = dy_ref.shape
+    part = width // count
+    y = home_ref[:, :width]
+    dy = dy_ref[...].astype(F32)
+    h1 = h1_ref[...].astype(F32)
+    scalars = scalar_ref[...]
+    probs, gate, r2 = scalars[:, :experts], scalars[:, experts : experts + 1], scalars[:, experts + 1 :]
+    dgate = jnp.sum(dy * y.astype(F32), axis=1, keepdims=True)
+    row = lax.broadcasted_iota(I32, (slots, experts), 0)
+    lane = lax.broadcasted_iota(I32, (slots, experts), 1)
+    hot = jnp.where(row // CAPACITY * count + me == lane, 1.0, 0.0)
+    dlogits = ((dgate * gate) * (hot - probs)).astype(BF16)
+    dn2 = home_ref[:, width:].astype(F32) + mm(dlogits, router_ref[...], NT)
+    scaled = dn2 * gain_ref[...]
+    inner = jnp.sum(scaled * h1, axis=1, keepdims=True)
+    dh1 = dy + r2 * scaled - h1 * (r2 * r2 * r2 * (1.0 / width) * inner)
+    gain_part_ref[...] = jnp.sum(dn2 * h1 * r2, axis=0, keepdims=True)
+    da = dh1.astype(BF16)
+    do = mm(da, out_ref[...], NT).astype(BF16)
+    router_high, router_low = two_parts(mm(n2_ref[...], dlogits, TN))
+    fill = jnp.zeros((slots - part, 2 * experts), BF16)
+    for d in range(count):
+        span = slice(d * part, (d + 1) * part)
+        router = jnp.concatenate([router_high[span], router_low[span]], axis=1)
+        router = jnp.concatenate([router, fill], axis=0)
+        parcel_ref[me ^ d] = jnp.concatenate(
+            [y[:, span], da[:, span], do[:, span], router], axis=1
+        )
+
+
+def slot_work(place, home, dy, n2, h1, scalars, router, out_proj, gain, count):
+    slots, width = dy.shape
+    experts = router.shape[1]
+    lanes = 3 * width // count + 2 * experts
+    fixed = lambda a: pl.BlockSpec(a.shape, lambda i, m: (0,) * len(a.shape))
+    ins = (home, dy, n2, h1, scalars, router, out_proj, gain)
+    outs = [
+        jax.ShapeDtypeStruct((count, slots, lanes), BF16),
+        jax.ShapeDtypeStruct((1, width), F32),
+    ]
+    return pl.pallas_call(
+        functools.partial(slot_kernel, count, experts),
+        grid_spec=pltpu.PrefetchScalarGridSpec(
+            num_scalar_prefetch=1,
+            grid=(1,),
+            in_specs=[fixed(a) for a in ins],
+            out_specs=[fixed(a) for a in outs],
+        ),
+        out_shape=outs,
+        compiler_params=pltpu.CompilerParams(vmem_limit_bytes=48 * 2**20),
+        cost_estimate=QUICK,
+    )(place, *ins)
+
+
+def row_gather(block):
+    me = lax.axis_index("row")
+    count = lax.axis_size("row")
+    far = lax.ppermute(block, "row", [(i, i ^ 2) for i in range(count)])
+    near = lax.ppermute(jnp.stack([block, far]), "row", [(i, i ^ 1) for i in range(count)])
+    held = jnp.stack([block, near[0], far, near[1]])
+    return jnp.concatenate(
+        [lax.dynamic_index_in_dim(held, p ^ me, 0, keepdims=True) for p in range(count)]
+    )
+
+
+def swap(blocks, axis):
+    return lax.all_to_all(blocks, axis, 0, 0)
+
+
+def col_gather(block):
+    count = lax.axis_size("col")
+    return swap(jnp.broadcast_to(block[None], (count,) + block.shape), "col")
+
+
+def trade(piece_for):
+    me = lax.axis_index("row")
+    count = lax.axis_size("row")
+    away = [k for k in (2, 3, 1)]
+    held = {
+        k: lax.ppermute(piece_for(me ^ k), "row", [(i, i ^ k) for i in range(count)]) for k in away
+    }
+    return [piece_for(me)] + [held[k] for k in range(1, count)]
+
+
+def trade_pieces(pieces):
+    count = len(pieces)
+    held = {
+        k: lax.ppermute(pieces[k], "row", [(i, i ^ k) for i in range(count)]) for k in (2, 3, 1)
+    }
+    return [pieces[0]] + [held[k] for k in range(1, count)]
+
+
+def lay(held):
+    me = lax.axis_index("row")
+    out = jnp.zeros((len(held),) + held[0].shape, held[0].dtype)
+    for k, piece in enumerate(held):
+        out = lax.dynamic_update_slice_in_dim(out, piece[None], me ^ k, 0)
+    return out
+
+
+def after(value, *earlier):
+    return lax.optimization_barrier((value,) + earlier)[0]
+
+
+def fill_kernel(count, me_ref, *refs):
+    step = pl.program_id(1)
+    for k in range(count):
+
+        @pl.when(step == k)
+        def _(k=k):
+            refs[count][...] = refs[k][...].astype(F32)
+
+
+def fill_columns(held, splits):
+    count = len(held)
+    height, width = held[0].shape
+    block = height // splits
+    me = lax.axis_index("row").astype(I32).reshape(1)
+    return pl.pallas_call(
+        functools.partial(fill_kernel, count),
+        grid_spec=pltpu.PrefetchScalarGridSpec(
+            num_scalar_prefetch=1,
+            grid=(splits, count),
+            in_specs=[pl.BlockSpec((block, width), lambda i, k, m: (i, 0))] * count,
+            out_specs=pl.BlockSpec((block, width), lambda i, k, m: (i, m[0] ^ k)),
+        ),
+        out_shape=jax.ShapeDtypeStruct((height, count * width), F32),
+        compiler_params=pltpu.CompilerParams(vmem_limit_bytes=48 * 2**20),
+        cost_estimate=QUICK,
+    )(me, *held)
+
+
+def own_rows(array, me, count):
+    return lax.dynamic_slice_in_dim(array, me * count, count, 0)
+
+
+def expert_plan(
+    tokens,
+    gain_one,
+    gain_two,
+    w_query,
+    w_key,
+    w_value,
+    w_out,
+    w_router,
+    w_in,
+    w_expert_out,
+    bias_table,
+    segment,
+    expert,
+    bucket,
+    cotangent,
+):
+    rows, cols = lax.axis_size("row"), lax.axis_size("col")
+    me, col = lax.axis_index("row"), lax.axis_index("col")
+    part, seq_len = tokens.shape[1:]
+    width = part * rows
+    tok_rows = seq_len // rows
+    buckets, all_heads = bias_table.shape
+    heads = all_heads // rows
+    head_dim = width // all_heads
+    experts = w_router.shape[1] * cols
+    hidden_width = w_expert_out.shape[0] * rows
+    slots = (experts // rows) * CAPACITY
+    out_cols = w_query.shape[1]
+    share = cols // rows
+
+    doc_ids = segment[0]
+    expert_ids = expert[0, :, 0]
+
+    tok_low = row_gather(tokens[0]).reshape(width, seq_len)
+    qkv_part = jnp.concatenate([w_query, w_key, w_value], axis=1)
+    qkv_cols = col_gather(qkv_part)
+    qkv_cols = qkv_cols.reshape(rows, share, part, 3 * out_cols)
+    qkv_rows = lay(trade(lambda d: lax.dynamic_index_in_dim(qkv_cols, d, 0, keepdims=False)))
+    qkv_own = jnp.transpose(
+        qkv_rows.reshape(rows, share, part, 3, out_cols), (0, 2, 3, 1, 4)
+    ).reshape(width, 3 * part)
+    same_doc = own_rows(doc_ids, me, tok_rows)[:, None] == doc_ids[None, :]
+    masked = jnp.where(same_doc, bucket[0], buckets).astype(BF16)
+    idx = row_gather(masked).reshape(seq_len, seq_len)
+    low_cols = col_gather(after(jnp.concatenate([w_out, w_router], axis=1), qkv_cols))
+    out_rows = jnp.transpose(low_cols[:, :, :out_cols], (1, 0, 2)).reshape(part, width)
+    router_rows = jnp.transpose(low_cols[:, :, out_cols:], (1, 0, 2)).reshape(part, experts)
+    out_router = row_gather(jnp.concatenate([out_rows, router_rows], axis=1)).reshape(
+        width, width + experts
+    )
+    out_full, router_full = out_router[:, :width], out_router[:, width:]
+    cot_low = row_gather(after(cotangent[0], qkv_rows, idx)).reshape(width, seq_len)
+    lane_cut = lambda array, count: lambda d: lax.dynamic_slice_in_dim(array, d * count, count, 1)
+    w_in = after(w_in, qkv_rows)
+    in_held = trade(lane_cut(w_in, hidden_width))
+
+    picked = expert_ids[None, :] == jnp.arange(experts, dtype=I32)[:, None]
+    picked_float = picked.astype(F32)
+    steps = jnp.arange(seq_len, dtype=I32)
+    upper = (steps[:, None] <= steps[None, :]).astype(BF16)
+    ranks = mm(picked.astype(BF16), upper, NN) - 1.0
+    slot_rank = jnp.sum(ranks * picked_float, axis=0).astype(I32)
+    slot = (expert_ids % rows) * slots + (expert_ids // rows) * CAPACITY + slot_rank
+    choose = (jnp.arange(slots, dtype=I32)[:, None] + me * slots == slot[None, :]).astype(BF16)
+
+    x = tok_low.astype(F32)
+    r1 = lax.rsqrt(jnp.mean(x * x, axis=0) + NORM_EPS)
+    n1 = (x * r1 * gain_one[:, None]).astype(BF16)
+    qkv = mm(qkv_own, n1, TN).astype(BF16)
+    q, k, v = qkv[:part], qkv[part : 2 * part], qkv[2 * part :]
+    table = lax.dynamic_slice_in_dim(jnp.transpose(bias_table), me * heads, heads, 0)
+    table = jnp.pad(
+        table, ((0, 8 - heads), (0, LANES - buckets)), constant_values=NEG_FILL
+    )
+    o32, p = attend(q, k, v, idx, table, heads, 128)
+    o_full = row_gather(o32.astype(BF16)).reshape(width, seq_len)
+    w_expert_out = after(w_expert_out, o_full)
+    eout_held = trade(lane_cut(w_expert_out, width))
+    h1 = x + mm(out_full, o_full, TN)
+    r2 = lax.rsqrt(jnp.mean(h1 * h1, axis=0) + NORM_EPS)
+    n2 = (h1 * r2 * gain_two[:, None]).astype(BF16)
+    logits = mm(router_full, n2, TN)
+    g = jax.nn.softmax(logits, axis=0)
+    gate = jnp.sum(g * picked_float, axis=0)
+
+    expert_at = lambda a: swap(a.reshape(cols, CAPACITY, width), "col").reshape(slots, width)
+    dy_low = mm(choose, cot_low, NT).astype(BF16)
+    dy_slots = expert_at(dy_low)
+    n2_low = mm(choose, n2, NT).astype(BF16)
+    slots_in = expert_at(n2_low)
+    place = jnp.stack([me, col * rows + me]).astype(I32)
+    back, in_pieces, eout_pieces = expert_work(
+        place, slots_in, dy_slots, router_full, in_held, eout_held
+    )
+    grad_eout_held = trade_pieces(eout_pieces)
+    home = swap(back.reshape(cols, CAPACITY, 2 * width), "col").reshape(slots, 2 * width)
+
+    h1_s = mm(choose, h1.astype(BF16), NT).astype(BF16)
+    scalars = lax.dot_general(
+        choose.astype(F32),
+        jnp.concatenate([g, gate[None], r2[None]], axis=0),
+        NT,
+        precision=lax.Precision.HIGHEST,
+        preferred_element_type=F32,
+    )
+    parcel, gain_two_part = slot_work(
+        place, home, dy_low, n2_low, h1_s, scalars, router_full, out_full, gain_two[None], rows
+    )
+    parcel = trade_pieces([parcel[k] for k in range(rows)])
+    grad_in_held = trade_pieces([after(piece, parcel[2]) for piece in in_pieces])
+
+    layer_out, da, proj_parcel, dn1_parcel = attend_back(
+        place,
+        q,
+        k,
+        v,
+        idx,
+        p,
+        o32,
+        slot[None],
+        own_rows(h1, me, part),
+        jnp.stack([r1, gate]),
+        gain_one[:, None],
+        tok_low,
+        n1,
+        o_full,
+        qkv_own,
+        gain_two_part,
+        parcel,
+        cols,
+        buckets,
+        128,
+    )
+    dn1_sum = sum(piece.astype(F32) for piece in trade_pieces(dn1_parcel))
+    dn1 = dn1_sum[:part]
+    extra_sum = dn1_sum[part : part + 4] + dn1_sum[part + 4 : part + 8]
+    inner_one = extra_sum[0]
+    proj_came = swap(proj_parcel, "col")
+    small = jnp.sum(col_gather(after(extra_sum[1:], proj_came)), axis=0)
+    gain_one_grad, gain_two_grad = small[0, :width], small[1, :width]
+    table_grad = jnp.transpose(
+        small[2].reshape(LOW_BINS, LANES)[:, : bias_table.size // LOW_BINS].reshape(
+            LOW_BINS, all_heads, buckets // LOW_BINS
+        ),
+        (2, 0, 1),
+    ).reshape(bias_table.shape)
+    gain_own = own_rows(gain_one, me, part)
+    grad_tokens = (
+        da.astype(F32)
+        + r1 * gain_own[:, None] * dn1
+        - own_rows(x, me, part) * (r1**3 / width * inner_one)
+    ).astype(BF16)
+
+    band = width // cols
+    proj_sum = jnp.sum(proj_came.astype(F32), axis=0)
+    router_rows = experts // cols
+    grad_router = jnp.transpose(
+        proj_sum[band : band + router_rows, :part]
+        + proj_sum[band + router_rows : band + 2 * router_rows, :part]
+    )
+    proj_own = jnp.transpose(
+        proj_sum[:band].reshape(band, 4, share, out_cols), (2, 0, 1, 3)
+    ).reshape(share, band, 4 * out_cols)
+    pieces = []
+    for turn in range(share):
+        moves = [
+            (r * cols + c, (c // share) * cols + share * r + (c + turn) % share)
+            for r in range(rows)
+            for c in range(cols)
+        ]
+        piece = lax.dynamic_index_in_dim(proj_own, (col + turn) % share, 0, keepdims=False)
+        pieces.append(lax.ppermute(piece, ("row", "col"), moves))
+    pieces = jnp.stack(pieces)
+    grad_four = jnp.concatenate(
+        [
+            lax.dynamic_index_in_dim(pieces, (col - half) % share, 0, keepdims=False)
+            for half in range(share)
+        ],
+        axis=0,
+    )
+    grad_query, grad_key, grad_value, grad_out = [
+        grad_four[:, w * out_cols : (w + 1) * out_cols] for w in range(4)
+    ]
+    grad_in, grad_eout = fill_columns(grad_in_held, 4), fill_columns(grad_eout_held, 4)
+    return (
+        layer_out[None],
+        grad_tokens[None],
+        gain_one_grad,
+        gain_two_grad,
+        grad_query,
+        grad_key,
+        grad_value,
+        grad_out,
+        grad_router,
+        grad_in,
+        grad_eout,
+        table_grad,
+    )
+
+
 def solution(mesh):
+    rows, cols = mesh.shape["row"], mesh.shape["col"]
+    paired = rows == 4 and cols == 2 * rows and EXPERTS == rows * cols
     return jax.shard_map(
-        on_device,
+        expert_plan if paired else general_plan,
         mesh=mesh,
         in_specs=(
             P("col", "row", None),

time: 4940 us -> 459 us (0.09)
  waiting for transfers between devices: 4060 us -> 194 us
  local copies, waits for them, and re-layouts: 305 us -> 46.8 us
  matrix products: 268 us -> 12.6 us
  blocking collectives: 222 us -> 0 us
  Pallas kernels: 0 us -> 96.3 us
  starting transfers between devices: 8.31 us -> 76.2 us
    reduce_scatter x6 -> x0, waiting for transfers between devices: 2470 us -> none  [the longest x1 1180 us: on_device(): lax.psum_scatter(grad_in_weight.reshape(dim_rows, experts * ffn_width), '...]
    all_gather x8 -> x0, waiting for transfers between devices: 1510 us -> none  [the longest x1 715 us: on_device(): lax.all_gather(w_expert_out, 'col', axis=1, tiled=True)]
    dot_general x36 -> x8, matrix products: 267 us -> 12.6 us  [the longest x7 11.8 us: mm(): return lax.dot_general(left, right, dims, preferred_element_type=F32)]
    ppermute x0 -> x33, waiting for transfers between devices: none -> 165 us  [the longest x12 71 us: trade_pieces(): lax.ppermute(pieces[k], 'row', [(i, i ^ k) for i in range(count)])]
    reshape x2 -> x8, local copies, waits for them, and re-layouts: 123 us -> 6.05 us  [the longest x2 3.79 us: expert_plan(): qkv_own = jnp.transpose(qkv_rows.reshape(rows, share, part, 3, out_cols),...]
    all_gather x5 -> x0, blocking collectives: 116 us -> none  [the longest x1 25.3 us: on_device(): lax.all_gather(w_key, 'col', axis=1, tiled=True)]
    pallas_call x0 -> x6, Pallas kernels: none -> 96.3 us  [the longest x1 35.6 us: attend_back(): pl.pallas_call(functools.partial(back_kernel, heads, count, experts, cols...]
    psum x6 -> x0, blocking collectives: 79.3 us -> none  [the longest x1 51.1 us: on_device(): lax.psum((place_one, place_two, grad_table), ('row', 'col'))]
  transfers between devices with their start and end apart: 22 -> 40, of which waited for: 15 -> 18; matrix products, arithmetic and copies ran while one was open for 7% -> 16% of each run, Pallas kernels for 0% -> 15%
where the time goes in v1:
time: 459 us; the launch traced here: 451 us
  waiting for transfers between devices  194 us (42%)
  Pallas kernels  96.3 us (21%)
  starting transfers between devices  76.2 us (17%)
  local copies, waits for them, and re-layouts  46.8 us (10%)
  other arithmetic  23.7 us (5%)
  matrix products  12.6 us (3%)
    ppermute x12, waiting for transfers between devices, trade_pieces(): lax.ppermute(pieces[k], 'row', [(i, i ^ k) for i in range(count)])  71 us
    ppermute x9, waiting for transfers between devices, trade(): lax.ppermute(piece_for(me ^ k), 'row', [(i, i ^ k) for i in range(count)])  70.9 us
    all_to_all x7, starting transfers between devices, swap(): return lax.all_to_all(blocks, axis, 0, 0)  41.5 us
    pallas_call x1, Pallas kernels, attend_back(): pl.pallas_call(functools.partial(back_kernel, heads, count, experts, cols...  35.6 us
    all_to_all x7, waiting for transfers between devices, swap(): return lax.all_to_all(blocks, axis, 0, 0)  29 us
    pallas_call x1, Pallas kernels, expert_work(): pl.pallas_call(functools.partial(expert_kernel, count), grid_spec=pltpu.P...  23.2 us
    pallas_call x1, Pallas kernels, attend(): pl.pallas_call(functools.partial(attend_kernel, heads, width // heads), g...  18.2 us
    ppermute x5, waiting for transfers between devices, row_gather(): far = lax.ppermute(block, 'row', [(i, i ^ 2) for i in range(count)])  15.6 us
  transfers between devices with their start and end apart: 40, of which 18 were waited for; matrix products, arithmetic and copies ran while one was open for 16% of the time, Pallas kernels for 15%

profile of v1, /device:TPU:25, one launch (start us, length us, event | category | flops | bytes accessed | tf_op | source)
XLA Modules:
  0.0 451.2 jit_solution(16561714185387800174)
XLA Ops:
  6.5 5.6 %all-to-all-start = ((bf16[8,192,288]{1,2,0:T(8,128)(2,1)}), bf16[8,192,288]{1,2,0:T(8,128)(2,1)S(1)}, u32[]{:S(2)}, u32[]{:S(2)}) async-start(bf16[8,192,288]{1,2,0:T(8,128)(2,1)} %broadcast_in_dim.29), calls=%async_computation | async-start | bytes 2359296 | tf_op jit(solution)/shard_map/all_to_all | solution.py:881
  30.5 7.8 %all-to-all-done = bf16[8,192,288]{1,2,0:T(8,128)(2,1)S(1)} async-done(((bf16[8,192,288]{1,2,0:T(8,128)(2,1)}), bf16[8,192,288]{1,2,0:T(8,128)(2,1)S(1)}, u32[]{:S(2)}, u32[]{:S(2)}) %all-to-all-start) | async-done | bytes 884768 | tf_op jit(solution)/shard_map/all_to_all | solution.py:881
  42.7 6.8 %all-to-all-start.1 = ((bf16[8,192,100]{2,1,0:T(8,128)(2,1)}), bf16[8,192,100]{2,1,0:T(8,128)(2,1)}, u32[]{:S(2)}, u32[]{:S(2)}) async-start(bf16[8,192,100]{2,1,0:T(8,128)(2,1)} %broadcast_in_dim.35), calls=%async_computation.1 | async-start | bytes 786432 | tf_op jit(solution)/shard_map/all_to_all | solution.py:881
  64.3 18.2 %shard_map.238 = (f32[192,1024]{1,0:T(8,128)S(1)}, bf16[3,1024,1024]{2,1,0:T(8,128)(2,1)}) custom-call(bf16[192,1024]{1,0:T(8,128)(2,1)S(1)} %get-tuple-element.182.q_ref, bf16[192,1024]{1,0:T(8,128)(2,1)S(1)} %get-tuple-element.181.k_ref, bf16[192,1024]{1,0:T(8,128)(2,1)S(1)} %get-tuple-element.180.v_ref, bf16[1024,1024]{1,0:T(8,128)(2,1)S(1)} %bitcast.115, ...), custom_call_target="tpu_custom_call" | custom-call | tf_op jit(solution)/shard_map/pallas_call | solution.py:453
  97.0 5.8 %collective-permute-done.11 = bf16[192,1024]{1,0:T(8,128)(2,1)S(1)} collective-permute-done((bf16[192,1024]{1,0:T(8,128)(2,1)S(1)}, bf16[192,1024]{1,0:T(8,128)(2,1)S(1)}, u32[]{:S(2)}, u32[]{:S(2)}) %collective-permute-start.11) | collective-permute-done | bytes 393248 | tf_op jit(solution)/shard_map/ppermute | solution.py:872
  115.8 6.3 %all-to-all-start.3 = ((bf16[8,48,768]{2,1,0:T(8,128)(2,1)}), bf16[8,48,768]{2,1,0:T(8,128)(2,1)S(1)}, u32[]{:S(2)}, u32[]{:S(2)}) async-start(bf16[8,48,768]{2,1,0:T(8,128)(2,1)} %bitcast.40), calls=%async_computation.3 | async-start | bytes 1179648 | tf_op jit(solution)/shard_map/all_to_all | solution.py:881
  122.3 5.2 %constant_dynamic-slice_fusion = (bf16[768,768]{1,0:T(8,128)(2,1)}, bf16[768,768]{1,0:T(8,128)(2,1)}, bf16[768,768]{1,0:T(8,128)(2,1)}, bf16[768,768]{1,0:T(8,128)(2,1)}) fusion(bf16[768,3072]{1,0:T(8,128)(2,1)} %param.24, s32[]{:T(128)S(6)} %select_n.161, s32[]{:T(128)S(6)} %select_n.160, s32[]{:T(128)S(6)} %select_n.159, s32[]{:T(128)S(6)} %select_n.158), kind=kLoop, calls=%fused_computation.111 | loop fusion | bytes 9437200 | tf_op jit(solution)/shard_map/dynamic_slice | solution.py:1004
  137.0 5.4 %all-to-all-start.2 = ((bf16[8,48,768]{2,1,0:T(8,128)(2,1)}), bf16[8,48,768]{2,1,0:T(8,128)(2,1)S(1)}, u32[]{:S(2)}, u32[]{:S(2)}) async-start(bf16[8,48,768]{2,1,0:T(8,128)(2,1)} %bitcast.34), calls=%async_computation.2 | async-start | bytes 1179648 | tf_op jit(solution)/shard_map/all_to_all | solution.py:881
  143.8 19.1 %collective-permute-done.15.refs_3_ = bf16[192,3072]{1,0:T(8,128)(2,1)} collective-permute-done((bf16[192,3072]{1,0:T(8,128)(2,1)}, bf16[192,3072]{1,0:T(8,128)(2,1)}, u32[]{:S(2)}, u32[]{:S(2)}) %collective-permute-start.15) | collective-permute-done | bytes 1179680 | tf_op jit(solution)/shard_map/ppermute | solution.py:894
  162.9 23.7 %collective-permute-done.17.refs_6_ = bf16[768,768]{1,0:T(8,128)(2,1)} collective-permute-done((bf16[768,768]{1,0:T(8,128)(2,1)}, bf16[768,768]{1,0:T(8,128)(2,1)}, u32[]{:S(2)}, u32[]{:S(2)}) %collective-permute-start.17) | collective-permute-done | bytes 1179680 | tf_op jit(solution)/shard_map/ppermute | solution.py:894
  186.6 25.9 %collective-permute-done.18.refs_7_ = bf16[768,768]{1,0:T(8,128)(2,1)} collective-permute-done((bf16[768,768]{1,0:T(8,128)(2,1)}, bf16[768,768]{1,0:T(8,128)(2,1)}, u32[]{:S(2)}, u32[]{:S(2)}) %collective-permute-start.18) | collective-permute-done | bytes 1179680 | tf_op jit(solution)/shard_map/ppermute | solution.py:894
  212.5 23.2 %shard_map.239 = (bf16[384,1536]{1,0:T(8,128)(2,1)}, bf16[192,3072]{1,0:T(8,128)(2,1)}, bf16[192,3072]{1,0:T(8,128)(2,1)}, bf16[192,3072]{1,0:T(8,128)(2,1)}, bf...) custom-call(s32[2]{0:T(128)} %pad_add_fusion.place_ref, ...), custom_call_target="tpu_custom_call" | custom-call | tf_op jit(solution)/shard_map/pallas_call | solution.py:772
  235.7 6.1 %all-to-all-start.4 = ((bf16[8,48,1536]{2,1,0:T(8,128)(2,1)}), bf16[8,48,1536]{2,1,0:T(8,128)(2,1)S(1)}, u32[]{:S(2)}, u32[]{:S(2)}) async-start(bf16[8,48,1536]{2,1,0:T(8,128)(2,1)} %bitcast.143), calls=%async_computation.4 | async-start | bytes 2359296 | tf_op jit(solution)/shard_map/all_to_all | solution.py:881
  248.6 21.1 %all-to-all-done.4 = bf16[8,48,1536]{2,1,0:T(8,128)(2,1)S(1)} async-done(((bf16[8,48,1536]{2,1,0:T(8,128)(2,1)}), bf16[8,48,1536]{2,1,0:T(8,128)(2,1)S(1)}, u32[]{:S(2)}, u32[]{:S(2)}) %all-to-all-start.4) | async-done | bytes 1179680 | tf_op jit(solution)/shard_map/all_to_all | solution.py:881
  296.7 5.3 %collective-permute-done.21.refs_3_ = bf16[384,640]{1,0:T(8,128)(2,1)} collective-permute-done((bf16[384,640]{1,0:T(8,128)(2,1)}, bf16[384,640]{1,0:T(8,128)(2,1)}, u32[]{:S(2)}, u32[]{:S(2)}) %collective-permute-start.21) | collective-permute-done | bytes 491552 | tf_op jit(solution)/shard_map/ppermute | solution.py:902
  302.0 35.6 %shard_map.241 = (bf16[192,1024]{1,0:T(8,128)(2,1)}, bf16[192,1024]{1,0:T(8,128)(2,1)}, bf16[8,112,768]{2,1,0:T(8,128)(2,1)}, bf16[208,1024]{1,0:T(8,128)(2,1)},...) custom-call(s32[2]{0:T(128)} %pad_add_fusion.place_ref, ...), custom_call_target="tpu_custom_call" | custom-call | tf_op jit(solution)/shard_map/pallas_call | solution.py:677
  337.6 5.8 %all-to-all-start.5 = ((bf16[8,112,768]{2,1,0:T(8,128)(2,1)}), bf16[8,112,768]{2,1,0:T(8,128)(2,1)}, u32[]{:S(2)}, u32[]{:S(2)}) async-start(bf16[8,112,768]{2,1,0:T(8,128)(2,1)} %get-tuple-element.56), calls=%async_computation.5 | async-start | bytes 2752512 | tf_op jit(solution)/shard_map/all_to_all | solution.py:881
  346.6 6.3 %collective-permute-done.32.refs_3_ = bf16[768,768]{1,0:T(8,128)(2,1)S(1)} collective-permute-done((bf16[768,768]{1,0:T(8,128)(2,1)}, bf16[768,768]{1,0:T(8,128)(2,1)S(1)}, u32[]{:S(2)}, u32[]{:S(2)}) %collective-permute-start.32) | collective-permute-done | bytes 1179680 | tf_op jit(solution)/shard_map/ppermute | solution.py:902
  355.9 7.1 %shard_map.243 = f32[768,3072]{1,0:T(8,128)} custom-call(s32[1]{0:T(128)} %bitcast.me_ref, bf16[768,768]{1,0:T(8,128)(2,1)S(1)} %copy-done.9, bf16[768,768]{1,0:T(8,128)(2,1)S(1)} %collective-permute-done.30.refs_1_, bf16[768,768]{1,0:T(8,128)(2,1)S(1)} %collective-permute-done.31.refs_2_, bf16[768,768]{1,0:T(8,128)(2,1)S(1)} %collective-permute-done.32.refs_3_), custom_call_target="tpu_custom_call" | custom-call | tf_op jit(solution)/shard_map/pallas_call | solution.py:933
  363.0 8.0 %collective-permute-done.24 = bf16[208,1024]{1,0:T(8,128)(2,1)} collective-permute-done((bf16[208,1024]{1,0:T(8,128)(2,1)}, bf16[208,1024]{1,0:T(8,128)(2,1)}, u32[]{:S(2)}, u32[]{:S(2)}) %collective-permute-start.24) | collective-permute-done | bytes 426016 | tf_op jit(solution)/shard_map/ppermute | solution.py:902
  373.6 22.4 %collective-permute-done.29.refs_3_ = bf16[192,3072]{1,0:T(8,128)(2,1)S(1)} collective-permute-done((bf16[192,3072]{1,0:T(8,128)(2,1)}, bf16[192,3072]{1,0:T(8,128)(2,1)S(1)}, u32[]{:S(2)}, u32[]{:S(2)}) %collective-permute-start.29) | collective-permute-done | bytes 1179680 | tf_op jit(solution)/shard_map/ppermute | solution.py:902
  396.0 23.9 %collective-permute-done.28.refs_2_ = bf16[192,3072]{1,0:T(8,128)(2,1)S(1)} collective-permute-done((bf16[192,3072]{1,0:T(8,128)(2,1)}, bf16[192,3072]{1,0:T(8,128)(2,1)S(1)}, u32[]{:S(2)}, u32[]{:S(2)}) %collective-permute-start.28) | collective-permute-done | bytes 1179680 | tf_op jit(solution)/shard_map/ppermute | solution.py:902
  419.9 7.1 %shard_map.242 = f32[192,12288]{1,0:T(8,128)} custom-call(s32[1]{0:T(128)} %bitcast.me_ref, bf16[192,3072]{1,0:T(8,128)(2,1)S(1)} %copy-done.8, bf16[192,3072]{1,0:T(8,128)(2,1)S(1)} %collective-permute-done.27.refs_1_, bf16[192,3072]{1,0:T(8,128)(2,1)S(1)} %collective-permute-done.28.refs_2_, bf16[192,3072]{1,0:T(8,128)(2,1)S(1)} %collective-permute-done.29.refs_3_), custom_call_target="tpu_custom_call" | custom-call | tf_op jit(solution)/shard_map/pallas_call | solution.py:933
  435.4 5.4 %all-to-all-start.6 = ((f32[8,3,1024]{2,1,0:T(4,128)}), f32[8,3,1024]{2,1,0:T(4,128)S(1)}, u32[]{:S(2)}, u32[]{:S(2)}) async-start(f32[8,3,1024]{2,1,0:T(4,128)} %broadcast_in_dim.40), calls=%async_computation.6 | async-start | bytes 262144 | tf_op jit(solution)/shard_map/all_to_all | solution.py:881
  (258 shorter events, 142.0 us)
Async XLA Ops:
  6.5 31.9 %all-to-all-start = ((bf16[8,192,288]{1,2,0:T(8,128)(2,1)}), bf16[8,192,288]{1,2,0:T(8,128)(2,1)S(1)}, u32[]{:S(2)}, u32[]{:S(2)}) async-start(bf16[8,192,288]{1,2,0:T(8,128)(2,1)} %broadcast_in_dim.29), calls=%async_computation | async-start | bytes 2359296 | tf_op jit(solution)/shard_map/all_to_all | solution.py:881
  23.2 26.3 %collective-permute-start.6 = (bf16[2,256,1024]{2,1,0:T(8,128)(2,1)}, bf16[2,256,1024]{2,1,0:T(8,128)(2,1)}, u32[]{:S(2)}, u32[]{:S(2)}) collective-permute-start(bf16[2,256,1024]{2,1,0:T(8,128)(2,1)} %pad_maximum_fusion.10), channel_id=1, source_target_pairs={{0,8},{8,0},{16,24},{24,16},{1,9},{9,1},{17,25},{25,17},{2,10},{10... | collective-permute-start | bytes 3145736 | tf_op jit(solution)/shard_map/ppermute | solution.py:873
  42.7 42.2 %all-to-all-start.1 = ((bf16[8,192,100]{2,1,0:T(8,128)(2,1)}), bf16[8,192,100]{2,1,0:T(8,128)(2,1)}, u32[]{:S(2)}, u32[]{:S(2)}) async-start(bf16[8,192,100]{2,1,0:T(8,128)(2,1)} %broadcast_in_dim.35), calls=%async_computation.1 | async-start | bytes 786432 | tf_op jit(solution)/shard_map/all_to_all | solution.py:881
  84.6 18.2 %collective-permute-start.11 = (bf16[192,1024]{1,0:T(8,128)(2,1)S(1)}, bf16[192,1024]{1,0:T(8,128)(2,1)S(1)}, u32[]{:S(2)}, u32[]{:S(2)}) collective-permute-start(bf16[192,1024]{1,0:T(8,128)(2,1)S(1)} %bitcast.135), channel_id=1, source_target_pairs={{0,16},{8,24},{16,0},{24,8},{1,17},{9,25},{17,1},{25,9},{2,18},{10... | collective-permute-start | bytes 1179656 | tf_op jit(solution)/shard_map/ppermute | solution.py:872
  94.4 18.5 %collective-permute-start.10 = (bf16[2,192,1024]{2,1,0:T(8,128)(2,1)S(1)}, bf16[2,192,1024]{2,1,0:T(8,128)(2,1)S(1)}, u32[]{:S(2)}, u32[]{:S(2)}) collective-permute-start(bf16[2,192,1024]{2,1,0:T(8,128)(2,1)S(1)} %pad_maximum_fusion.12), channel_id=1, source_target_pairs={{0,8},{8,0},{16,24},{24,16},{1,9},{9,1},{17,25},{25,17},{2,10},{10... | collective-permute-start | bytes 2359304 | tf_op jit(solution)/shard_map/ppermute | solution.py:873
  108.7 25.0 %collective-permute-start.13 = (bf16[192,3072]{1,0:T(8,128)(2,1)}, bf16[192,3072]{1,0:T(8,128)(2,1)}, u32[]{:S(2)}, u32[]{:S(2)}) collective-permute-start(bf16[192,3072]{1,0:T(8,128)(2,1)} %get-tuple-element.154), channel_id=1, source_target_pairs={{0,8},{8,0},{16,24},{24,16},{1,9},{9,1},{17,25},{25,17},{2,10},{10... | collective-permute-start | bytes 3538952 | tf_op jit(solution)/shard_map/ppermute | solution.py:894
  108.7 35.1 %collective-permute-start.14 = (bf16[192,3072]{1,0:T(8,128)(2,1)}, bf16[192,3072]{1,0:T(8,128)(2,1)}, u32[]{:S(2)}, u32[]{:S(2)}) collective-permute-start(bf16[192,3072]{1,0:T(8,128)(2,1)} %get-tuple-element.153), channel_id=1, source_target_pairs={{0,16},{8,24},{16,0},{24,8},{1,17},{9,25},{17,1},{25,9},{2,18},{10... | collective-permute-start | bytes 3538952 | tf_op jit(solution)/shard_map/ppermute | solution.py:894
  110.2 52.8 %collective-permute-start.15 = (bf16[192,3072]{1,0:T(8,128)(2,1)}, bf16[192,3072]{1,0:T(8,128)(2,1)}, u32[]{:S(2)}, u32[]{:S(2)}) collective-permute-start(bf16[192,3072]{1,0:T(8,128)(2,1)} %get-tuple-element.152), channel_id=1, source_target_pairs={{0,24},{8,16},{16,8},{24,0},{1,25},{9,17},{17,9},{25,1},{2,26},{10... | collective-permute-start | bytes 3538952 | tf_op jit(solution)/shard_map/ppermute | solution.py:894
  115.8 21.3 %all-to-all-start.3 = ((bf16[8,48,768]{2,1,0:T(8,128)(2,1)}), bf16[8,48,768]{2,1,0:T(8,128)(2,1)S(1)}, u32[]{:S(2)}, u32[]{:S(2)}) async-start(bf16[8,48,768]{2,1,0:T(8,128)(2,1)} %bitcast.40), calls=%async_computation.3 | async-start | bytes 1179648 | tf_op jit(solution)/shard_map/all_to_all | solution.py:881
  127.5 35.4 %collective-permute-start.16 = (bf16[768,768]{1,0:T(8,128)(2,1)}, bf16[768,768]{1,0:T(8,128)(2,1)}, u32[]{:S(2)}, u32[]{:S(2)}) collective-permute-start(bf16[768,768]{1,0:T(8,128)(2,1)} %get-tuple-element.150), channel_id=1, source_target_pairs={{0,8},{8,0},{16,24},{24,16},{1,9},{9,1},{17,25},{25,17},{2,10},{10... | collective-permute-start | bytes 3538952 | tf_op jit(solution)/shard_map/ppermute | solution.py:894
  128.3 58.3 %collective-permute-start.17 = (bf16[768,768]{1,0:T(8,128)(2,1)}, bf16[768,768]{1,0:T(8,128)(2,1)}, u32[]{:S(2)}, u32[]{:S(2)}) collective-permute-start(bf16[768,768]{1,0:T(8,128)(2,1)} %get-tuple-element.149), channel_id=1, source_target_pairs={{0,16},{8,24},{16,0},{24,8},{1,17},{9,25},{17,1},{25,9},{2,18},{10... | collective-permute-start | bytes 3538952 | tf_op jit(solution)/shard_map/ppermute | solution.py:894
  133.7 78.9 %collective-permute-start.18 = (bf16[768,768]{1,0:T(8,128)(2,1)}, bf16[768,768]{1,0:T(8,128)(2,1)}, u32[]{:S(2)}, u32[]{:S(2)}) collective-permute-start(bf16[768,768]{1,0:T(8,128)(2,1)} %get-tuple-element.148), channel_id=1, source_target_pairs={{0,24},{8,16},{16,8},{24,0},{1,25},{9,17},{17,9},{25,1},{2,26},{10... | collective-permute-start | bytes 3538952 | tf_op jit(solution)/shard_map/ppermute | solution.py:894
  137.0 25.9 %all-to-all-start.2 = ((bf16[8,48,768]{2,1,0:T(8,128)(2,1)}), bf16[8,48,768]{2,1,0:T(8,128)(2,1)S(1)}, u32[]{:S(2)}, u32[]{:S(2)}) async-start(bf16[8,48,768]{2,1,0:T(8,128)(2,1)} %bitcast.34), calls=%async_computation.2 | async-start | bytes 1179648 | tf_op jit(solution)/shard_map/all_to_all | solution.py:881
  235.7 34.0 %all-to-all-start.4 = ((bf16[8,48,1536]{2,1,0:T(8,128)(2,1)}), bf16[8,48,1536]{2,1,0:T(8,128)(2,1)S(1)}, u32[]{:S(2)}, u32[]{:S(2)}) async-start(bf16[8,48,1536]{2,1,0:T(8,128)(2,1)} %bitcast.143), calls=%async_computation.4 | async-start | bytes 2359296 | tf_op jit(solution)/shard_map/all_to_all | solution.py:881
  280.1 21.9 %collective-permute-start.21 = (bf16[384,640]{1,0:T(8,128)(2,1)}, bf16[384,640]{1,0:T(8,128)(2,1)}, u32[]{:S(2)}, u32[]{:S(2)}) collective-permute-start(bf16[384,640]{1,0:T(8,128)(2,1)} %get-tuple-element.160), channel_id=1, source_target_pairs={{0,24},{8,16},{16,8},{24,0},{1,25},{9,17},{17,9},{25,1},{2,26},{10... | collective-permute-start | bytes 1474568 | tf_op jit(solution)/shard_map/ppermute | solution.py:902
  283.2 61.5 %collective-permute-start.30 = (bf16[768,768]{1,0:T(8,128)(2,1)}, bf16[768,768]{1,0:T(8,128)(2,1)S(1)}, u32[]{:S(2)}, u32[]{:S(2)}) collective-permute-start(bf16[768,768]{1,0:T(8,128)(2,1)} %get-tuple-element.67), channel_id=1, source_target_pairs={{0,8},{8,0},{16,24},{24,16},{1,9},{9,1},{17,25},{25,17},{2,10},{10... | collective-permute-start | bytes 3538952 | tf_op jit(solution)/shard_map/ppermute | solution.py:902
  283.7 62.0 %collective-permute-start.31 = (bf16[768,768]{1,0:T(8,128)(2,1)}, bf16[768,768]{1,0:T(8,128)(2,1)S(1)}, u32[]{:S(2)}, u32[]{:S(2)}) collective-permute-start(bf16[768,768]{1,0:T(8,128)(2,1)} %get-tuple-element.68), channel_id=1, source_target_pairs={{0,16},{8,24},{16,0},{24,8},{1,17},{9,25},{17,1},{25,9},{2,18},{10... | collective-permute-start | bytes 3538952 | tf_op jit(solution)/shard_map/ppermute | solution.py:902
  290.8 62.1 %collective-permute-start.32 = (bf16[768,768]{1,0:T(8,128)(2,1)}, bf16[768,768]{1,0:T(8,128)(2,1)S(1)}, u32[]{:S(2)}, u32[]{:S(2)}) collective-permute-start(bf16[768,768]{1,0:T(8,128)(2,1)} %get-tuple-element.69), channel_id=1, source_target_pairs={{0,24},{8,16},{16,8},{24,0},{1,25},{9,17},{17,9},{25,1},{2,26},{10... | collective-permute-start | bytes 3538952 | tf_op jit(solution)/shard_map/ppermute | solution.py:902
  337.6 89.4 %all-to-all-start.5 = ((bf16[8,112,768]{2,1,0:T(8,128)(2,1)}), bf16[8,112,768]{2,1,0:T(8,128)(2,1)}, u32[]{:S(2)}, u32[]{:S(2)}) async-start(bf16[8,112,768]{2,1,0:T(8,128)(2,1)} %get-tuple-element.56), calls=%async_computation.5 | async-start | bytes 2752512 | tf_op jit(solution)/shard_map/all_to_all | solution.py:881
  343.5 19.5 %collective-permute-start.23 = (bf16[208,1024]{1,0:T(8,128)(2,1)}, bf16[208,1024]{1,0:T(8,128)(2,1)}, u32[]{:S(2)}, u32[]{:S(2)}) collective-permute-start(bf16[208,1024]{1,0:T(8,128)(2,1)} %get-tuple-element.54), channel_id=1, source_target_pairs={{0,16},{8,24},{16,0},{24,8},{1,17},{9,25},{17,1},{25,9},{2,18},{10... | collective-permute-start | bytes 1277960 | tf_op jit(solution)/shard_map/ppermute | solution.py:902
  344.7 26.3 %collective-permute-start.24 = (bf16[208,1024]{1,0:T(8,128)(2,1)}, bf16[208,1024]{1,0:T(8,128)(2,1)}, u32[]{:S(2)}, u32[]{:S(2)}) collective-permute-start(bf16[208,1024]{1,0:T(8,128)(2,1)} %get-tuple-element.55), channel_id=1, source_target_pairs={{0,24},{8,16},{16,8},{24,0},{1,25},{9,17},{17,9},{25,1},{2,26},{10... | collective-permute-start | bytes 1277960 | tf_op jit(solution)/shard_map/ppermute | solution.py:902
  345.7 50.3 %collective-permute-start.29 = (bf16[192,3072]{1,0:T(8,128)(2,1)}, bf16[192,3072]{1,0:T(8,128)(2,1)S(1)}, u32[]{:S(2)}, u32[]{:S(2)}) collective-permute-start(bf16[192,3072]{1,0:T(8,128)(2,1)} %get-tuple-element.65), channel_id=1, source_target_pairs={{0,24},{8,16},{16,8},{24,0},{1,25},{9,17},{17,9},{25,1},{2,26},{10... | collective-permute-start | bytes 3538952 | tf_op jit(solution)/shard_map/ppermute | solution.py:902
  352.9 67.0 %collective-permute-start.28 = (bf16[192,3072]{1,0:T(8,128)(2,1)}, bf16[192,3072]{1,0:T(8,128)(2,1)S(1)}, u32[]{:S(2)}, u32[]{:S(2)}) collective-permute-start(bf16[192,3072]{1,0:T(8,128)(2,1)} %get-tuple-element.63), channel_id=1, source_target_pairs={{0,16},{8,24},{16,0},{24,8},{1,17},{9,25},{17,1},{25,9},{2,18},{10... | collective-permute-start | bytes 3538952 | tf_op jit(solution)/shard_map/ppermute | solution.py:902
  354.1 65.8 %collective-permute-start.27 = (bf16[192,3072]{1,0:T(8,128)(2,1)}, bf16[192,3072]{1,0:T(8,128)(2,1)S(1)}, u32[]{:S(2)}, u32[]{:S(2)}) collective-permute-start(bf16[192,3072]{1,0:T(8,128)(2,1)} %get-tuple-element.61), channel_id=1, source_target_pairs={{0,8},{8,0},{16,24},{24,16},{1,9},{9,1},{17,25},{25,17},{2,10},{10... | collective-permute-start | bytes 3538952 | tf_op jit(solution)/shard_map/ppermute | solution.py:902
  (61 other events, 729.4 us)

commit v2 on v1

--- a/solution.py
+++ b/solution.py
@@ -586,15 +586,8 @@
             dn1_acc[d] = dn1.astype(BF16)
             dn1_x = dn1 * x_ref[rows, :].astype(F32)
             inner = inner + jnp.sum(dn1_x * col_ref[rows, :], axis=0, keepdims=True)
-            gain_rows.append(
-                lax.dot_general(
-                    jnp.broadcast_to(r1, (8, keys)),
-                    dn1_x,
-                    NT,
-                    precision=lax.Precision.HIGHEST,
-                    preferred_element_type=F32,
-                )[:1]
-            )
+            gain = jnp.sum(dn1_x * r1, axis=1, keepdims=True)
+            gain_rows.append(jnp.transpose(jnp.broadcast_to(gain, (part, LANES)))[:1])
         cells = hist[...]
         same = lax.broadcasted_iota(I32, cells.shape, 0) % PAIR_ROWS == (
             lax.broadcasted_iota(I32, cells.shape, 1) % PAIR_ROWS
@@ -622,38 +615,44 @@
             preferred_element_type=F32,
         )
         table = exact(exact(sum_rows, cells), sum_cols)
-        table_row = jnp.concatenate([table[n : n + 1] for n in range(LOW_BINS)], axis=1)
-        pad = jnp.zeros((1, keys - width), F32)
-        gain_row = jnp.concatenate(gain_rows + [pad], axis=1)
-        gain_two_row = jnp.concatenate([gain_two_ref[...], pad], axis=1)
-        extra = jnp.concatenate([inner, gain_row, gain_two_row, table_row], axis=0)
-        extra_high = extra.astype(BF16).astype(F32)
+        half = LOW_BINS // 2
+        tail = jnp.zeros((1, width - half * LANES), F32)
+        table_rows = [
+            jnp.concatenate([table[n + m : n + m + 1] for m in range(half)] + [tail], axis=1)
+            for n in (0, half)
+        ]
+        small = jnp.concatenate(
+            [jnp.concatenate(gain_rows, axis=1), gain_two_ref[...]] + table_rows, axis=0
+        )
+        inner_high = inner.astype(BF16).astype(F32)
         extra = jnp.concatenate(
-            [extra_high, extra - extra_high, jnp.zeros((PAIR_ROWS - 8, keys), F32)], axis=0
+            [inner_high, inner - inner_high, jnp.zeros((PAIR_ROWS - 2, keys), F32)], axis=0
         ).astype(BF16)
         for k in range(count):
             dn1_refs[k][:part, :] = dn1_acc[me ^ k]
             dn1_refs[k][part:, :] = extra
         router = jnp.transpose(router_acc[...])
-        router_high = router.astype(BF16).astype(F32)
-        router_low = router - router_high
         band = width // cols
         share = experts // cols
-        blank = jnp.zeros((PAIR_ROWS - 2 * share, width), F32)
         pad = jnp.zeros((share, width - part), F32)
-        dqkv_all, da_all = dqkv[...], da_ref[...]
+        pieces_of = lambda a, first: a[first : first + band, :]
+        halves = part // band
+        for b in range(halves):
+            three = jnp.concatenate(
+                [pieces_of(dqkv, w * part + b * band) for w in range(3)], axis=0
+            )
+            da_part = pieces_of(da_ref, b * band)
+            for c in range(cols):
+                rows = slice(c * band, (c + 1) * band)
+                proj_ref[c, :band, b * 4 * band : (b + 1) * 4 * band] = jnp.concatenate(
+                    [mm(n1_ref[rows, :], three, NT), mm(ofull_ref[rows, :], da_part, NT)], axis=1
+                ).astype(BF16)
         for c in range(cols):
-            rows = slice(c * band, (c + 1) * band)
-            proj_ref[c, :band, : 3 * part] = mm(n1_ref[rows, :], dqkv_all, NT).astype(BF16)
-            proj_ref[c, :band, 3 * part :] = mm(ofull_ref[rows, :], da_all, NT).astype(BF16)
-            own = slice(c * share, (c + 1) * share)
+            own = jnp.concatenate([router[c * share : (c + 1) * share], pad], axis=1)
+            facts = jnp.concatenate([own, small], axis=0)
+            facts_high = facts.astype(BF16).astype(F32)
             proj_ref[c, band:, :] = jnp.concatenate(
-                [
-                    jnp.concatenate([router_high[own], pad], axis=1),
-                    jnp.concatenate([router_low[own], pad], axis=1),
-                    blank,
-                ],
-                axis=0,
+                [facts_high, facts - facts_high], axis=0
             ).astype(BF16)
 
 
@@ -706,15 +705,17 @@
     return out[0], out[1], out[2], out[3:]
 
 
-def expert_kernel(count, place_ref, x_ref, dy_ref, router_ref, *refs):
-    in_refs, eout_refs = refs[:count], refs[count : 2 * count]
-    back_ref = refs[2 * count]
-    gi_refs = refs[2 * count + 1 : 3 * count + 1]
-    ge_refs = refs[3 * count + 1 : 4 * count + 1]
-    win, eout, dys, y_acc, dx_acc, gi = refs[4 * count + 1 :]
+def fill_rows(place_ref, places, in_refs, win, part):
+    for in_ref, (k, offset) in zip(in_refs, places):
+        first = pl.multiple_of((place_ref[0] ^ k) * part + offset, PAIR_ROWS)
+        win[pl.ds(first, in_ref.shape[0]), :] = in_ref[...]
+
+
+def inner_kernel(count, places, place_ref, x_ref, dy_ref, router_ref, *refs):
+    in_refs, refs = refs[: len(places)], refs[len(places) :]
+    dys_ref, hidden_ref, slope_ref = refs[:3]
+    ge_refs, win = refs[3 : 3 + count], refs[3 + count]
     step = pl.program_id(0)
-    me = place_ref[0]
-    part = in_refs[0].shape[0]
 
     @pl.when(step == 0)
     def _():
@@ -723,36 +724,53 @@
         own = lax.broadcasted_iota(I32, logits.shape, 1) == place_ref[1]
         gate = jnp.sum(jnp.where(own, probs, 0.0), axis=1, keepdims=True)
         gate = gate / jnp.sum(probs, axis=1, keepdims=True)
-        dys[...] = (gate * dy_ref[...].astype(F32)).astype(BF16)
-        y_acc[...] = jnp.zeros_like(y_acc)
-        dx_acc[...] = jnp.zeros_like(dx_acc)
-
-    for k in range(count):
-        win[pl.ds(pl.multiple_of((me ^ k) * part, part), part), :] = in_refs[k][...]
-
-        @pl.when(step == k)
-        def _(k=k):
-            eout[...] = eout_refs[k][...]
-
+        dys_ref[...] = (gate * dy_ref[...].astype(F32)).astype(BF16)
+
+    fill_rows(place_ref, places, in_refs, win, win.shape[0] // count)
     pre = mm(x_ref[...], win[...], NN)
     square = pre * pre
     curve = jnp.tanh(GELU_SCALE * pre * (1.0 + GELU_CUBE * square))
     half = 0.5 * (1.0 + curve)
     hidden = (pre * half).astype(BF16)
+    hidden_ref[...] = hidden
     slope = half + 0.5 * pre * (1.0 - curve * curve) * (
         GELU_SCALE * (1.0 + 3.0 * GELU_CUBE * square)
     )
-    dpre = (mm(dys[...], eout[...], NT) * slope).astype(BF16)
-    y_acc[...] += mm(hidden, eout[...], NN)
-    dx_acc[...] += mm(dpre, win[...], NT)
-    ge = mm(hidden, dys[...], TN).astype(BF16)
-    gi[...] = mm(x_ref[...], dpre, TN).astype(BF16)
+    slope_ref[...] = slope.astype(BF16)
+    ge = mm(hidden, dys_ref[...], TN).astype(BF16)
     for k in range(count):
-        gi_refs[k][...] = gi[pl.ds(pl.multiple_of((me ^ k) * part, part), part), :]
 
         @pl.when(step == k)
         def _(k=k):
             ge_refs[k][...] = ge
+
+
+def outer_kernel(count, places, place_ref, x_ref, dys_ref, hidden_ref, slope_ref, *refs):
+    in_refs, refs = refs[: len(places)], refs[len(places) :]
+    eout_refs, back_ref = refs[:count], refs[count]
+    gi_refs = refs[count + 1 : 2 * count + 1]
+    win, eout, y_acc, dx_acc, gi = refs[2 * count + 1 :]
+    step = pl.program_id(0)
+    part = gi_refs[0].shape[0]
+
+    @pl.when(step == 0)
+    def _():
+        y_acc[...] = jnp.zeros_like(y_acc)
+        dx_acc[...] = jnp.zeros_like(dx_acc)
+
+    fill_rows(place_ref, places, in_refs, win, part)
+    for k in range(count):
+
+        @pl.when(step == k)
+        def _(k=k):
+            eout[...] = eout_refs[k][...]
+
+    y_acc[...] += mm(hidden_ref[...], eout[...], NN)
+    dpre = (mm(dys_ref[...], eout[...], NT) * slope_ref[...].astype(F32)).astype(BF16)
+    dx_acc[...] += mm(dpre, win[...], NT)
+    gi[...] = mm(x_ref[...], dpre, TN).astype(BF16)
+    for k in range(count):
+        gi_refs[k][...] = gi[pl.ds(pl.multiple_of((place_ref[0] ^ k) * part, part), part), :]
 
     @pl.when(step == count - 1)
     def _():
@@ -761,39 +779,64 @@
         back_ref[:, width:] = dx_acc[...].astype(BF16)
 
 
-def expert_work(place, x, dy, router, in_held, eout_held):
-    count = len(in_held)
+def expert_inner(place, x, dy, router, in_held, places, count):
     slots, width = x.shape
-    part, hidden_width = in_held[0].shape
+    hidden_width = in_held[0].shape[1]
     chunk = hidden_width // count
-    fixed = lambda a: pl.BlockSpec(a.shape, lambda i, m: (0, 0))
-    lanes = pl.BlockSpec((part, chunk), lambda i, m: (0, m[0] ^ i))
+    fixed = lambda shape: pl.BlockSpec(shape, lambda i, m: (0, 0))
+    wide = pl.BlockSpec((slots, chunk), lambda i, m: (0, i))
     shape = lambda s: jax.ShapeDtypeStruct(s, BF16)
     out = pl.pallas_call(
-        functools.partial(expert_kernel, count),
+        functools.partial(inner_kernel, count, places),
         grid_spec=pltpu.PrefetchScalarGridSpec(
             num_scalar_prefetch=1,
             grid=(count,),
-            in_specs=[fixed(x), fixed(dy), fixed(router)]
-            + [lanes] * count
-            + [fixed(eout_held[0])] * count,
-            out_specs=[pl.BlockSpec((slots, 2 * width), lambda i, m: (0, 0))] + [lanes] * count + [fixed(eout_held[0])] * count,
+            in_specs=[fixed(x.shape), fixed(dy.shape), fixed(router.shape)]
+            + [pl.BlockSpec((a.shape[0], chunk), lambda i, m: (0, m[0] ^ i)) for a in in_held],
+            out_specs=[fixed(x.shape), wide, wide] + [fixed((chunk, width))] * count,
+            scratch_shapes=[pltpu.VMEM((width, chunk), BF16)],
+        ),
+        out_shape=[shape(x.shape)]
+        + [shape((slots, hidden_width))] * 2
+        + [shape((chunk, width))] * count,
+        compiler_params=pltpu.CompilerParams(vmem_limit_bytes=56 * 2**20),
+        cost_estimate=QUICK,
+    )(place, x, dy, router, *in_held)
+    return out[0], out[1], out[2], out[3:]
+
+
+def expert_outer(place, x, dys, hidden, slope, in_held, places, eout_held):
+    count = len(eout_held)
+    slots, width = x.shape
+    hidden_width = in_held[0].shape[1]
+    part = width // count
+    chunk = hidden_width // count
+    fixed = lambda shape: pl.BlockSpec(shape, lambda i, m: (0, 0))
+    wide = pl.BlockSpec((slots, chunk), lambda i, m: (0, i))
+    lanes = lambda rows: pl.BlockSpec((rows, chunk), lambda i, m: (0, m[0] ^ i))
+    out = pl.pallas_call(
+        functools.partial(outer_kernel, count, places),
+        grid_spec=pltpu.PrefetchScalarGridSpec(
+            num_scalar_prefetch=1,
+            grid=(count,),
+            in_specs=[fixed(x.shape), fixed(x.shape), wide, wide]
+            + [lanes(a.shape[0]) for a in in_held]
+            + [fixed((chunk, width))] * count,
+            out_specs=[fixed((slots, 2 * width))] + [lanes(part)] * count,
             scratch_shapes=[
                 pltpu.VMEM((width, chunk), BF16),
                 pltpu.VMEM((chunk, width), BF16),
-                pltpu.VMEM((slots, width), BF16),
                 pltpu.VMEM((slots, width), F32),
                 pltpu.VMEM((slots, width), F32),
                 pltpu.VMEM((width, chunk), BF16),
             ],
         ),
-        out_shape=[shape((slots, 2 * width))]
-        + [shape((part, hidden_width))] * count
-        + [shape((chunk, width))] * count,
+        out_shape=[jax.ShapeDtypeStruct((slots, 2 * width), BF16)]
+        + [jax.ShapeDtypeStruct((part, hidden_width), BF16)] * count,
         compiler_params=pltpu.CompilerParams(vmem_limit_bytes=56 * 2**20),
         cost_estimate=QUICK,
-    )(place, x, dy, router, *in_held, *eout_held)
-    return out[0], out[1 : 1 + count], out[1 + count :]
+    )(place, x, dys, hidden, slope, *in_held, *eout_held)
+    return out[0], out[1:]
 
 
 def slot_kernel(
@@ -808,10 +851,11 @@
     router_ref,
     out_ref,
     gain_ref,
-    parcel_ref,
     gain_part_ref,
+    *refs,
 ):
     me = place_ref[0]
+    parcel_refs, parcel = refs[:count], refs[count]
     slots, width = dy_ref.shape
     part = width // count
     y = home_ref[:, :width]
@@ -837,9 +881,9 @@
         span = slice(d * part, (d + 1) * part)
         router = jnp.concatenate([router_high[span], router_low[span]], axis=1)
         router = jnp.concatenate([router, fill], axis=0)
-        parcel_ref[me ^ d] = jnp.concatenate(
-            [y[:, span], da[:, span], do[:, span], router], axis=1
-        )
+        parcel[me ^ d] = jnp.concatenate([y[:, span], da[:, span], do[:, span], router], axis=1)
+    for k in range(count):
+        parcel_refs[k][...] = parcel[k]
 
 
 def slot_work(place, home, dy, n2, h1, scalars, router, out_proj, gain, count):
@@ -848,35 +892,43 @@
     lanes = 3 * width // count + 2 * experts
     fixed = lambda a: pl.BlockSpec(a.shape, lambda i, m: (0,) * len(a.shape))
     ins = (home, dy, n2, h1, scalars, router, out_proj, gain)
-    outs = [
-        jax.ShapeDtypeStruct((count, slots, lanes), BF16),
-        jax.ShapeDtypeStruct((1, width), F32),
-    ]
-    return pl.pallas_call(
+    outs = [jax.ShapeDtypeStruct((1, width), F32)]
+    outs += [jax.ShapeDtypeStruct((slots, lanes), BF16)] * count
+    out = pl.pallas_call(
         functools.partial(slot_kernel, count, experts),
         grid_spec=pltpu.PrefetchScalarGridSpec(
             num_scalar_prefetch=1,
             grid=(1,),
             in_specs=[fixed(a) for a in ins],
             out_specs=[fixed(a) for a in outs],
+            scratch_shapes=[pltpu.VMEM((count, slots, lanes), BF16)],
         ),
         out_shape=outs,
         compiler_params=pltpu.CompilerParams(vmem_limit_bytes=48 * 2**20),
         cost_estimate=QUICK,
     )(place, *ins)
-
-
-def row_gather(block):
+    return out[1:], out[0]
+
+
+def send(piece, offset):
+    count = lax.axis_size("row")
+    return lax.ppermute(piece, "row", [(i, i ^ offset) for i in range(count)])
+
+
+def row_join(block, far):
     me = lax.axis_index("row")
     count = lax.axis_size("row")
-    far = lax.ppermute(block, "row", [(i, i ^ 2) for i in range(count)])
-    near = lax.ppermute(jnp.stack([block, far]), "row", [(i, i ^ 1) for i in range(count)])
+    near = send(jnp.stack([block, far]), 1)
     held = jnp.stack([block, near[0], far, near[1]])
     return jnp.concatenate(
         [lax.dynamic_index_in_dim(held, p ^ me, 0, keepdims=True) for p in range(count)]
     )
 
 
+def row_gather(block):
+    return row_join(block, send(block, 2))
+
+
 def swap(blocks, axis):
     return lax.all_to_all(blocks, axis, 0, 0)
 
@@ -888,19 +940,12 @@
 
 def trade(piece_for):
     me = lax.axis_index("row")
-    count = lax.axis_size("row")
-    away = [k for k in (2, 3, 1)]
-    held = {
-        k: lax.ppermute(piece_for(me ^ k), "row", [(i, i ^ k) for i in range(count)]) for k in away
-    }
-    return [piece_for(me)] + [held[k] for k in range(1, count)]
+    return trade_pieces([piece_for(me ^ k) for k in range(lax.axis_size("row"))])
 
 
 def trade_pieces(pieces):
     count = len(pieces)
-    held = {
-        k: lax.ppermute(pieces[k], "row", [(i, i ^ k) for i in range(count)]) for k in (2, 3, 1)
-    }
+    held = {k: send(pieces[k], k) for k in (2, 3, 1)}
     return [pieces[0]] + [held[k] for k in range(1, count)]
 
 
@@ -982,28 +1027,31 @@
     doc_ids = segment[0]
     expert_ids = expert[0, :, 0]
 
-    tok_low = row_gather(tokens[0]).reshape(width, seq_len)
-    qkv_part = jnp.concatenate([w_query, w_key, w_value], axis=1)
-    qkv_cols = col_gather(qkv_part)
+    tok_far = send(tokens[0], 2)
+    tok_low = row_join(tokens[0], tok_far).reshape(width, seq_len)
+    qkv_cols = col_gather(jnp.concatenate([w_query, w_key, w_value], axis=1))
+    same_doc = own_rows(doc_ids, me, tok_rows)[:, None] == doc_ids[None, :]
+    masked = jnp.where(same_doc, after(bucket, tok_far)[0], buckets).astype(BF16)
+    idx_far = send(masked, 2)
+    cot_own = cotangent[0]
+    cot_far = send(cot_own, 2)
+    lane_cut = lambda array, count, k: lax.dynamic_slice_in_dim(array, (me ^ k) * count, count, 1)
+    half = part // 2
+    in_first = send(lane_cut(after(w_in, tok_far)[:half], hidden_width, 2), 2)
+    qkv_cols = after(qkv_cols, idx_far, cot_far, in_first)
+    out_part = after(jnp.concatenate([w_out, w_router], axis=1), qkv_cols)
+    out_gathered = col_gather(out_part)
     qkv_cols = qkv_cols.reshape(rows, share, part, 3 * out_cols)
-    qkv_rows = lay(trade(lambda d: lax.dynamic_index_in_dim(qkv_cols, d, 0, keepdims=False)))
+    qkv_held = trade(lambda d: lax.dynamic_index_in_dim(qkv_cols, d, 0, keepdims=False))
+    second_cut = lane_cut(after(w_in, idx_far)[half:], hidden_width, 2)
+    in_second = send(after(second_cut, qkv_cols), 2)
+    eout_cuts = [lane_cut(after(w_expert_out, qkv_cols), width, k) for k in range(rows)]
+    qkv_held = after(tuple(qkv_held), in_second, *eout_cuts)
     qkv_own = jnp.transpose(
-        qkv_rows.reshape(rows, share, part, 3, out_cols), (0, 2, 3, 1, 4)
+        lay(qkv_held).reshape(rows, share, part, 3, out_cols), (0, 2, 3, 1, 4)
     ).reshape(width, 3 * part)
-    same_doc = own_rows(doc_ids, me, tok_rows)[:, None] == doc_ids[None, :]
-    masked = jnp.where(same_doc, bucket[0], buckets).astype(BF16)
-    idx = row_gather(masked).reshape(seq_len, seq_len)
-    low_cols = col_gather(after(jnp.concatenate([w_out, w_router], axis=1), qkv_cols))
-    out_rows = jnp.transpose(low_cols[:, :, :out_cols], (1, 0, 2)).reshape(part, width)
-    router_rows = jnp.transpose(low_cols[:, :, out_cols:], (1, 0, 2)).reshape(part, experts)
-    out_router = row_gather(jnp.concatenate([out_rows, router_rows], axis=1)).reshape(
-        width, width + experts
-    )
-    out_full, router_full = out_router[:, :width], out_router[:, width:]
-    cot_low = row_gather(after(cotangent[0], qkv_rows, idx)).reshape(width, seq_len)
-    lane_cut = lambda array, count: lambda d: lax.dynamic_slice_in_dim(array, d * count, count, 1)
-    w_in = after(w_in, qkv_rows)
-    in_held = trade(lane_cut(w_in, hidden_width))
+    idx = row_join(masked, idx_far).reshape(seq_len, seq_len)
+    cot_low = row_join(cot_own, cot_far).reshape(width, seq_len)
 
     picked = expert_ids[None, :] == jnp.arange(experts, dtype=I32)[:, None]
     picked_float = picked.astype(F32)
@@ -1018,15 +1066,34 @@
     r1 = lax.rsqrt(jnp.mean(x * x, axis=0) + NORM_EPS)
     n1 = (x * r1 * gain_one[:, None]).astype(BF16)
     qkv = mm(qkv_own, n1, TN).astype(BF16)
+    later_in = after(w_in, tok_low)
+    in_places = ((0, 0), (2, 0), (2, half), (3, 0), (1, 0))
+    in_held = [lane_cut(later_in, hidden_width, 0), in_first, in_second]
+    for k in (3, 1):
+        in_held.append(send(after(lane_cut(later_in, hidden_width, k), qkv), k))
+    qkv, n1, qkv_own = lax.optimization_barrier((qkv, n1, qkv_own))
     q, k, v = qkv[:part], qkv[part : 2 * part], qkv[2 * part :]
     table = lax.dynamic_slice_in_dim(jnp.transpose(bias_table), me * heads, heads, 0)
     table = jnp.pad(
         table, ((0, 8 - heads), (0, LANES - buckets)), constant_values=NEG_FILL
     )
-    o32, p = attend(q, k, v, idx, table, heads, 128)
-    o_full = row_gather(o32.astype(BF16)).reshape(width, seq_len)
-    w_expert_out = after(w_expert_out, o_full)
-    eout_held = trade(lane_cut(w_expert_out, width))
+    o32, p = attend(q, k, v, idx, table, heads, 256)
+    expert_at = lambda a: swap(a.reshape(cols, CAPACITY, width), "col").reshape(slots, width)
+    dy_low = mm(choose, cot_low, NT).astype(BF16)
+    o_low = after(o32.astype(BF16), in_held[3])
+    dy_slots = expert_at(dy_low)
+    o_far = send(o_low, 2)
+    o_full = row_join(o_low, o_far).reshape(width, seq_len)
+    out_gathered = after(out_gathered, o32)
+    out_rows = jnp.transpose(out_gathered[:, :, :out_cols], (1, 0, 2)).reshape(part, width)
+    router_rows = jnp.transpose(out_gathered[:, :, out_cols:], (1, 0, 2)).reshape(part, experts)
+    out_router = jnp.concatenate([out_rows, router_rows], axis=1)
+    out_router = row_gather(out_router).reshape(width, width + experts)
+    out_full, router_full = out_router[:, :width], out_router[:, width:]
+    eout_two = send(after(eout_cuts[2], o_far), 2)
+    eout_one = send(after(eout_cuts[1], o_full), 1)
+    eout_three = send(after(eout_cuts[3], o_full), 3)
+    eout_held = [eout_cuts[0], eout_one, eout_two, eout_three]
     h1 = x + mm(out_full, o_full, TN)
     r2 = lax.rsqrt(jnp.mean(h1 * h1, axis=0) + NORM_EPS)
     n2 = (h1 * r2 * gain_two[:, None]).astype(BF16)
@@ -1034,19 +1101,30 @@
     g = jax.nn.softmax(logits, axis=0)
     gate = jnp.sum(g * picked_float, axis=0)
 
-    expert_at = lambda a: swap(a.reshape(cols, CAPACITY, width), "col").reshape(slots, width)
-    dy_low = mm(choose, cot_low, NT).astype(BF16)
-    dy_slots = expert_at(dy_low)
     n2_low = mm(choose, n2, NT).astype(BF16)
-    slots_in = expert_at(n2_low)
+    slots_in = expert_at(after(n2_low, eout_two))
     place = jnp.stack([me, col * rows + me]).astype(I32)
-    back, in_pieces, eout_pieces = expert_work(
-        place, slots_in, dy_slots, router_full, in_held, eout_held
-    )
-    grad_eout_held = trade_pieces(eout_pieces)
+    dys, hidden, slope, eout_pieces = expert_inner(
+        place, slots_in, dy_slots, router_full, in_held, in_places, rows
+    )
+    hidden = after(hidden, *eout_pieces)
+    back, in_pieces = expert_outer(
+        place, slots_in, dys, hidden, slope, in_held, in_places, eout_held
+    )
+    eout_half = w_expert_out.shape[0] // 2
+    grad_eout_half = send(eout_pieces[2][:eout_half], 2)
+    back = after(back, grad_eout_half)
+    grad_eout_held = [
+        eout_pieces[0],
+        send(after(eout_pieces[1], back), 1),
+        send(after(eout_pieces[2][eout_half:], back), 2),
+        send(after(eout_pieces[3], back), 3),
+    ]
     home = swap(back.reshape(cols, CAPACITY, 2 * width), "col").reshape(slots, 2 * width)
 
     h1_s = mm(choose, h1.astype(BF16), NT).astype(BF16)
+    h1_own = own_rows(h1, me, part)
+    home = after(home, grad_eout_held[2], h1_own)
     scalars = lax.dot_general(
         choose.astype(F32),
         jnp.concatenate([g, gate[None], r2[None]], axis=0),
@@ -1057,8 +1135,14 @@
     parcel, gain_two_part = slot_work(
         place, home, dy_low, n2_low, h1_s, scalars, router_full, out_full, gain_two[None], rows
     )
-    parcel = trade_pieces([parcel[k] for k in range(rows)])
-    grad_in_held = trade_pieces([after(piece, parcel[2]) for piece in in_pieces])
+    parcel = trade_pieces(after(tuple(parcel), grad_eout_held[3]))
+    in_turn = lambda piece: after(piece, parcel[2], parcel[3])
+    grad_in_held = [
+        in_pieces[0],
+        send(in_turn(in_pieces[1]), 1),
+        send(in_turn(in_pieces[2]), 2),
+    ]
+    grad_in_half = send(in_turn(in_pieces[3][:half]), 3)
 
     layer_out, da, proj_parcel, dn1_parcel = attend_back(
         place,
@@ -1069,7 +1153,7 @@
         p,
         o32,
         slot[None],
-        own_rows(h1, me, part),
+        h1_own,
         jnp.stack([r1, gate]),
         gain_one[:, None],
         tok_low,
@@ -1080,21 +1164,16 @@
         parcel,
         cols,
         buckets,
-        128,
-    )
-    dn1_sum = sum(piece.astype(F32) for piece in trade_pieces(dn1_parcel))
+        256,
+    )
+    dn1_parcel, proj_parcel = after(
+        (tuple(dn1_parcel), proj_parcel), grad_in_half, grad_in_held[2]
+    )
+    dn1_held = trade_pieces(dn1_parcel)
+    grad_in_held.append(send(after(in_pieces[3][half:], dn1_held[2], dn1_held[3]), 3))
+    dn1_sum = sum(piece.astype(F32) for piece in dn1_held)
     dn1 = dn1_sum[:part]
-    extra_sum = dn1_sum[part : part + 4] + dn1_sum[part + 4 : part + 8]
-    inner_one = extra_sum[0]
-    proj_came = swap(proj_parcel, "col")
-    small = jnp.sum(col_gather(after(extra_sum[1:], proj_came)), axis=0)
-    gain_one_grad, gain_two_grad = small[0, :width], small[1, :width]
-    table_grad = jnp.transpose(
-        small[2].reshape(LOW_BINS, LANES)[:, : bias_table.size // LOW_BINS].reshape(
-            LOW_BINS, all_heads, buckets // LOW_BINS
-        ),
-        (2, 0, 1),
-    ).reshape(bias_table.shape)
+    inner_one = dn1_sum[part] + dn1_sum[part + 1]
     gain_own = own_rows(gain_one, me, part)
     grad_tokens = (
         da.astype(F32)
@@ -1103,15 +1182,19 @@
     ).astype(BF16)
 
     band = width // cols
-    proj_sum = jnp.sum(proj_came.astype(F32), axis=0)
+    proj_sum = jnp.sum(swap(proj_parcel, "col").astype(F32), axis=0)
+    half = PAIR_ROWS // 2
+    extra_sum = proj_sum[band : band + half] + proj_sum[band + half :]
     router_rows = experts // cols
-    grad_router = jnp.transpose(
-        proj_sum[band : band + router_rows, :part]
-        + proj_sum[band + router_rows : band + 2 * router_rows, :part]
-    )
-    proj_own = jnp.transpose(
-        proj_sum[:band].reshape(band, 4, share, out_cols), (2, 0, 1, 3)
-    ).reshape(share, band, 4 * out_cols)
+    grad_router = jnp.transpose(extra_sum[:router_rows, :part])
+    small = sum(trade_pieces([extra_sum[router_rows:]] * rows))
+    gain_one_grad, gain_two_grad = small[0], small[1]
+    table_grad = jnp.transpose(
+        small[2:, : LOW_BINS // 2 * LANES]
+        .reshape(LOW_BINS, LANES)[:, : bias_table.size // LOW_BINS]
+        .reshape(LOW_BINS, all_heads, buckets // LOW_BINS),
+        (2, 0, 1),
+    ).reshape(bias_table.shape)
     pieces = []
     for turn in range(share):
         moves = [
@@ -1119,7 +1202,8 @@
             for r in range(rows)
             for c in range(cols)
         ]
-        piece = lax.dynamic_index_in_dim(proj_own, (col + turn) % share, 0, keepdims=False)
+        first = (col + turn) % share * 4 * out_cols
+        piece = lax.dynamic_slice_in_dim(proj_sum[:band], first, 4 * out_cols, 1)
         pieces.append(lax.ppermute(piece, ("row", "col"), moves))
     pieces = jnp.stack(pieces)
     grad_four = jnp.concatenate(
@@ -1132,7 +1216,10 @@
     grad_query, grad_key, grad_value, grad_out = [
         grad_four[:, w * out_cols : (w + 1) * out_cols] for w in range(4)
     ]
-    grad_in, grad_eout = fill_columns(grad_in_held, 4), fill_columns(grad_eout_held, 4)
+    last = after(grad_in_held[3], proj_sum)
+    grad_in_held[3] = jnp.concatenate([grad_in_half, last], axis=0)
+    grad_eout_held[2] = jnp.concatenate([grad_eout_half, grad_eout_held[2]], axis=0)
+    grad_in, grad_eout = fill_columns(grad_in_held, 2), fill_columns(grad_eout_held, 2)
     return (
         layer_out[None],
         grad_tokens[None],

time: 459 us -> 412 us (0.90)
  waiting for transfers between devices: 194 us -> 149 us
    ppermute x31 -> x37, waiting for transfers between devices: 158 us -> 125 us  [send(): return lax.ppermute(piece, 'row', [(i, i ^ offset) for i in range(count)])]
    all_to_all x7 -> x6, waiting for transfers between devices: 29 us -> 16.9 us  [swap(): return lax.all_to_all(blocks, axis, 0, 0)]
    ppermute x31 -> x37, starting transfers between devices: 29.4 us -> 39.6 us  [send(): return lax.ppermute(piece, 'row', [(i, i ^ offset) for i in range(count)])]
    pallas_call x1 -> x2, Pallas kernels: 23.2 us -> 31 us  [the longest x1 16.4 us: expert_outer(): pl.pallas_call(functools.partial(outer_kernel, count, places), grid_spec=...]
    all_to_all x7 -> x6, starting transfers between devices: 41.5 us -> 34.9 us  [swap(): return lax.all_to_all(blocks, axis, 0, 0)]
    dynamic_slice x6 -> x9, local copies, waits for them, and re-layouts: 10.6 us -> 9.16 us  [the longest x4 7.41 us: expert_plan(): lax.dynamic_slice_in_dim(array, (me ^ k) * count, count, 1)]
  transfers between devices with their start and end apart: 40 -> 45, of which waited for: 18 -> 18; matrix products, arithmetic and copies ran while one was open for 16% -> 17% of each run, Pallas kernels for 15% -> 24%
where the time goes in v2:
time: 412 us; the launch traced here: 406 us
  waiting for transfers between devices  149 us (36%)
  Pallas kernels  96.5 us (23%)
  starting transfers between devices  80.7 us (20%)
  local copies, waits for them, and re-layouts  42.9 us (10%)
  other arithmetic  22.5 us (5%)
  matrix products  12.4 us (3%)
    ppermute x37, waiting for transfers between devices, send(): return lax.ppermute(piece, 'row', [(i, i ^ offset) for i in range(count)])  125 us
    ppermute x37, starting transfers between devices, send(): return lax.ppermute(piece, 'row', [(i, i ^ offset) for i in range(count)])  39.6 us
    all_to_all x6, starting transfers between devices, swap(): return lax.all_to_all(blocks, axis, 0, 0)  34.9 us
    pallas_call x1, Pallas kernels, attend_back(): pl.pallas_call(functools.partial(back_kernel, heads, count, experts, cols...  32.9 us
    all_to_all x6, waiting for transfers between devices, swap(): return lax.all_to_all(blocks, axis, 0, 0)  16.9 us
    pallas_call x1, Pallas kernels, expert_outer(): pl.pallas_call(functools.partial(outer_kernel, count, places), grid_spec=...  16.4 us
    pallas_call x1, Pallas kernels, attend(): pl.pallas_call(functools.partial(attend_kernel, heads, width // heads), g...  16 us
    pallas_call x1, Pallas kernels, expert_inner(): pl.pallas_call(functools.partial(inner_kernel, count, places), grid_spec=...  14.7 us
  transfers between devices with their start and end apart: 45, of which 18 were waited for; matrix products, arithmetic and copies ran while one was open for 17% of the time, Pallas kernels for 24%

profile of v2, /device:TPU:25, one launch (start us, length us, event | category | flops | bytes accessed | tf_op | source)
XLA Modules:
  0.0 406.1 jit_solution(3243635895944117896)
XLA Ops:
  4.4 5.6 %all-to-all-start = ((bf16[8,192,288]{1,2,0:T(8,128)(2,1)}), bf16[8,192,288]{1,2,0:T(8,128)(2,1)S(1)}, u32[]{:S(2)}, u32[]{:S(2)}) async-start(bf16[8,192,288]{1,2,0:T(8,128)(2,1)} %broadcast_in_dim.29), calls=%async_computation | async-start | bytes 2359296 | tf_op jit(solution)/shard_map/all_to_all | solution.py:933
  24.8 5.8 %collective-permute-done.1 = bf16[256,1024]{1,0:T(8,128)(2,1)S(1)} collective-permute-done((bf16[256,1024]{1,0:T(8,128)(2,1)S(1)}, bf16[256,1024]{1,0:T(8,128)(2,1)S(1)}, u32[]{:S(2)}, u32[]{:S(2)}) %collective-permute-start.1) | collective-permute-done | bytes 524320 | tf_op jit(solution)/shard_map/ppermute | solution.py:915
  50.4 5.7 %all-to-all-start.1 = ((bf16[8,192,100]{2,1,0:T(8,128)(2,1)}), bf16[8,192,100]{2,1,0:T(8,128)(2,1)}, u32[]{:S(2)}, u32[]{:S(2)}) async-start(bf16[8,192,100]{2,1,0:T(8,128)(2,1)} %broadcast_in_dim.36), calls=%async_computation.1 | async-start | bytes 786432 | tf_op jit(solution)/shard_map/all_to_all | solution.py:933
  62.9 11.7 %collective-permute-done.7.refs_2_ = bf16[96,3072]{1,0:T(8,128)(2,1)S(1)} collective-permute-done((bf16[96,3072]{1,0:T(8,128)(2,1)}, bf16[96,3072]{1,0:T(8,128)(2,1)S(1)}, u32[]{:S(2)}, u32[]{:S(2)}) %collective-permute-start.7) | collective-permute-done | bytes 589856 | tf_op jit(solution)/shard_map/ppermute | solution.py:915
  85.6 16.0 %shard_map.238 = (f32[192,1024]{1,0:T(8,128)S(1)}, bf16[3,1024,1024]{2,1,0:T(8,128)(2,1)}) custom-call(bf16[192,1024]{1,0:T(8,128)(2,1)S(1)} %get-tuple-element.237.q_ref, bf16[192,1024]{1,0:T(8,128)(2,1)S(1)} %get-tuple-element.236.k_ref, bf16[192,1024]{1,0:T(8,128)(2,1)S(1)} %get-tuple-element.235.v_ref, bf16[1024,1024]{1,0:T(8,128)(2,1)S(1)} %bitcast.101, ...), custom_call_target="tpu_custom_call" | custom-call | tf_op jit(solution)/shard_map/pallas_call | solution.py:453
  106.7 5.9 %collective-permute-done.12.refs_3_ = bf16[192,3072]{1,0:T(8,128)(2,1)} collective-permute-done((bf16[192,3072]{1,0:T(8,128)(2,1)}, bf16[192,3072]{1,0:T(8,128)(2,1)}, u32[]{:S(2)}, u32[]{:S(2)}) %collective-permute-start.12) | collective-permute-done | bytes 1179680 | tf_op jit(solution)/shard_map/ppermute | solution.py:915
  113.6 6.2 %collective-permute-done.10 = bf16[192,800]{1,0:T(8,128)(2,1)S(1)} collective-permute-done((bf16[192,800]{1,0:T(8,128)(2,1)S(1)}, bf16[192,800]{1,0:T(8,128)(2,1)S(1)}, u32[]{:S(2)}, u32[]{:S(2)}) %collective-permute-start.10) | collective-permute-done | bytes 307232 | tf_op jit(solution)/shard_map/ppermute | solution.py:915
  120.7 7.5 %collective-permute-done.13 = bf16[192,1024]{1,0:T(8,128)(2,1)S(1)} collective-permute-done((bf16[192,1024]{1,0:T(8,128)(2,1)S(1)}, bf16[192,1024]{1,0:T(8,128)(2,1)S(1)}, u32[]{:S(2)}, u32[]{:S(2)}) %collective-permute-start.13) | collective-permute-done | bytes 393248 | tf_op jit(solution)/shard_map/ppermute | solution.py:915
  131.3 5.7 %all-to-all-start.3 = ((bf16[8,48,768]{2,1,0:T(8,128)(2,1)}), bf16[8,48,768]{2,1,0:T(8,128)(2,1)S(1)}, u32[]{:S(2)}, u32[]{:S(2)}) async-start(bf16[8,48,768]{2,1,0:T(8,128)(2,1)} %bitcast.41), calls=%async_computation.3 | async-start | bytes 1179648 | tf_op jit(solution)/shard_map/all_to_all | solution.py:933
  148.6 19.6 %collective-permute-done.15.refs_7_ = bf16[768,768]{1,0:T(8,128)(2,1)} collective-permute-done((bf16[768,768]{1,0:T(8,128)(2,1)S(1)}, bf16[768,768]{1,0:T(8,128)(2,1)}, u32[]{:S(2)}, u32[]{:S(2)}) %collective-permute-start.15) | collective-permute-done | bytes 1179680 | tf_op jit(solution)/shard_map/ppermute | solution.py:915
  168.2 5.4 %all-to-all-start.2 = ((bf16[8,48,768]{2,1,0:T(8,128)(2,1)}), bf16[8,48,768]{2,1,0:T(8,128)(2,1)S(1)}, u32[]{:S(2)}, u32[]{:S(2)}) async-start(bf16[8,48,768]{2,1,0:T(8,128)(2,1)} %bitcast.37), calls=%async_computation.2 | async-start | bytes 1179648 | tf_op jit(solution)/shard_map/all_to_all | solution.py:933
  177.3 9.3 %all-to-all-done.2 = bf16[8,48,768]{2,1,0:T(8,128)(2,1)S(1)} async-done(((bf16[8,48,768]{2,1,0:T(8,128)(2,1)}), bf16[8,48,768]{2,1,0:T(8,128)(2,1)S(1)}, u32[]{:S(2)}, u32[]{:S(2)}) %all-to-all-start.2) | async-done | bytes 589856 | tf_op jit(solution)/shard_map/all_to_all | solution.py:933
  187.5 14.7 %shard_map.239 = (bf16[384,768]{1,0:T(8,128)(2,1)}, bf16[384,3072]{1,0:T(8,128)(2,1)}, bf16[384,3072]{1,0:T(8,128)(2,1)}, bf16[768,768]{1,0:T(8,128)(2,1)}, bf16...) custom-call(s32[2]{0:T(128)} %pad_add_fusion.place_ref, bf16[384,768]{1,0:T(8,128)(2,1)} %bitcast.114, ...), custom_call_target="tpu_custom_call" | custom-call | tf_op jit(solution)/shard_map/pallas_call | solution.py:789
  205.4 16.4 %shard_map.240 = (bf16[384,1536]{1,0:T(8,128)(2,1)}, bf16[192,3072]{1,0:T(8,128)(2,1)}, bf16[192,3072]{1,0:T(8,128)(2,1)}, bf16[192,3072]{1,0:T(8,128)(2,1)}, bf16[192,3072]{1,0:T(8,128)(2,1)}) custom-call(s32[2]{0:T(128)} %pad_add_fusion.place_ref, bf16[384,768]{1,0:T(8,128)(2,1)} %bitcast.115, bf16[384,768]{1,0:T(8,128)(2,1)} %get-tuple-element.104.dys_ref, ...), custom_call_target="tpu_custom_call" | custom-call | tf_op jit(solution)/shard_map/pallas_call | solution.py:817
  221.8 6.8 %all-to-all-start.4 = ((bf16[8,48,1536]{2,1,0:T(8,128)(2,1)}), bf16[8,48,1536]{2,1,0:T(8,128)(2,1)S(1)}, u32[]{:S(2)}, u32[]{:S(2)}) async-start(bf16[8,48,1536]{2,1,0:T(8,128)(2,1)} %bitcast.133), calls=%async_computation.4 | async-start | bytes 2359296 | tf_op jit(solution)/shard_map/all_to_all | solution.py:933
  237.7 33.2 %collective-permute-done.21 = bf16[384,768]{1,0:T(8,128)(2,1)} collective-permute-done((bf16[384,768]{1,0:T(8,128)(2,1)}, bf16[384,768]{1,0:T(8,128)(2,1)}, u32[]{:S(2)}, u32[]{:S(2)}) %collective-permute-start.21) | collective-permute-done | bytes 589856 | tf_op jit(solution)/shard_map/ppermute | solution.py:915
  270.9 5.0 %shard_map.241 = (f32[1,768]{1,0:T(1,128)S(1)}, bf16[384,640]{1,0:T(8,128)(2,1)S(1)}, bf16[384,640]{1,0:T(8,128)(2,1)}, bf16[384,640]{1,0:T(8,128)(2,1)S(1)}, bf16[384,640]{1,0:T(8,128)(2,1)S(1)}) custom-call(s32[2]{0:T(128)S(1)} %copy-done.12, bf16[384,1536]{1,0:T(8,128)(2,1)S(1)} %bitcast.103, bf16[384,768]{1,0:T(8,128)(2,1)} %fusion.16.dy_ref, ...), custom_call_target="tpu_custom_call" | custom-call | tf_op jit(solution)/shard_map/pallas_call | solution.py:897
  278.5 11.1 %collective-permute-done.24.refs_2_ = bf16[384,640]{1,0:T(8,128)(2,1)S(1)} collective-permute-done((bf16[384,640]{1,0:T(8,128)(2,1)S(1)}, bf16[384,640]{1,0:T(8,128)(2,1)S(1)}, u32[]{:S(2)}, u32[]{:S(2)}) %collective-permute-start.24) | collective-permute-done | bytes 491552 | tf_op jit(solution)/shard_map/ppermute | solution.py:915
  289.6 10.7 %collective-permute-done.25.refs_3_ = bf16[384,640]{1,0:T(8,128)(2,1)S(1)} collective-permute-done((bf16[384,640]{1,0:T(8,128)(2,1)S(1)}, bf16[384,640]{1,0:T(8,128)(2,1)S(1)}, u32[]{:S(2)}, u32[]{:S(2)}) %collective-permute-start.25) | collective-permute-done | bytes 491552 | tf_op jit(solution)/shard_map/ppermute | solution.py:915
  306.8 32.9 %shard_map.242 = (bf16[192,1024]{1,0:T(8,128)(2,1)}, bf16[192,1024]{1,0:T(8,128)(2,1)}, bf16[8,112,768]{2,1,0:T(8,128)(2,1)}, bf16[208,1024]{1,0:T(8,128)(2,1)},...) custom-call(s32[2]{0:T(128)} %pad_add_fusion.place_ref, ...), custom_call_target="tpu_custom_call" | custom-call | tf_op jit(solution)/shard_map/pallas_call | solution.py:676
  340.9 5.7 %all-to-all-start.5 = ((bf16[8,112,768]{2,1,0:T(8,128)(2,1)}), bf16[8,112,768]{2,1,0:T(8,128)(2,1)}, u32[]{:S(2)}, u32[]{:S(2)}) async-start(bf16[8,112,768]{2,1,0:T(8,128)(2,1)} %get-tuple-element.143), calls=%async_computation.5 | async-start | bytes 2752512 | tf_op jit(solution)/shard_map/all_to_all | solution.py:933
  352.7 6.8 %shard_map.244 = f32[768,3072]{1,0:T(8,128)} custom-call(s32[1]{0:T(128)} %bitcast.me_ref, bf16[768,768]{1,0:T(8,128)(2,1)S(1)} %copy-done.10, bf16[768,768]{1,0:T(8,128)(2,1)} %collective-permute-done.38.refs_1_, bf16[768,768]{1,0:T(8,128)(2,1)S(1)} %pad_maximum_fusion.11.refs_2_, bf16[768,768]{1,0:T(8,128)(2,1)S(1)} %collective-permute-done.22.refs_3_), custom_call_target="tpu_custom_call" | custom-call | tf_op jit(solution)/shard_map/pallas_call | solution.py:978
  359.8 8.5 %collective-permute-done.30 = bf16[208,1024]{1,0:T(8,128)(2,1)S(1)} collective-permute-done((bf16[208,1024]{1,0:T(8,128)(2,1)}, bf16[208,1024]{1,0:T(8,128)(2,1)S(1)}, u32[]{:S(2)}, u32[]{:S(2)}) %collective-permute-start.30) | collective-permute-done | bytes 426016 | tf_op jit(solution)/shard_map/ppermute | solution.py:915
  371.0 7.6 %all-to-all-done.5 = bf16[8,112,768]{2,1,0:T(8,128)(2,1)} async-done(((bf16[8,112,768]{2,1,0:T(8,128)(2,1)}), bf16[8,112,768]{2,1,0:T(8,128)(2,1)}, u32[]{:S(2)}, u32[]{:S(2)}) %all-to-all-start.5) | async-done | bytes 1376288 | tf_op jit(solution)/shard_map/all_to_all | solution.py:933
  (286 shorter events, 140.5 us)
Async XLA Ops:
  4.4 39.7 %all-to-all-start = ((bf16[8,192,288]{1,2,0:T(8,128)(2,1)}), bf16[8,192,288]{1,2,0:T(8,128)(2,1)S(1)}, u32[]{:S(2)}, u32[]{:S(2)}) async-start(bf16[8,192,288]{1,2,0:T(8,128)(2,1)} %broadcast_in_dim.29), calls=%async_computation | async-start | bytes 2359296 | tf_op jit(solution)/shard_map/all_to_all | solution.py:933
  11.9 18.7 %collective-permute-start.1 = (bf16[256,1024]{1,0:T(8,128)(2,1)S(1)}, bf16[256,1024]{1,0:T(8,128)(2,1)S(1)}, u32[]{:S(2)}, u32[]{:S(2)}) collective-permute-start(bf16[256,1024]{1,0:T(8,128)(2,1)S(1)} %fusion.27), channel_id=1, source_target_pairs={{0,16},{8,24},{16,0},{24,8},{1,17},{9,25},{17,1},{25,9},{2,18},{10... | collective-permute-start | bytes 1572872 | tf_op jit(solution)/shard_map/ppermute | solution.py:915
  14.2 21.1 %collective-permute-start.8 = (bf16[2,192,1024]{2,1,0:T(8,128)(2,1)S(1)}, bf16[2,192,1024]{2,1,0:T(8,128)(2,1)S(1)}, u32[]{:S(2)}, u32[]{:S(2)}) collective-permute-start(bf16[2,192,1024]{2,1,0:T(8,128)(2,1)S(1)} %pad_maximum_fusion.13), channel_id=1, source_target_pairs={{0,8},{8,0},{16,24},{24,16},{1,9},{9,1},{17,25},{25,17},{2,10},{10... | collective-permute-start | bytes 2359304 | tf_op jit(solution)/shard_map/ppermute | solution.py:915
  23.3 20.7 %collective-permute-start.3 = (bf16[96,3072]{1,0:T(8,128)(2,1)S(1)}, bf16[96,3072]{1,0:T(8,128)(2,1)}, u32[]{:S(2)}, u32[]{:S(2)}) collective-permute-start(bf16[96,3072]{1,0:T(8,128)(2,1)S(1)} %constant_dynamic-slice_fusion.32), channel_id=1, source_target_pairs={{0,16},{8,24},{16,0},{24,8},{1,17},{9,25},{17,1},{25,9},{2,18},{10... | collective-permute-start | bytes 1769480 | tf_op jit(solution)/shard_map/ppermute | solution.py:915
  31.7 29.1 %collective-permute-start.9 = (bf16[2,256,1024]{2,1,0:T(8,128)(2,1)}, bf16[2,256,1024]{2,1,0:T(8,128)(2,1)}, u32[]{:S(2)}, u32[]{:S(2)}) collective-permute-start(bf16[2,256,1024]{2,1,0:T(8,128)(2,1)} %pad_maximum_fusion.12), channel_id=1, source_target_pairs={{0,8},{8,0},{16,24},{24,16},{1,9},{9,1},{17,25},{25,17},{2,10},{10... | collective-permute-start | bytes 3145736 | tf_op jit(solution)/shard_map/ppermute | solution.py:915
  48.4 26.2 %collective-permute-start.7 = (bf16[96,3072]{1,0:T(8,128)(2,1)}, bf16[96,3072]{1,0:T(8,128)(2,1)S(1)}, u32[]{:S(2)}, u32[]{:S(2)}) collective-permute-start(bf16[96,3072]{1,0:T(8,128)(2,1)} %constant_dynamic-slice_fusion.31), channel_id=1, source_target_pairs={{0,16},{8,24},{16,0},{24,8},{1,17},{9,25},{17,1},{25,9},{2,18},{10... | collective-permute-start | bytes 1769480 | tf_op jit(solution)/shard_map/ppermute | solution.py:915
  50.4 52.1 %all-to-all-start.1 = ((bf16[8,192,100]{2,1,0:T(8,128)(2,1)}), bf16[8,192,100]{2,1,0:T(8,128)(2,1)}, u32[]{:S(2)}, u32[]{:S(2)}) async-start(bf16[8,192,100]{2,1,0:T(8,128)(2,1)} %broadcast_in_dim.36), calls=%async_computation.1 | async-start | bytes 786432 | tf_op jit(solution)/shard_map/all_to_all | solution.py:933
  83.5 29.0 %collective-permute-start.12 = (bf16[192,3072]{1,0:T(8,128)(2,1)}, bf16[192,3072]{1,0:T(8,128)(2,1)}, u32[]{:S(2)}, u32[]{:S(2)}) collective-permute-start(bf16[192,3072]{1,0:T(8,128)(2,1)} %get-tuple-element.97), channel_id=1, source_target_pairs={{0,24},{8,16},{16,8},{24,0},{1,25},{9,17},{17,9},{25,1},{2,26},{10... | collective-permute-start | bytes 3538952 | tf_op jit(solution)/shard_map/ppermute | solution.py:915
  131.3 36.9 %all-to-all-start.3 = ((bf16[8,48,768]{2,1,0:T(8,128)(2,1)}), bf16[8,48,768]{2,1,0:T(8,128)(2,1)S(1)}, u32[]{:S(2)}, u32[]{:S(2)}) async-start(bf16[8,48,768]{2,1,0:T(8,128)(2,1)} %bitcast.41), calls=%async_computation.3 | async-start | bytes 1179648 | tf_op jit(solution)/shard_map/all_to_all | solution.py:933
  137.0 40.3 %collective-permute-start.17 = (bf16[192,3072]{1,0:T(8,128)(2,1)}, bf16[192,3072]{1,0:T(8,128)(2,1)}, u32[]{:S(2)}, u32[]{:S(2)}) collective-permute-start(bf16[192,3072]{1,0:T(8,128)(2,1)} %get-tuple-element.103), channel_id=1, source_target_pairs={{0,8},{8,0},{16,24},{24,16},{1,9},{9,1},{17,25},{25,17},{2,10},{10... | collective-permute-start | bytes 3538952 | tf_op jit(solution)/shard_map/ppermute | solution.py:915
  140.5 27.7 %collective-permute-start.15 = (bf16[768,768]{1,0:T(8,128)(2,1)S(1)}, bf16[768,768]{1,0:T(8,128)(2,1)}, u32[]{:S(2)}, u32[]{:S(2)}) collective-permute-start(bf16[768,768]{1,0:T(8,128)(2,1)S(1)} %copy-done.34), channel_id=1, source_target_pairs={{0,16},{8,24},{16,0},{24,8},{1,17},{9,25},{17,1},{25,9},{2,18},{10... | collective-permute-start | bytes 3538952 | tf_op jit(solution)/shard_map/ppermute | solution.py:915
  168.2 18.4 %all-to-all-start.2 = ((bf16[8,48,768]{2,1,0:T(8,128)(2,1)}), bf16[8,48,768]{2,1,0:T(8,128)(2,1)S(1)}, u32[]{:S(2)}, u32[]{:S(2)}) async-start(bf16[8,48,768]{2,1,0:T(8,128)(2,1)} %bitcast.37), calls=%async_computation.2 | async-start | bytes 1179648 | tf_op jit(solution)/shard_map/all_to_all | solution.py:933
  173.7 31.7 %collective-permute-start.18 = (bf16[768,768]{1,0:T(8,128)(2,1)}, bf16[768,768]{1,0:T(8,128)(2,1)}, u32[]{:S(2)}, u32[]{:S(2)}) collective-permute-start(bf16[768,768]{1,0:T(8,128)(2,1)} %get-tuple-element.112), channel_id=1, source_target_pairs={{0,8},{8,0},{16,24},{24,16},{1,9},{9,1},{17,25},{25,17},{2,10},{10... | collective-permute-start | bytes 3538952 | tf_op jit(solution)/shard_map/ppermute | solution.py:915
  175.0 30.4 %collective-permute-start.19 = (bf16[768,768]{1,0:T(8,128)(2,1)}, bf16[768,768]{1,0:T(8,128)(2,1)}, u32[]{:S(2)}, u32[]{:S(2)}) collective-permute-start(bf16[768,768]{1,0:T(8,128)(2,1)} %get-tuple-element.113), channel_id=1, source_target_pairs={{0,24},{8,16},{16,8},{24,0},{1,25},{9,17},{17,9},{25,1},{2,26},{10... | collective-permute-start | bytes 3538952 | tf_op jit(solution)/shard_map/ppermute | solution.py:915
  221.8 49.1 %all-to-all-start.4 = ((bf16[8,48,1536]{2,1,0:T(8,128)(2,1)}), bf16[8,48,1536]{2,1,0:T(8,128)(2,1)S(1)}, u32[]{:S(2)}, u32[]{:S(2)}) async-start(bf16[8,48,1536]{2,1,0:T(8,128)(2,1)} %bitcast.133), calls=%async_computation.4 | async-start | bytes 2359296 | tf_op jit(solution)/shard_map/all_to_all | solution.py:933
  229.7 47.1 %collective-permute-start.22 = (bf16[768,768]{1,0:T(8,128)(2,1)}, bf16[768,768]{1,0:T(8,128)(2,1)S(1)}, u32[]{:S(2)}, u32[]{:S(2)}) collective-permute-start(bf16[768,768]{1,0:T(8,128)(2,1)} %get-tuple-element.123), channel_id=1, source_target_pairs={{0,24},{8,16},{16,8},{24,0},{1,25},{9,17},{17,9},{25,1},{2,26},{10... | collective-permute-start | bytes 3538952 | tf_op jit(solution)/shard_map/ppermute | solution.py:915
  233.9 37.0 %collective-permute-start.21 = (bf16[384,768]{1,0:T(8,128)(2,1)}, bf16[384,768]{1,0:T(8,128)(2,1)}, u32[]{:S(2)}, u32[]{:S(2)}) collective-permute-start(bf16[384,768]{1,0:T(8,128)(2,1)} %get-tuple-element.116), channel_id=1, source_target_pairs={{0,16},{8,24},{16,0},{24,8},{1,17},{9,25},{17,1},{25,9},{2,18},{10... | collective-permute-start | bytes 1769480 | tf_op jit(solution)/shard_map/ppermute | solution.py:915
  277.9 22.4 %collective-permute-start.25 = (bf16[384,640]{1,0:T(8,128)(2,1)S(1)}, bf16[384,640]{1,0:T(8,128)(2,1)S(1)}, u32[]{:S(2)}, u32[]{:S(2)}) collective-permute-start(bf16[384,640]{1,0:T(8,128)(2,1)S(1)} %get-tuple-element.127), channel_id=1, source_target_pairs={{0,24},{8,16},{16,8},{24,0},{1,25},{9,17},{17,9},{25,1},{2,26},{10... | collective-permute-start | bytes 1474568 | tf_op jit(solution)/shard_map/ppermute | solution.py:915
  300.3 40.7 %collective-permute-start.27 = (bf16[192,3072]{1,0:T(8,128)(2,1)}, bf16[192,3072]{1,0:T(8,128)(2,1)S(1)}, u32[]{:S(2)}, u32[]{:S(2)}) collective-permute-start(bf16[192,3072]{1,0:T(8,128)(2,1)} %get-tuple-element.138), channel_id=1, source_target_pairs={{0,16},{8,24},{16,0},{24,8},{1,17},{9,25},{17,1},{25,9},{2,18},{10... | collective-permute-start | bytes 3538952 | tf_op jit(solution)/shard_map/ppermute | solution.py:915
  302.5 38.4 %collective-permute-start.26 = (bf16[96,3072]{1,0:T(8,128)(2,1)}, bf16[96,3072]{1,0:T(8,128)(2,1)}, u32[]{:S(2)}, u32[]{:S(2)}) collective-permute-start(bf16[96,3072]{1,0:T(8,128)(2,1)} %get-tuple-element.136), channel_id=1, source_target_pairs={{0,24},{8,16},{16,8},{24,0},{1,25},{9,17},{17,9},{25,1},{2,26},{10... | collective-permute-start | bytes 1769480 | tf_op jit(solution)/shard_map/ppermute | solution.py:915
  340.9 37.7 %all-to-all-start.5 = ((bf16[8,112,768]{2,1,0:T(8,128)(2,1)}), bf16[8,112,768]{2,1,0:T(8,128)(2,1)}, u32[]{:S(2)}, u32[]{:S(2)}) async-start(bf16[8,112,768]{2,1,0:T(8,128)(2,1)} %get-tuple-element.143), calls=%async_computation.5 | async-start | bytes 2752512 | tf_op jit(solution)/shard_map/all_to_all | solution.py:933
  348.8 19.5 %collective-permute-start.30 = (bf16[208,1024]{1,0:T(8,128)(2,1)}, bf16[208,1024]{1,0:T(8,128)(2,1)S(1)}, u32[]{:S(2)}, u32[]{:S(2)}) collective-permute-start(bf16[208,1024]{1,0:T(8,128)(2,1)} %get-tuple-element.142), channel_id=1, source_target_pairs={{0,24},{8,16},{16,8},{24,0},{1,25},{9,17},{17,9},{25,1},{2,26},{10... | collective-permute-start | bytes 1277960 | tf_op jit(solution)/shard_map/ppermute | solution.py:915
  349.1 20.7 %collective-permute-start.28 = (bf16[208,1024]{1,0:T(8,128)(2,1)}, bf16[208,1024]{1,0:T(8,128)(2,1)S(1)}, u32[]{:S(2)}, u32[]{:S(2)}) collective-permute-start(bf16[208,1024]{1,0:T(8,128)(2,1)} %get-tuple-element.140), channel_id=1, source_target_pairs={{0,8},{8,0},{16,24},{24,16},{1,9},{9,1},{17,25},{25,17},{2,10},{10... | collective-permute-start | bytes 1277960 | tf_op jit(solution)/shard_map/ppermute | solution.py:915
  359.4 29.4 %collective-permute-start.36 = (bf16[192,3072]{1,0:T(8,128)(2,1)}, bf16[192,3072]{1,0:T(8,128)(2,1)S(1)}, u32[]{:S(2)}, u32[]{:S(2)}) collective-permute-start(bf16[192,3072]{1,0:T(8,128)(2,1)} %get-tuple-element.146), channel_id=1, source_target_pairs={{0,8},{8,0},{16,24},{24,16},{1,9},{9,1},{17,25},{25,17},{2,10},{10... | collective-permute-start | bytes 3538952 | tf_op jit(solution)/shard_map/ppermute | solution.py:915
  (73 other events, 881.4 us)

commit v3 on v2

--- a/solution.py
+++ b/solution.py
@@ -711,10 +711,10 @@
         win[pl.ds(first, in_ref.shape[0]), :] = in_ref[...]
 
 
-def inner_kernel(count, places, place_ref, x_ref, dy_ref, router_ref, *refs):
+def inner_kernel(count, places, ge_places, place_ref, x_ref, dy_ref, router_ref, *refs):
     in_refs, refs = refs[: len(places)], refs[len(places) :]
     dys_ref, hidden_ref, slope_ref = refs[:3]
-    ge_refs, win = refs[3 : 3 + count], refs[3 + count]
+    ge_refs, win = refs[3:-1], refs[-1]
     step = pl.program_id(0)
 
     @pl.when(step == 0)
@@ -738,18 +738,20 @@
     )
     slope_ref[...] = slope.astype(BF16)
     ge = mm(hidden, dys_ref[...], TN).astype(BF16)
-    for k in range(count):
+    for ge_ref, (k, first, size) in zip(ge_refs, ge_places):
 
         @pl.when(step == k)
-        def _(k=k):
-            ge_refs[k][...] = ge
-
-
-def outer_kernel(count, places, place_ref, x_ref, dys_ref, hidden_ref, slope_ref, *refs):
+        def _(ge_ref=ge_ref, first=first, size=size):
+            ge_ref[...] = ge[first : first + size]
+
+
+def outer_kernel(
+    count, places, eout_places, place_ref, x_ref, dys_ref, hidden_ref, slope_ref, *refs
+):
     in_refs, refs = refs[: len(places)], refs[len(places) :]
-    eout_refs, back_ref = refs[:count], refs[count]
-    gi_refs = refs[count + 1 : 2 * count + 1]
-    win, eout, y_acc, dx_acc, gi = refs[2 * count + 1 :]
+    eout_refs, refs = refs[: len(eout_places)], refs[len(eout_places) :]
+    back_ref, gi_refs = refs[0], refs[1 : count + 1]
+    win, eout, y_acc, dx_acc, gi = refs[count + 1 :]
     step = pl.program_id(0)
     part = gi_refs[0].shape[0]
 
@@ -759,11 +761,11 @@
         dx_acc[...] = jnp.zeros_like(dx_acc)
 
     fill_rows(place_ref, places, in_refs, win, part)
-    for k in range(count):
+    for eout_ref, (k, first) in zip(eout_refs, eout_places):
 
         @pl.when(step == k)
-        def _(k=k):
-            eout[...] = eout_refs[k][...]
+        def _(eout_ref=eout_ref, first=first):
+            eout[first : first + eout_ref.shape[0], :] = eout_ref[...]
 
     y_acc[...] += mm(hidden_ref[...], eout[...], NN)
     dpre = (mm(dys_ref[...], eout[...], NT) * slope_ref[...].astype(F32)).astype(BF16)
@@ -779,7 +781,7 @@
         back_ref[:, width:] = dx_acc[...].astype(BF16)
 
 
-def expert_inner(place, x, dy, router, in_held, places, count):
+def expert_inner(place, x, dy, router, in_held, places, ge_places, count):
     slots, width = x.shape
     hidden_width = in_held[0].shape[1]
     chunk = hidden_width // count
@@ -787,26 +789,26 @@
     wide = pl.BlockSpec((slots, chunk), lambda i, m: (0, i))
     shape = lambda s: jax.ShapeDtypeStruct(s, BF16)
     out = pl.pallas_call(
-        functools.partial(inner_kernel, count, places),
+        functools.partial(inner_kernel, count, places, ge_places),
         grid_spec=pltpu.PrefetchScalarGridSpec(
             num_scalar_prefetch=1,
             grid=(count,),
             in_specs=[fixed(x.shape), fixed(dy.shape), fixed(router.shape)]
             + [pl.BlockSpec((a.shape[0], chunk), lambda i, m: (0, m[0] ^ i)) for a in in_held],
-            out_specs=[fixed(x.shape), wide, wide] + [fixed((chunk, width))] * count,
+            out_specs=[fixed(x.shape), wide, wide]
+            + [fixed((size, width)) for _, _, size in ge_places],
             scratch_shapes=[pltpu.VMEM((width, chunk), BF16)],
         ),
         out_shape=[shape(x.shape)]
         + [shape((slots, hidden_width))] * 2
-        + [shape((chunk, width))] * count,
+        + [shape((size, width)) for _, _, size in ge_places],
         compiler_params=pltpu.CompilerParams(vmem_limit_bytes=56 * 2**20),
         cost_estimate=QUICK,
     )(place, x, dy, router, *in_held)
     return out[0], out[1], out[2], out[3:]
 
 
-def expert_outer(place, x, dys, hidden, slope, in_held, places, eout_held):
-    count = len(eout_held)
+def expert_outer(place, x, dys, hidden, slope, in_held, places, eout_held, eout_places, count):
     slots, width = x.shape
     hidden_width = in_held[0].shape[1]
     part = width // count
@@ -815,13 +817,13 @@
     wide = pl.BlockSpec((slots, chunk), lambda i, m: (0, i))
     lanes = lambda rows: pl.BlockSpec((rows, chunk), lambda i, m: (0, m[0] ^ i))
     out = pl.pallas_call(
-        functools.partial(outer_kernel, count, places),
+        functools.partial(outer_kernel, count, places, eout_places),
         grid_spec=pltpu.PrefetchScalarGridSpec(
             num_scalar_prefetch=1,
             grid=(count,),
             in_specs=[fixed(x.shape), fixed(x.shape), wide, wide]
             + [lanes(a.shape[0]) for a in in_held]
-            + [fixed((chunk, width))] * count,
+            + [fixed(a.shape) for a in eout_held],
             out_specs=[fixed((slots, 2 * width))] + [lanes(part)] * count,
             scratch_shapes=[
                 pltpu.VMEM((width, chunk), BF16),
@@ -1043,10 +1045,13 @@
     out_gathered = col_gather(out_part)
     qkv_cols = qkv_cols.reshape(rows, share, part, 3 * out_cols)
     qkv_held = trade(lambda d: lax.dynamic_index_in_dim(qkv_cols, d, 0, keepdims=False))
-    second_cut = lane_cut(after(w_in, idx_far)[half:], hidden_width, 2)
-    in_second = send(after(second_cut, qkv_cols), 2)
-    eout_cuts = [lane_cut(after(w_expert_out, qkv_cols), width, k) for k in range(rows)]
-    qkv_held = after(tuple(qkv_held), in_second, *eout_cuts)
+    second_cut = lane_cut(after(w_in, qkv_cols)[half:], hidden_width, 2)
+    eout_half = w_expert_out.shape[0] // 4
+    later_eout = after(w_expert_out, qkv_cols)
+    eout_cuts = [lane_cut(later_eout, width, k) for k in range(3)]
+    eout_cuts.append(lane_cut(later_eout[:eout_half], width, 3))
+    eout_cuts.append(lane_cut(later_eout[eout_half:], width, 3))
+    qkv_held = after(tuple(qkv_held), *eout_cuts)
     qkv_own = jnp.transpose(
         lay(qkv_held).reshape(rows, share, part, 3, out_cols), (0, 2, 3, 1, 4)
     ).reshape(width, 3 * part)
@@ -1068,6 +1073,7 @@
     qkv = mm(qkv_own, n1, TN).astype(BF16)
     later_in = after(w_in, tok_low)
     in_places = ((0, 0), (2, 0), (2, half), (3, 0), (1, 0))
+    in_second = send(after(second_cut, qkv), 2)
     in_held = [lane_cut(later_in, hidden_width, 0), in_first, in_second]
     for k in (3, 1):
         in_held.append(send(after(lane_cut(later_in, hidden_width, k), qkv), k))
@@ -1080,10 +1086,10 @@
     o32, p = attend(q, k, v, idx, table, heads, 256)
     expert_at = lambda a: swap(a.reshape(cols, CAPACITY, width), "col").reshape(slots, width)
     dy_low = mm(choose, cot_low, NT).astype(BF16)
-    o_low = after(o32.astype(BF16), in_held[3])
+    o_low = after(o32.astype(BF16), in_second, in_held[3])
     dy_slots = expert_at(dy_low)
     o_far = send(o_low, 2)
-    o_full = row_join(o_low, o_far).reshape(width, seq_len)
+    o_full = row_join(o_low, after(o_far, dy_slots)).reshape(width, seq_len)
     out_gathered = after(out_gathered, o32)
     out_rows = jnp.transpose(out_gathered[:, :, :out_cols], (1, 0, 2)).reshape(part, width)
     router_rows = jnp.transpose(out_gathered[:, :, out_cols:], (1, 0, 2)).reshape(part, experts)
@@ -1091,9 +1097,7 @@
     out_router = row_gather(out_router).reshape(width, width + experts)
     out_full, router_full = out_router[:, :width], out_router[:, width:]
     eout_two = send(after(eout_cuts[2], o_far), 2)
-    eout_one = send(after(eout_cuts[1], o_full), 1)
-    eout_three = send(after(eout_cuts[3], o_full), 3)
-    eout_held = [eout_cuts[0], eout_one, eout_two, eout_three]
+    eout_three = send(after(eout_cuts[3], o_far), 3)
     h1 = x + mm(out_full, o_full, TN)
     r2 = lax.rsqrt(jnp.mean(h1 * h1, axis=0) + NORM_EPS)
     n2 = (h1 * r2 * gain_two[:, None]).astype(BF16)
@@ -1102,29 +1106,35 @@
     gate = jnp.sum(g * picked_float, axis=0)
 
     n2_low = mm(choose, n2, NT).astype(BF16)
-    slots_in = expert_at(after(n2_low, eout_two))
+    slots_in = after(expert_at(n2_low), eout_two, eout_three)
+    eout_last = send(after(eout_cuts[4], slots_in), 3)
+    eout_one = send(after(eout_cuts[1], slots_in), 1)
+    eout_held = [eout_cuts[0], eout_one, eout_two, eout_three, eout_last]
+    eout_places = ((0, 0), (1, 0), (2, 0), (3, 0), (3, eout_half))
     place = jnp.stack([me, col * rows + me]).astype(I32)
-    dys, hidden, slope, eout_pieces = expert_inner(
-        place, slots_in, dy_slots, router_full, in_held, in_places, rows
-    )
-    hidden = after(hidden, *eout_pieces)
+    hid = w_expert_out.shape[0]
+    ge_cut = hid // 4 * 3
+    ge_places = ((0, 0, hid), (1, 0, hid), (2, 0, ge_cut), (2, ge_cut, hid - ge_cut), (3, 0, hid))
+    dys, hidden, slope, ge = expert_inner(
+        place, slots_in, dy_slots, router_full, in_held, in_places, ge_places, rows
+    )
+    hidden = after(hidden, *ge)
     back, in_pieces = expert_outer(
-        place, slots_in, dys, hidden, slope, in_held, in_places, eout_held
-    )
-    eout_half = w_expert_out.shape[0] // 2
-    grad_eout_half = send(eout_pieces[2][:eout_half], 2)
-    back = after(back, grad_eout_half)
+        place, slots_in, dys, hidden, slope, in_held, in_places, eout_held, eout_places, rows
+    )
+    grad_eout_first = send(ge[2], 2)
+    back = after(back, grad_eout_first)
     grad_eout_held = [
-        eout_pieces[0],
-        send(after(eout_pieces[1], back), 1),
-        send(after(eout_pieces[2][eout_half:], back), 2),
-        send(after(eout_pieces[3], back), 3),
+        ge[0],
+        send(after(ge[1], back), 1),
+        send(after(ge[3], back), 2),
+        send(after(ge[4], back), 3),
     ]
     home = swap(back.reshape(cols, CAPACITY, 2 * width), "col").reshape(slots, 2 * width)
 
     h1_s = mm(choose, h1.astype(BF16), NT).astype(BF16)
     h1_own = own_rows(h1, me, part)
-    home = after(home, grad_eout_held[2], h1_own)
+    home = after(home, h1_own)
     scalars = lax.dot_general(
         choose.astype(F32),
         jnp.concatenate([g, gate[None], r2[None]], axis=0),
@@ -1135,7 +1145,7 @@
     parcel, gain_two_part = slot_work(
         place, home, dy_low, n2_low, h1_s, scalars, router_full, out_full, gain_two[None], rows
     )
-    parcel = trade_pieces(after(tuple(parcel), grad_eout_held[3]))
+    parcel = trade_pieces(after(tuple(parcel), *grad_eout_held[2:]))
     in_turn = lambda piece: after(piece, parcel[2], parcel[3])
     grad_in_held = [
         in_pieces[0],
@@ -1218,7 +1228,7 @@
     ]
     last = after(grad_in_held[3], proj_sum)
     grad_in_held[3] = jnp.concatenate([grad_in_half, last], axis=0)
-    grad_eout_held[2] = jnp.concatenate([grad_eout_half, grad_eout_held[2]], axis=0)
+    grad_eout_held[2] = jnp.concatenate([grad_eout_first, grad_eout_held[2]], axis=0)
     grad_in, grad_eout = fill_columns(grad_in_held, 2), fill_columns(grad_eout_held, 2)
     return (
         layer_out[None],

time: 412 us -> 386 us (0.937); the launches traced: 406 us -> 385 us
  waiting for transfers between devices: 149 us -> 126 us
  starting transfers between devices: 80.7 us -> 87.7 us
    ppermute x37 -> x38, waiting for transfers between devices: 125 us -> 93.2 us  [send(): return lax.ppermute(piece, 'row', [(i, i ^ offset) for i in range(count)])]
    all_to_all x6, starting transfers between devices: 34.9 us -> 44.7 us  [swap(): return lax.all_to_all(blocks, axis, 0, 0)]
    all_to_all x6, waiting for transfers between devices: 16.9 us -> 26 us  [swap(): return lax.all_to_all(blocks, axis, 0, 0)]
    ppermute x37 -> x38, starting transfers between devices: 39.6 us -> 36.5 us  [send(): return lax.ppermute(piece, 'row', [(i, i ^ offset) for i in range(count)])]
    dynamic_slice x4 -> x6, local copies, waits for them, and re-layouts: 7.41 us -> 8.5 us  [expert_plan(): lax.dynamic_slice_in_dim(array, (me ^ k) * count, count, 1)]
  transfers between devices with their start and end apart: 45 -> 46, of which waited for: 18 -> 18; matrix products, arithmetic and copies ran while one was open for 17% -> 17% of each run, Pallas kernels for 24% -> 25%
where the time goes in v3:
time: 386 us; the launch traced here: 385 us
  waiting for transfers between devices  126 us (33%)
  Pallas kernels  96.2 us (25%)
  starting transfers between devices  87.7 us (23%)
  local copies, waits for them, and re-layouts  39.2 us (10%)
  other arithmetic  21.6 us (6%)
  matrix products  12.5 us (3%)
    ppermute x38, waiting for transfers between devices, send(): return lax.ppermute(piece, 'row', [(i, i ^ offset) for i in range(count)])  93.2 us
    all_to_all x6, starting transfers between devices, swap(): return lax.all_to_all(blocks, axis, 0, 0)  44.7 us
    ppermute x38, starting transfers between devices, send(): return lax.ppermute(piece, 'row', [(i, i ^ offset) for i in range(count)])  36.5 us
    pallas_call x1, Pallas kernels, attend_back(): pl.pallas_call(functools.partial(back_kernel, heads, count, experts, cols...  32.5 us
    all_to_all x6, waiting for transfers between devices, swap(): return lax.all_to_all(blocks, axis, 0, 0)  26 us
    pallas_call x1, Pallas kernels, expert_outer(): pl.pallas_call(functools.partial(outer_kernel, count, places, eout_places...  16.5 us
    pallas_call x1, Pallas kernels, attend(): pl.pallas_call(functools.partial(attend_kernel, heads, width // heads), g...  16 us
    pallas_call x1, Pallas kernels, expert_inner(): pl.pallas_call(functools.partial(inner_kernel, count, places, ge_places),...  14.7 us
  transfers between devices with their start and end apart: 46, of which 18 were waited for; matrix products, arithmetic and copies ran while one was open for 17% of the time, Pallas kernels for 25%

profile of v3, /device:TPU:25, one launch (start us, length us, event | category | flops | bytes accessed | tf_op | source)
XLA Modules:
  0.0 385.2 jit_solution(10046555827840391554)
XLA Ops:
  4.4 5.6 %all-to-all-start = ((bf16[8,192,288]{1,2,0:T(8,128)(2,1)}), bf16[8,192,288]{1,2,0:T(8,128)(2,1)S(1)}, u32[]{:S(2)}, u32[]{:S(2)}) async-start(bf16[8,192,288]{1,2,0:T(8,128)(2,1)} %broadcast_in_dim.29), calls=%async_computation | async-start | bytes 2359296 | tf_op jit(solution)/shard_map/all_to_all | solution.py:935
  24.5 6.1 %collective-permute-done.1 = bf16[256,1024]{1,0:T(8,128)(2,1)S(1)} collective-permute-done((bf16[256,1024]{1,0:T(8,128)(2,1)S(1)}, bf16[256,1024]{1,0:T(8,128)(2,1)S(1)}, u32[]{:S(2)}, u32[]{:S(2)}) %collective-permute-start.1) | collective-permute-done | bytes 524320 | tf_op jit(solution)/shard_map/ppermute | solution.py:917
  48.4 5.9 %all-to-all-start.1 = ((bf16[8,192,100]{2,1,0:T(8,128)(2,1)}), bf16[8,192,100]{2,1,0:T(8,128)(2,1)}, u32[]{:S(2)}, u32[]{:S(2)}) async-start(bf16[8,192,100]{2,1,0:T(8,128)(2,1)} %broadcast_in_dim.36), calls=%async_computation.1 | async-start | bytes 786432 | tf_op jit(solution)/shard_map/all_to_all | solution.py:935
  72.3 16.0 %shard_map.238 = (f32[192,1024]{1,0:T(8,128)S(1)}, bf16[3,1024,1024]{2,1,0:T(8,128)(2,1)}) custom-call(bf16[192,1024]{1,0:T(8,128)(2,1)S(1)} %get-tuple-element.240.q_ref, bf16[192,1024]{1,0:T(8,128)(2,1)S(1)} %get-tuple-element.239.k_ref, bf16[192,1024]{1,0:T(8,128)(2,1)S(1)} %get-tuple-element.238.v_ref, bf16[1024,1024]{1,0:T(8,128)(2,1)S(1)} %bitcast.101, ...), custom_call_target="tpu_custom_call" | custom-call | tf_op jit(solution)/shard_map/pallas_call | solution.py:453
  89.2 5.8 %all-to-all-start.2 = ((bf16[8,48,768]{2,1,0:T(8,128)(2,1)}), bf16[8,48,768]{2,1,0:T(8,128)(2,1)}, u32[]{:S(2)}, u32[]{:S(2)}) async-start(bf16[8,48,768]{2,1,0:T(8,128)(2,1)} %bitcast.35), calls=%async_computation.2 | async-start | bytes 1179648 | tf_op jit(solution)/shard_map/all_to_all | solution.py:935
  101.3 7.6 %collective-permute-done.11.refs_2_ = bf16[96,3072]{1,0:T(8,128)(2,1)} collective-permute-done((bf16[96,3072]{1,0:T(8,128)(2,1)}, bf16[96,3072]{1,0:T(8,128)(2,1)}, u32[]{:S(2)}, u32[]{:S(2)}) %collective-permute-start.11) | collective-permute-done | bytes 589856 | tf_op jit(solution)/shard_map/ppermute | solution.py:917
  110.2 6.0 %collective-permute-done.9 = bf16[192,800]{1,0:T(8,128)(2,1)S(1)} collective-permute-done((bf16[192,800]{1,0:T(8,128)(2,1)S(1)}, bf16[192,800]{1,0:T(8,128)(2,1)S(1)}, u32[]{:S(2)}, u32[]{:S(2)}) %collective-permute-start.9) | collective-permute-done | bytes 307232 | tf_op jit(solution)/shard_map/ppermute | solution.py:917
  117.6 7.0 %collective-permute-done.13 = bf16[192,1024]{1,0:T(8,128)(2,1)S(1)} collective-permute-done((bf16[192,1024]{1,0:T(8,128)(2,1)S(1)}, bf16[192,1024]{1,0:T(8,128)(2,1)S(1)}, u32[]{:S(2)}, u32[]{:S(2)}) %collective-permute-start.13) | collective-permute-done | bytes 393248 | tf_op jit(solution)/shard_map/ppermute | solution.py:917
  134.0 5.4 %all-to-all-start.3 = ((bf16[8,48,768]{2,1,0:T(8,128)(2,1)}), bf16[8,48,768]{2,1,0:T(8,128)(2,1)S(1)}, u32[]{:S(2)}, u32[]{:S(2)}) async-start(bf16[8,48,768]{2,1,0:T(8,128)(2,1)} %bitcast.41), calls=%async_computation.3 | async-start | bytes 1179648 | tf_op jit(solution)/shard_map/all_to_all | solution.py:935
  140.8 20.5 %collective-permute-done.17.refs_8_ = bf16[192,768]{1,0:T(8,128)(2,1)S(1)} collective-permute-done((bf16[192,768]{1,0:T(8,128)(2,1)S(1)}, bf16[192,768]{1,0:T(8,128)(2,1)S(1)}, u32[]{:S(2)}, u32[]{:S(2)}) %collective-permute-start.17) | collective-permute-done | bytes 294944 | tf_op jit(solution)/shard_map/ppermute | solution.py:917
  164.1 14.7 %shard_map.239 = (bf16[384,768]{1,0:T(8,128)(2,1)}, bf16[384,3072]{1,0:T(8,128)(2,1)}, bf16[384,3072]{1,0:T(8,128)(2,1)}, bf16[768,768]{1,0:T(8,128)(2,1)}, bf16...) custom-call(s32[2]{0:T(128)} %pad_add_fusion.place_ref, ...), custom_call_target="tpu_custom_call" | custom-call | tf_op jit(solution)/shard_map/pallas_call | solution.py:791
  179.3 4.8 %collective-permute-done.20.refs_9_ = bf16[576,768]{1,0:T(8,128)(2,1)S(1)} collective-permute-done((bf16[576,768]{1,0:T(8,128)(2,1)S(1)}, bf16[576,768]{1,0:T(8,128)(2,1)S(1)}, u32[]{:S(2)}, u32[]{:S(2)}) %collective-permute-start.20) | collective-permute-done | bytes 884768 | tf_op jit(solution)/shard_map/ppermute | solution.py:917
  185.0 16.5 %shard_map.240 = (bf16[384,1536]{1,0:T(8,128)(2,1)}, bf16[192,3072]{1,0:T(8,128)(2,1)}, bf16[192,3072]{1,0:T(8,128)(2,1)}, bf16[192,3072]{1,0:T(8,128)(2,1)}, bf16[192,3072]{1,0:T(8,128)(2,1)}) custom-call(s32[2]{0:T(128)} %pad_add_fusion.place_ref, bf16[384,768]{1,0:T(8,128)(2,1)} %bitcast.115, bf16[384,768]{1,0:T(8,128)(2,1)} %get-tuple-element.109.dys_ref, ...), custom_call_target="tpu_custom_call" | custom-call | tf_op jit(solution)/shard_map/pallas_call | solution.py:819
  202.8 16.3 %all-to-all-start.4 = ((bf16[8,48,1536]{2,1,0:T(8,128)(2,1)}), bf16[8,48,1536]{2,1,0:T(8,128)(2,1)S(1)}, u32[]{:S(2)}, u32[]{:S(2)}) async-start(bf16[8,48,1536]{2,1,0:T(8,128)(2,1)} %bitcast.134), calls=%async_computation.4 | async-start | bytes 2359296 | tf_op jit(solution)/shard_map/all_to_all | solution.py:935
  228.2 17.6 %all-to-all-done.4 = bf16[8,48,1536]{2,1,0:T(8,128)(2,1)S(1)} async-done(((bf16[8,48,1536]{2,1,0:T(8,128)(2,1)}), bf16[8,48,1536]{2,1,0:T(8,128)(2,1)S(1)}, u32[]{:S(2)}, u32[]{:S(2)}) %all-to-all-start.4) | async-done | bytes 1179680 | tf_op jit(solution)/shard_map/all_to_all | solution.py:935
  245.9 5.0 %shard_map.241 = (f32[1,768]{1,0:T(1,128)S(1)}, bf16[384,640]{1,0:T(8,128)(2,1)S(1)}, bf16[384,640]{1,0:T(8,128)(2,1)}, bf16[384,640]{1,0:T(8,128)(2,1)S(1)}, bf16[384,640]{1,0:T(8,128)(2,1)S(1)}) custom-call(s32[2]{0:T(128)S(1)} %copy-done.12, bf16[384,1536]{1,0:T(8,128)(2,1)S(1)} %bitcast.103, bf16[384,768]{1,0:T(8,128)(2,1)} %fusion.13.dy_ref, ...), custom_call_target="tpu_custom_call" | custom-call | tf_op jit(solution)/shard_map/pallas_call | solution.py:899
  257.7 10.4 %collective-permute-done.25.refs_2_ = bf16[384,640]{1,0:T(8,128)(2,1)S(1)} collective-permute-done((bf16[384,640]{1,0:T(8,128)(2,1)S(1)}, bf16[384,640]{1,0:T(8,128)(2,1)S(1)}, u32[]{:S(2)}, u32[]{:S(2)}) %collective-permute-start.25) | collective-permute-done | bytes 491552 | tf_op jit(solution)/shard_map/ppermute | solution.py:917
  268.1 11.1 %collective-permute-done.26.refs_3_ = bf16[384,640]{1,0:T(8,128)(2,1)S(1)} collective-permute-done((bf16[384,640]{1,0:T(8,128)(2,1)S(1)}, bf16[384,640]{1,0:T(8,128)(2,1)S(1)}, u32[]{:S(2)}, u32[]{:S(2)}) %collective-permute-start.26) | collective-permute-done | bytes 491552 | tf_op jit(solution)/shard_map/ppermute | solution.py:917
  285.7 32.5 %shard_map.242 = (bf16[192,1024]{1,0:T(8,128)(2,1)}, bf16[192,1024]{1,0:T(8,128)(2,1)}, bf16[8,112,768]{2,1,0:T(8,128)(2,1)}, bf16[208,1024]{1,0:T(8,128)(2,1)},...) custom-call(s32[2]{0:T(128)} %pad_add_fusion.place_ref, ...), custom_call_target="tpu_custom_call" | custom-call | tf_op jit(solution)/shard_map/pallas_call | solution.py:676
  319.8 5.7 %all-to-all-start.5 = ((bf16[8,112,768]{2,1,0:T(8,128)(2,1)}), bf16[8,112,768]{2,1,0:T(8,128)(2,1)}, u32[]{:S(2)}, u32[]{:S(2)}) async-start(bf16[8,112,768]{2,1,0:T(8,128)(2,1)} %get-tuple-element.149), calls=%async_computation.5 | async-start | bytes 2752512 | tf_op jit(solution)/shard_map/all_to_all | solution.py:935
  331.9 6.8 %shard_map.244 = f32[768,3072]{1,0:T(8,128)} custom-call(s32[1]{0:T(128)} %bitcast.me_ref, bf16[768,768]{1,0:T(8,128)(2,1)S(1)} %copy-done.10, bf16[768,768]{1,0:T(8,128)(2,1)} %collective-permute-done.39.refs_1_, bf16[768,768]{1,0:T(8,128)(2,1)S(1)} %pad_maximum_fusion.11.refs_2_, bf16[768,768]{1,0:T(8,128)(2,1)S(1)} %collective-permute-done.23.refs_3_), custom_call_target="tpu_custom_call" | custom-call | tf_op jit(solution)/shard_map/pallas_call | solution.py:980
  339.0 8.5 %collective-permute-done.31 = bf16[208,1024]{1,0:T(8,128)(2,1)S(1)} collective-permute-done((bf16[208,1024]{1,0:T(8,128)(2,1)S(1)}, bf16[208,1024]{1,0:T(8,128)(2,1)S(1)}, u32[]{:S(2)}, u32[]{:S(2)}) %collective-permute-start.31) | collective-permute-done | bytes 426016 | tf_op jit(solution)/shard_map/ppermute | solution.py:917
  349.1 8.4 %all-to-all-done.5 = bf16[8,112,768]{2,1,0:T(8,128)(2,1)} async-done(((bf16[8,112,768]{2,1,0:T(8,128)(2,1)}), bf16[8,112,768]{2,1,0:T(8,128)(2,1)}, u32[]{:S(2)}, u32[]{:S(2)}) %all-to-all-start.5) | async-done | bytes 1376288 | tf_op jit(solution)/shard_map/all_to_all | solution.py:935
  371.1 4.8 %shard_map.243 = f32[192,12288]{1,0:T(8,128)} custom-call(s32[1]{0:T(128)} %bitcast.me_ref, bf16[192,3072]{1,0:T(8,128)(2,1)S(1)} %copy-done.9, bf16[192,3072]{1,0:T(8,128)(2,1)S(1)} %collective-permute-done.37.refs_1_, bf16[192,3072]{1,0:T(8,128)(2,1)S(1)} %collective-permute-done.28.refs_2_, bf16[192,3072]{1,0:T(8,128)(2,1)S(1)} %pad_maximum_fusion.10.refs_3_), custom_call_target="tpu_custom_call" | custom-call | tf_op jit(solution)/shard_map/pallas_call | solution.py:980
  (331 shorter events, 134.2 us)
Async XLA Ops:
  4.4 39.8 %all-to-all-start = ((bf16[8,192,288]{1,2,0:T(8,128)(2,1)}), bf16[8,192,288]{1,2,0:T(8,128)(2,1)S(1)}, u32[]{:S(2)}, u32[]{:S(2)}) async-start(bf16[8,192,288]{1,2,0:T(8,128)(2,1)} %broadcast_in_dim.29), calls=%async_computation | async-start | bytes 2359296 | tf_op jit(solution)/shard_map/all_to_all | solution.py:935
  14.3 20.0 %collective-permute-start.7 = (bf16[2,192,1024]{2,1,0:T(8,128)(2,1)S(1)}, bf16[2,192,1024]{2,1,0:T(8,128)(2,1)S(1)}, u32[]{:S(2)}, u32[]{:S(2)}) collective-permute-start(bf16[2,192,1024]{2,1,0:T(8,128)(2,1)S(1)} %pad_maximum_fusion.13), channel_id=1, source_target_pairs={{0,8},{8,0},{16,24},{24,16},{1,9},{9,1},{17,25},{25,17},{2,10},{10... | collective-permute-start | bytes 2359304 | tf_op jit(solution)/shard_map/ppermute | solution.py:917
  23.0 21.2 %collective-permute-start.3 = (bf16[96,3072]{1,0:T(8,128)(2,1)S(1)}, bf16[96,3072]{1,0:T(8,128)(2,1)}, u32[]{:S(2)}, u32[]{:S(2)}) collective-permute-start(bf16[96,3072]{1,0:T(8,128)(2,1)S(1)} %constant_dynamic-slice_fusion.33), channel_id=1, source_target_pairs={{0,16},{8,24},{16,0},{24,8},{1,17},{9,25},{17,1},{25,9},{2,18},{10... | collective-permute-start | bytes 1769480 | tf_op jit(solution)/shard_map/ppermute | solution.py:917
  31.7 38.0 %collective-permute-start.8 = (bf16[2,256,1024]{2,1,0:T(8,128)(2,1)}, bf16[2,256,1024]{2,1,0:T(8,128)(2,1)}, u32[]{:S(2)}, u32[]{:S(2)}) collective-permute-start(bf16[2,256,1024]{2,1,0:T(8,128)(2,1)} %pad_maximum_fusion.12), channel_id=1, source_target_pairs={{0,8},{8,0},{16,24},{24,16},{1,9},{9,1},{17,25},{25,17},{2,10},{10... | collective-permute-start | bytes 3145736 | tf_op jit(solution)/shard_map/ppermute | solution.py:917
  48.4 40.9 %all-to-all-start.1 = ((bf16[8,192,100]{2,1,0:T(8,128)(2,1)}), bf16[8,192,100]{2,1,0:T(8,128)(2,1)}, u32[]{:S(2)}, u32[]{:S(2)}) async-start(bf16[8,192,100]{2,1,0:T(8,128)(2,1)} %broadcast_in_dim.36), calls=%async_computation.1 | async-start | bytes 786432 | tf_op jit(solution)/shard_map/all_to_all | solution.py:935
  67.3 41.6 %collective-permute-start.12 = (bf16[192,3072]{1,0:T(8,128)(2,1)}, bf16[192,3072]{1,0:T(8,128)(2,1)S(1)}, u32[]{:S(2)}, u32[]{:S(2)}) collective-permute-start(bf16[192,3072]{1,0:T(8,128)(2,1)} %get-tuple-element.100), channel_id=1, source_target_pairs={{0,24},{8,16},{16,8},{24,0},{1,25},{9,17},{17,9},{25,1},{2,26},{10... | collective-permute-start | bytes 3538952 | tf_op jit(solution)/shard_map/ppermute | solution.py:917
  69.3 39.7 %collective-permute-start.11 = (bf16[96,3072]{1,0:T(8,128)(2,1)}, bf16[96,3072]{1,0:T(8,128)(2,1)}, u32[]{:S(2)}, u32[]{:S(2)}) collective-permute-start(bf16[96,3072]{1,0:T(8,128)(2,1)} %constant_dynamic-slice_fusion.14), channel_id=1, source_target_pairs={{0,16},{8,24},{16,0},{24,8},{1,17},{9,25},{17,1},{25,9},{2,18},{10... | collective-permute-start | bytes 1769480 | tf_op jit(solution)/shard_map/ppermute | solution.py:917
  89.2 28.4 %all-to-all-start.2 = ((bf16[8,48,768]{2,1,0:T(8,128)(2,1)}), bf16[8,48,768]{2,1,0:T(8,128)(2,1)}, u32[]{:S(2)}, u32[]{:S(2)}) async-start(bf16[8,48,768]{2,1,0:T(8,128)(2,1)} %bitcast.35), calls=%async_computation.2 | async-start | bytes 1179648 | tf_op jit(solution)/shard_map/all_to_all | solution.py:935
  127.0 34.3 %collective-permute-start.16 = (bf16[768,768]{1,0:T(8,128)(2,1)}, bf16[768,768]{1,0:T(8,128)(2,1)}, u32[]{:S(2)}, u32[]{:S(2)}) collective-permute-start(bf16[768,768]{1,0:T(8,128)(2,1)} %get-tuple-element.105), channel_id=1, source_target_pairs={{0,16},{8,24},{16,0},{24,8},{1,17},{9,25},{17,1},{25,9},{2,18},{10... | collective-permute-start | bytes 3538952 | tf_op jit(solution)/shard_map/ppermute | solution.py:917
  134.0 27.3 %all-to-all-start.3 = ((bf16[8,48,768]{2,1,0:T(8,128)(2,1)}), bf16[8,48,768]{2,1,0:T(8,128)(2,1)S(1)}, u32[]{:S(2)}, u32[]{:S(2)}) async-start(bf16[8,48,768]{2,1,0:T(8,128)(2,1)} %bitcast.41), calls=%async_computation.3 | async-start | bytes 1179648 | tf_op jit(solution)/shard_map/all_to_all | solution.py:935
  139.4 24.6 %collective-permute-start.18 = (bf16[192,3072]{1,0:T(8,128)(2,1)}, bf16[192,3072]{1,0:T(8,128)(2,1)}, u32[]{:S(2)}, u32[]{:S(2)}) collective-permute-start(bf16[192,3072]{1,0:T(8,128)(2,1)} %get-tuple-element.108), channel_id=1, source_target_pairs={{0,8},{8,0},{16,24},{24,16},{1,9},{9,1},{17,25},{25,17},{2,10},{10... | collective-permute-start | bytes 3538952 | tf_op jit(solution)/shard_map/ppermute | solution.py:917
  140.4 20.9 %collective-permute-start.17 = (bf16[192,768]{1,0:T(8,128)(2,1)S(1)}, bf16[192,768]{1,0:T(8,128)(2,1)S(1)}, u32[]{:S(2)}, u32[]{:S(2)}) collective-permute-start(bf16[192,768]{1,0:T(8,128)(2,1)S(1)} %copy-done.46), channel_id=1, source_target_pairs={{0,24},{8,16},{16,8},{24,0},{1,25},{9,17},{17,9},{25,1},{2,26},{10... | collective-permute-start | bytes 884744 | tf_op jit(solution)/shard_map/ppermute | solution.py:917
  161.3 22.7 %collective-permute-start.19 = (bf16[768,768]{1,0:T(8,128)(2,1)}, bf16[768,768]{1,0:T(8,128)(2,1)}, u32[]{:S(2)}, u32[]{:S(2)}) collective-permute-start(bf16[768,768]{1,0:T(8,128)(2,1)} %get-tuple-element.118), channel_id=1, source_target_pairs={{0,8},{8,0},{16,24},{24,16},{1,9},{9,1},{17,25},{25,17},{2,10},{10... | collective-permute-start | bytes 3538952 | tf_op jit(solution)/shard_map/ppermute | solution.py:917
  162.2 21.9 %collective-permute-start.20 = (bf16[576,768]{1,0:T(8,128)(2,1)S(1)}, bf16[576,768]{1,0:T(8,128)(2,1)S(1)}, u32[]{:S(2)}, u32[]{:S(2)}) collective-permute-start(bf16[576,768]{1,0:T(8,128)(2,1)S(1)} %copy-done.39), channel_id=1, source_target_pairs={{0,24},{8,16},{16,8},{24,0},{1,25},{9,17},{17,9},{25,1},{2,26},{10... | collective-permute-start | bytes 2654216 | tf_op jit(solution)/shard_map/ppermute | solution.py:917
  178.8 24.0 %collective-permute-start.21 = (bf16[576,768]{1,0:T(8,128)(2,1)}, bf16[576,768]{1,0:T(8,128)(2,1)}, u32[]{:S(2)}, u32[]{:S(2)}) collective-permute-start(bf16[576,768]{1,0:T(8,128)(2,1)} %get-tuple-element.113), channel_id=1, source_target_pairs={{0,16},{8,24},{16,0},{24,8},{1,17},{9,25},{17,1},{25,9},{2,18},{10... | collective-permute-start | bytes 2654216 | tf_op jit(solution)/shard_map/ppermute | solution.py:917
  202.8 43.1 %all-to-all-start.4 = ((bf16[8,48,1536]{2,1,0:T(8,128)(2,1)}), bf16[8,48,1536]{2,1,0:T(8,128)(2,1)S(1)}, u32[]{:S(2)}, u32[]{:S(2)}) async-start(bf16[8,48,1536]{2,1,0:T(8,128)(2,1)} %bitcast.134), calls=%async_computation.4 | async-start | bytes 2359296 | tf_op jit(solution)/shard_map/all_to_all | solution.py:935
  220.2 35.5 %collective-permute-start.23 = (bf16[768,768]{1,0:T(8,128)(2,1)}, bf16[768,768]{1,0:T(8,128)(2,1)S(1)}, u32[]{:S(2)}, u32[]{:S(2)}) collective-permute-start(bf16[768,768]{1,0:T(8,128)(2,1)} %get-tuple-element.129), channel_id=1, source_target_pairs={{0,24},{8,16},{16,8},{24,0},{1,25},{9,17},{17,9},{25,1},{2,26},{10... | collective-permute-start | bytes 3538952 | tf_op jit(solution)/shard_map/ppermute | solution.py:917
  226.9 28.8 %collective-permute-start.22 = (bf16[192,768]{1,0:T(8,128)(2,1)}, bf16[192,768]{1,0:T(8,128)(2,1)}, u32[]{:S(2)}, u32[]{:S(2)}) collective-permute-start(bf16[192,768]{1,0:T(8,128)(2,1)} %get-tuple-element.128), channel_id=1, source_target_pairs={{0,16},{8,24},{16,0},{24,8},{1,17},{9,25},{17,1},{25,9},{2,18},{10... | collective-permute-start | bytes 884744 | tf_op jit(solution)/shard_map/ppermute | solution.py:917
  256.1 23.0 %collective-permute-start.26 = (bf16[384,640]{1,0:T(8,128)(2,1)S(1)}, bf16[384,640]{1,0:T(8,128)(2,1)S(1)}, u32[]{:S(2)}, u32[]{:S(2)}) collective-permute-start(bf16[384,640]{1,0:T(8,128)(2,1)S(1)} %get-tuple-element.133), channel_id=1, source_target_pairs={{0,24},{8,16},{16,8},{24,0},{1,25},{9,17},{17,9},{25,1},{2,26},{10... | collective-permute-start | bytes 1474568 | tf_op jit(solution)/shard_map/ppermute | solution.py:917
  279.2 40.7 %collective-permute-start.28 = (bf16[192,3072]{1,0:T(8,128)(2,1)}, bf16[192,3072]{1,0:T(8,128)(2,1)S(1)}, u32[]{:S(2)}, u32[]{:S(2)}) collective-permute-start(bf16[192,3072]{1,0:T(8,128)(2,1)} %get-tuple-element.144), channel_id=1, source_target_pairs={{0,16},{8,24},{16,0},{24,8},{1,17},{9,25},{17,1},{25,9},{2,18},{10... | collective-permute-start | bytes 3538952 | tf_op jit(solution)/shard_map/ppermute | solution.py:917
  280.8 39.0 %collective-permute-start.27 = (bf16[96,3072]{1,0:T(8,128)(2,1)}, bf16[96,3072]{1,0:T(8,128)(2,1)}, u32[]{:S(2)}, u32[]{:S(2)}) collective-permute-start(bf16[96,3072]{1,0:T(8,128)(2,1)} %get-tuple-element.142), channel_id=1, source_target_pairs={{0,24},{8,16},{16,8},{24,0},{1,25},{9,17},{17,9},{25,1},{2,26},{10... | collective-permute-start | bytes 1769480 | tf_op jit(solution)/shard_map/ppermute | solution.py:917
  319.8 37.7 %all-to-all-start.5 = ((bf16[8,112,768]{2,1,0:T(8,128)(2,1)}), bf16[8,112,768]{2,1,0:T(8,128)(2,1)}, u32[]{:S(2)}, u32[]{:S(2)}) async-start(bf16[8,112,768]{2,1,0:T(8,128)(2,1)} %get-tuple-element.149), calls=%async_computation.5 | async-start | bytes 2752512 | tf_op jit(solution)/shard_map/all_to_all | solution.py:935
  326.9 20.6 %collective-permute-start.31 = (bf16[208,1024]{1,0:T(8,128)(2,1)S(1)}, bf16[208,1024]{1,0:T(8,128)(2,1)S(1)}, u32[]{:S(2)}, u32[]{:S(2)}) collective-permute-start(bf16[208,1024]{1,0:T(8,128)(2,1)S(1)} %copy-done.66), channel_id=1, source_target_pairs={{0,24},{8,16},{16,8},{24,0},{1,25},{9,17},{17,9},{25,1},{2,26},{10... | collective-permute-start | bytes 1277960 | tf_op jit(solution)/shard_map/ppermute | solution.py:917
  338.7 28.5 %collective-permute-start.37 = (bf16[192,3072]{1,0:T(8,128)(2,1)}, bf16[192,3072]{1,0:T(8,128)(2,1)S(1)}, u32[]{:S(2)}, u32[]{:S(2)}) collective-permute-start(bf16[192,3072]{1,0:T(8,128)(2,1)} %get-tuple-element.152), channel_id=1, source_target_pairs={{0,8},{8,0},{16,24},{24,16},{1,9},{9,1},{17,25},{25,17},{2,10},{10... | collective-permute-start | bytes 3538952 | tf_op jit(solution)/shard_map/ppermute | solution.py:917
  (95 other events, 956.0 us)

commit v4 on v3

--- a/solution.py
+++ b/solution.py
@@ -642,11 +642,13 @@
                 [pieces_of(dqkv, w * part + b * band) for w in range(3)], axis=0
             )
             da_part = pieces_of(da_ref, b * band)
+            whole = jnp.concatenate(
+                [mm(n1_ref[...], three, NT), mm(ofull_ref[...], da_part, NT)], axis=1
+            ).astype(BF16)
             for c in range(cols):
-                rows = slice(c * band, (c + 1) * band)
-                proj_ref[c, :band, b * 4 * band : (b + 1) * 4 * band] = jnp.concatenate(
-                    [mm(n1_ref[rows, :], three, NT), mm(ofull_ref[rows, :], da_part, NT)], axis=1
-                ).astype(BF16)
+                proj_ref[c, :band, b * 4 * band : (b + 1) * 4 * band] = whole[
+                    c * band : (c + 1) * band
+                ]
         for c in range(cols):
             own = jnp.concatenate([router[c * share : (c + 1) * share], pad], axis=1)
             facts = jnp.concatenate([own, small], axis=0)
@@ -1040,18 +1042,20 @@
     lane_cut = lambda array, count, k: lax.dynamic_slice_in_dim(array, (me ^ k) * count, count, 1)
     half = part // 2
     in_first = send(lane_cut(after(w_in, tok_far)[:half], hidden_width, 2), 2)
-    qkv_cols = after(qkv_cols, idx_far, cot_far, in_first)
+    eout_half = w_expert_out.shape[0] // 4
+    later_eout = after(w_expert_out, tok_far)
+    eout_cuts = [lane_cut(later_eout, width, k) for k in range(3)]
+    eout_cuts.append(lane_cut(later_eout[:eout_half], width, 3))
+    eout_cuts.append(lane_cut(later_eout[eout_half:], width, 3))
+    later_in = after(w_in, tok_far)
+    second_cut = lane_cut(later_in[half:], hidden_width, 2)
+    in_cuts = {k: lane_cut(later_in, hidden_width, k) for k in (1, 3)}
+    cuts = (*eout_cuts, second_cut, in_cuts[1], in_cuts[3])
+    qkv_cols = after(qkv_cols, idx_far, cot_far, in_first, *cuts)
     out_part = after(jnp.concatenate([w_out, w_router], axis=1), qkv_cols)
     out_gathered = col_gather(out_part)
     qkv_cols = qkv_cols.reshape(rows, share, part, 3 * out_cols)
     qkv_held = trade(lambda d: lax.dynamic_index_in_dim(qkv_cols, d, 0, keepdims=False))
-    second_cut = lane_cut(after(w_in, qkv_cols)[half:], hidden_width, 2)
-    eout_half = w_expert_out.shape[0] // 4
-    later_eout = after(w_expert_out, qkv_cols)
-    eout_cuts = [lane_cut(later_eout, width, k) for k in range(3)]
-    eout_cuts.append(lane_cut(later_eout[:eout_half], width, 3))
-    eout_cuts.append(lane_cut(later_eout[eout_half:], width, 3))
-    qkv_held = after(tuple(qkv_held), *eout_cuts)
     qkv_own = jnp.transpose(
         lay(qkv_held).reshape(rows, share, part, 3, out_cols), (0, 2, 3, 1, 4)
     ).reshape(width, 3 * part)
@@ -1067,16 +1071,15 @@
     slot = (expert_ids % rows) * slots + (expert_ids // rows) * CAPACITY + slot_rank
     choose = (jnp.arange(slots, dtype=I32)[:, None] + me * slots == slot[None, :]).astype(BF16)
 
-    x = tok_low.astype(F32)
+    x = after(tok_low, qkv_cols).astype(F32)
     r1 = lax.rsqrt(jnp.mean(x * x, axis=0) + NORM_EPS)
     n1 = (x * r1 * gain_one[:, None]).astype(BF16)
     qkv = mm(qkv_own, n1, TN).astype(BF16)
-    later_in = after(w_in, tok_low)
     in_places = ((0, 0), (2, 0), (2, half), (3, 0), (1, 0))
     in_second = send(after(second_cut, qkv), 2)
-    in_held = [lane_cut(later_in, hidden_width, 0), in_first, in_second]
+    in_held = [lane_cut(after(w_in, qkv), hidden_width, 0), in_first, in_second]
     for k in (3, 1):
-        in_held.append(send(after(lane_cut(later_in, hidden_width, k), qkv), k))
+        in_held.append(send(after(in_cuts[k], qkv), k))
     qkv, n1, qkv_own = lax.optimization_barrier((qkv, n1, qkv_own))
     q, k, v = qkv[:part], qkv[part : 2 * part], qkv[2 * part :]
     table = lax.dynamic_slice_in_dim(jnp.transpose(bias_table), me * heads, heads, 0)
@@ -1085,7 +1088,7 @@
     )
     o32, p = attend(q, k, v, idx, table, heads, 256)
     expert_at = lambda a: swap(a.reshape(cols, CAPACITY, width), "col").reshape(slots, width)
-    dy_low = mm(choose, cot_low, NT).astype(BF16)
+    dy_low = mm(choose, after(cot_low, qkv), NT).astype(BF16)
     o_low = after(o32.astype(BF16), in_second, in_held[3])
     dy_slots = expert_at(dy_low)
     o_far = send(o_low, 2)

time: 386 us -> 381 us (0.987); the launches traced: 385 us -> 375 us
  starting transfers between devices: 87.7 us -> 74.2 us
  local copies, waits for them, and re-layouts: 39.2 us -> 47.6 us
  waiting for transfers between devices: 126 us -> 121 us
    all_to_all x6, starting transfers between devices: 44.7 us -> 32.9 us  [swap(): return lax.all_to_all(blocks, axis, 0, 0)]
    dynamic_update_slice x4 -> x3, local copies, waits for them, and re-layouts: 0.11 us -> 4.36 us  [lay(): out = lax.dynamic_update_slice_in_dim(out, piece[None], me ^ k, 0)]
    unnamed x141 -> x129, local copies, waits for them, and re-layouts: 8.12 us -> 7.22 us
    dynamic_slice x6 -> x7, local copies, waits for them, and re-layouts: 8.5 us -> 8.66 us  [expert_plan(): lax.dynamic_slice_in_dim(array, (me ^ k) * count, count, 1)]
  transfers between devices with their start and end apart: 46 -> 46, of which waited for: 18 -> 19; matrix products, arithmetic and copies ran while one was open for 17% -> 20% of each run, Pallas kernels for 25% -> 25%
where the time goes in v4:
time: 381 us; the launch traced here: 375 us
  waiting for transfers between devices  121 us (32%)
  Pallas kernels  94.9 us (25%)
  starting transfers between devices  74.2 us (19%)
  local copies, waits for them, and re-layouts  47.6 us (12%)
  other arithmetic  23.4 us (6%)
  matrix products  11.9 us (3%)
    ppermute x38, waiting for transfers between devices, send(): return lax.ppermute(piece, 'row', [(i, i ^ offset) for i in range(count)])  91.2 us
    ppermute x38, starting transfers between devices, send(): return lax.ppermute(piece, 'row', [(i, i ^ offset) for i in range(count)])  34.8 us
    all_to_all x6, starting transfers between devices, swap(): return lax.all_to_all(blocks, axis, 0, 0)  32.9 us
    pallas_call x1, Pallas kernels, attend_back(): pl.pallas_call(functools.partial(back_kernel, heads, count, experts, cols...  31.1 us
    all_to_all x6, waiting for transfers between devices, swap(): return lax.all_to_all(blocks, axis, 0, 0)  23.6 us
    pallas_call x1, Pallas kernels, expert_outer(): pl.pallas_call(functools.partial(outer_kernel, count, places, eout_places...  16.5 us
    pallas_call x1, Pallas kernels, attend(): pl.pallas_call(functools.partial(attend_kernel, heads, width // heads), g...  16 us
    pallas_call x1, Pallas kernels, expert_inner(): pl.pallas_call(functools.partial(inner_kernel, count, places, ge_places),...  14.7 us
  transfers between devices with their start and end apart: 46, of which 19 were waited for; matrix products, arithmetic and copies ran while one was open for 20% of the time, Pallas kernels for 25%

profile of v4, /device:TPU:25, one launch (start us, length us, event | category | flops | bytes accessed | tf_op | source)
XLA Modules:
  0.0 375.3 jit_solution(659816158486628797)
XLA Ops:
  4.4 5.6 %all-to-all-start = ((bf16[8,192,288]{1,2,0:T(8,128)(2,1)}), bf16[8,192,288]{1,2,0:T(8,128)(2,1)S(1)}, u32[]{:S(2)}, u32[]{:S(2)}) async-start(bf16[8,192,288]{1,2,0:T(8,128)(2,1)} %broadcast_in_dim.27), calls=%async_computation | async-start | bytes 2359296 | tf_op jit(solution)/shard_map/all_to_all | solution.py:937
  37.0 6.3 %collective-permute-done.3.refs_1_ = bf16[96,3072]{1,0:T(8,128)(2,1)} collective-permute-done((bf16[96,3072]{1,0:T(8,128)(2,1)S(1)}, bf16[96,3072]{1,0:T(8,128)(2,1)}, u32[]{:S(2)}, u32[]{:S(2)}) %collective-permute-start.3) | collective-permute-done | bytes 589856 | tf_op jit(solution)/shard_map/ppermute | solution.py:919
  49.8 5.7 %all-to-all-start.1 = ((bf16[8,192,100]{2,1,0:T(8,128)(2,1)}), bf16[8,192,100]{2,1,0:T(8,128)(2,1)}, u32[]{:S(2)}, u32[]{:S(2)}) async-start(bf16[8,192,100]{2,1,0:T(8,128)(2,1)} %broadcast_in_dim.33), calls=%async_computation.1 | async-start | bytes 786432 | tf_op jit(solution)/shard_map/all_to_all | solution.py:937
  76.0 16.0 %shard_map.238 = (f32[192,1024]{1,0:T(8,128)S(1)}, bf16[3,1024,1024]{2,1,0:T(8,128)(2,1)}) custom-call(bf16[192,1024]{1,0:T(8,128)(2,1)S(1)} %get-tuple-element.233.q_ref, bf16[192,1024]{1,0:T(8,128)(2,1)S(1)} %get-tuple-element.232.k_ref, bf16[192,1024]{1,0:T(8,128)(2,1)S(1)} %get-tuple-element.231.v_ref, bf16[1024,1024]{1,0:T(8,128)(2,1)S(1)} %bitcast.94, ...), custom_call_target="tpu_custom_call" | custom-call | tf_op jit(solution)/shard_map/pallas_call | solution.py:453
  93.0 6.0 %all-to-all-start.2 = ((bf16[8,48,768]{2,1,0:T(8,128)(2,1)}), bf16[8,48,768]{2,1,0:T(8,128)(2,1)}, u32[]{:S(2)}, u32[]{:S(2)}) async-start(bf16[8,48,768]{2,1,0:T(8,128)(2,1)} %bitcast.32), calls=%async_computation.2 | async-start | bytes 1179648 | tf_op jit(solution)/shard_map/all_to_all | solution.py:937
  105.2 6.0 %collective-permute-done.12.refs_3_ = bf16[192,3072]{1,0:T(8,128)(2,1)S(1)} collective-permute-done((bf16[192,3072]{1,0:T(8,128)(2,1)}, bf16[192,3072]{1,0:T(8,128)(2,1)S(1)}, u32[]{:S(2)}, u32[]{:S(2)}) %collective-permute-start.12) | collective-permute-done | bytes 1179680 | tf_op jit(solution)/shard_map/ppermute | solution.py:919
  112.4 5.9 %collective-permute-done.9 = bf16[192,800]{1,0:T(8,128)(2,1)S(1)} collective-permute-done((bf16[192,800]{1,0:T(8,128)(2,1)S(1)}, bf16[192,800]{1,0:T(8,128)(2,1)S(1)}, u32[]{:S(2)}, u32[]{:S(2)}) %collective-permute-start.9) | collective-permute-done | bytes 307232 | tf_op jit(solution)/shard_map/ppermute | solution.py:919
  120.2 6.6 %collective-permute-done.13 = bf16[192,1024]{1,0:T(8,128)(2,1)S(1)} collective-permute-done((bf16[192,1024]{1,0:T(8,128)(2,1)S(1)}, bf16[192,1024]{1,0:T(8,128)(2,1)S(1)}, u32[]{:S(2)}, u32[]{:S(2)}) %collective-permute-start.13) | collective-permute-done | bytes 393248 | tf_op jit(solution)/shard_map/ppermute | solution.py:919
  136.5 5.1 %all-to-all-start.3 = ((bf16[8,48,768]{2,1,0:T(8,128)(2,1)}), bf16[8,48,768]{2,1,0:T(8,128)(2,1)S(1)}, u32[]{:S(2)}, u32[]{:S(2)}) async-start(bf16[8,48,768]{2,1,0:T(8,128)(2,1)} %bitcast.38), calls=%async_computation.3 | async-start | bytes 1179648 | tf_op jit(solution)/shard_map/all_to_all | solution.py:937
  143.3 20.4 %collective-permute-done.17.refs_8_ = bf16[192,768]{1,0:T(8,128)(2,1)S(1)} collective-permute-done((bf16[192,768]{1,0:T(8,128)(2,1)S(1)}, bf16[192,768]{1,0:T(8,128)(2,1)S(1)}, u32[]{:S(2)}, u32[]{:S(2)}) %collective-permute-start.17) | collective-permute-done | bytes 294944 | tf_op jit(solution)/shard_map/ppermute | solution.py:919
  168.4 14.7 %shard_map.239 = (bf16[384,768]{1,0:T(8,128)(2,1)}, bf16[384,3072]{1,0:T(8,128)(2,1)}, bf16[384,3072]{1,0:T(8,128)(2,1)}, bf16[768,768]{1,0:T(8,128)(2,1)}, bf16...) custom-call(s32[2]{0:T(128)} %pad_add_fusion.place_ref, ...), custom_call_target="tpu_custom_call" | custom-call | tf_op jit(solution)/shard_map/pallas_call | solution.py:793
  186.6 16.5 %shard_map.240 = (bf16[384,1536]{1,0:T(8,128)(2,1)}, bf16[192,3072]{1,0:T(8,128)(2,1)}, bf16[192,3072]{1,0:T(8,128)(2,1)}, bf16[192,3072]{1,0:T(8,128)(2,1)}, bf16[192,3072]{1,0:T(8,128)(2,1)}) custom-call(s32[2]{0:T(128)} %pad_add_fusion.place_ref, bf16[384,768]{1,0:T(8,128)(2,1)} %bitcast.113, bf16[384,768]{1,0:T(8,128)(2,1)} %get-tuple-element.103.dys_ref, ...), custom_call_target="tpu_custom_call" | custom-call | tf_op jit(solution)/shard_map/pallas_call | solution.py:821
  204.5 5.1 %all-to-all-start.4 = ((bf16[8,48,1536]{2,1,0:T(8,128)(2,1)}), bf16[8,48,1536]{2,1,0:T(8,128)(2,1)S(1)}, u32[]{:S(2)}, u32[]{:S(2)}) async-start(bf16[8,48,1536]{2,1,0:T(8,128)(2,1)} %bitcast.130), calls=%async_computation.4 | async-start | bytes 2359296 | tf_op jit(solution)/shard_map/all_to_all | solution.py:937
  219.0 17.0 %all-to-all-done.4 = bf16[8,48,1536]{2,1,0:T(8,128)(2,1)S(1)} async-done(((bf16[8,48,1536]{2,1,0:T(8,128)(2,1)}), bf16[8,48,1536]{2,1,0:T(8,128)(2,1)S(1)}, u32[]{:S(2)}, u32[]{:S(2)}) %all-to-all-start.4) | async-done | bytes 1179680 | tf_op jit(solution)/shard_map/all_to_all | solution.py:937
  236.0 5.0 %shard_map.241 = (f32[1,768]{1,0:T(1,128)S(1)}, bf16[384,640]{1,0:T(8,128)(2,1)S(1)}, bf16[384,640]{1,0:T(8,128)(2,1)}, bf16[384,640]{1,0:T(8,128)(2,1)S(1)}, bf16[384,640]{1,0:T(8,128)(2,1)S(1)}) custom-call(s32[2]{0:T(128)S(1)} %copy-done.12, bf16[384,1536]{1,0:T(8,128)(2,1)S(1)} %bitcast.96, bf16[384,768]{1,0:T(8,128)(2,1)} %fusion.10.dy_ref, ...), custom_call_target="tpu_custom_call" | custom-call | tf_op jit(solution)/shard_map/pallas_call | solution.py:901
  241.8 4.2 %collective-permute-done.22 = bf16[192,768]{1,0:T(8,128)(2,1)} collective-permute-done((bf16[192,768]{1,0:T(8,128)(2,1)}, bf16[192,768]{1,0:T(8,128)(2,1)}, u32[]{:S(2)}, u32[]{:S(2)}) %collective-permute-start.22) | collective-permute-done | bytes 294944 | tf_op jit(solution)/shard_map/ppermute | solution.py:919
  248.0 10.6 %collective-permute-done.25.refs_2_ = bf16[384,640]{1,0:T(8,128)(2,1)S(1)} collective-permute-done((bf16[384,640]{1,0:T(8,128)(2,1)S(1)}, bf16[384,640]{1,0:T(8,128)(2,1)S(1)}, u32[]{:S(2)}, u32[]{:S(2)}) %collective-permute-start.25) | collective-permute-done | bytes 491552 | tf_op jit(solution)/shard_map/ppermute | solution.py:919
  258.6 10.9 %collective-permute-done.26.refs_3_ = bf16[384,640]{1,0:T(8,128)(2,1)S(1)} collective-permute-done((bf16[384,640]{1,0:T(8,128)(2,1)S(1)}, bf16[384,640]{1,0:T(8,128)(2,1)S(1)}, u32[]{:S(2)}, u32[]{:S(2)}) %collective-permute-start.26) | collective-permute-done | bytes 491552 | tf_op jit(solution)/shard_map/ppermute | solution.py:919
  276.1 31.1 %shard_map.242 = (bf16[192,1024]{1,0:T(8,128)(2,1)}, bf16[192,1024]{1,0:T(8,128)(2,1)}, bf16[8,112,768]{2,1,0:T(8,128)(2,1)}, bf16[208,1024]{1,0:T(8,128)(2,1)},...) custom-call(s32[2]{0:T(128)} %pad_add_fusion.place_ref, ...), custom_call_target="tpu_custom_call" | custom-call | tf_op jit(solution)/shard_map/pallas_call | solution.py:678
  310.2 5.4 %all-to-all-start.5 = ((bf16[8,112,768]{2,1,0:T(8,128)(2,1)}), bf16[8,112,768]{2,1,0:T(8,128)(2,1)}, u32[]{:S(2)}, u32[]{:S(2)}) async-start(bf16[8,112,768]{2,1,0:T(8,128)(2,1)} %get-tuple-element.143), calls=%async_computation.5 | async-start | bytes 2752512 | tf_op jit(solution)/shard_map/all_to_all | solution.py:937
  321.9 6.8 %shard_map.244 = f32[768,3072]{1,0:T(8,128)} custom-call(s32[1]{0:T(128)} %bitcast.me_ref, bf16[768,768]{1,0:T(8,128)(2,1)S(1)} %copy-done.10, bf16[768,768]{1,0:T(8,128)(2,1)} %collective-permute-done.39.refs_1_, bf16[768,768]{1,0:T(8,128)(2,1)S(1)} %pad_maximum_fusion.11.refs_2_, bf16[768,768]{1,0:T(8,128)(2,1)S(1)} %collective-permute-done.23.refs_3_), custom_call_target="tpu_custom_call" | custom-call | tf_op jit(solution)/shard_map/pallas_call | solution.py:982
  328.9 8.6 %collective-permute-done.31 = bf16[208,1024]{1,0:T(8,128)(2,1)} collective-permute-done((bf16[208,1024]{1,0:T(8,128)(2,1)}, bf16[208,1024]{1,0:T(8,128)(2,1)}, u32[]{:S(2)}, u32[]{:S(2)}) %collective-permute-start.31) | collective-permute-done | bytes 426016 | tf_op jit(solution)/shard_map/ppermute | solution.py:919
  341.1 6.7 %all-to-all-done.5 = bf16[8,112,768]{2,1,0:T(8,128)(2,1)} async-done(((bf16[8,112,768]{2,1,0:T(8,128)(2,1)}), bf16[8,112,768]{2,1,0:T(8,128)(2,1)}, u32[]{:S(2)}, u32[]{:S(2)}) %all-to-all-start.5) | async-done | bytes 1376288 | tf_op jit(solution)/shard_map/all_to_all | solution.py:937
  361.3 4.8 %shard_map.243 = f32[192,12288]{1,0:T(8,128)} custom-call(s32[1]{0:T(128)} %bitcast.me_ref, bf16[192,3072]{1,0:T(8,128)(2,1)S(1)} %copy-done.9, bf16[192,3072]{1,0:T(8,128)(2,1)S(1)} %collective-permute-done.37.refs_1_, bf16[192,3072]{1,0:T(8,128)(2,1)S(1)} %collective-permute-done.28.refs_2_, bf16[192,3072]{1,0:T(8,128)(2,1)S(1)} %pad_maximum_fusion.10.refs_3_), custom_call_target="tpu_custom_call" | custom-call | tf_op jit(solution)/shard_map/pallas_call | solution.py:982
  (316 shorter events, 142.4 us)
Async XLA Ops:
  1.9 23.9 %collective-permute-start.2 = (bf16[192,1024]{1,0:T(8,128)(2,1)}, bf16[192,1024]{1,0:T(8,128)(2,1)S(1)}, u32[]{:S(2)}, u32[]{:S(2)}) collective-permute-start(bf16[192,1024]{1,0:T(8,128)(2,1)} %bitcast.121), channel_id=1, source_target_pairs={{0,16},{8,24},{16,0},{24,8},{1,17},{9,25},{17,1},{25,9},{2,18},{10... | collective-permute-start | bytes 1179656 | tf_op jit(solution)/shard_map/ppermute | solution.py:919
  4.4 38.9 %all-to-all-start = ((bf16[8,192,288]{1,2,0:T(8,128)(2,1)}), bf16[8,192,288]{1,2,0:T(8,128)(2,1)S(1)}, u32[]{:S(2)}, u32[]{:S(2)}) async-start(bf16[8,192,288]{1,2,0:T(8,128)(2,1)} %broadcast_in_dim.27), calls=%async_computation | async-start | bytes 2359296 | tf_op jit(solution)/shard_map/all_to_all | solution.py:937
  21.1 22.2 %collective-permute-start.3 = (bf16[96,3072]{1,0:T(8,128)(2,1)S(1)}, bf16[96,3072]{1,0:T(8,128)(2,1)}, u32[]{:S(2)}, u32[]{:S(2)}) collective-permute-start(bf16[96,3072]{1,0:T(8,128)(2,1)S(1)} %constant_dynamic-slice_fusion.33), channel_id=1, source_target_pairs={{0,16},{8,24},{16,0},{24,8},{1,17},{9,25},{17,1},{25,9},{2,18},{10... | collective-permute-start | bytes 1769480 | tf_op jit(solution)/shard_map/ppermute | solution.py:919
  31.7 42.0 %collective-permute-start.8 = (bf16[2,256,1024]{2,1,0:T(8,128)(2,1)}, bf16[2,256,1024]{2,1,0:T(8,128)(2,1)}, u32[]{:S(2)}, u32[]{:S(2)}) collective-permute-start(bf16[2,256,1024]{2,1,0:T(8,128)(2,1)} %pad_maximum_fusion.12), channel_id=1, source_target_pairs={{0,8},{8,0},{16,24},{24,16},{1,9},{9,1},{17,25},{25,17},{2,10},{10... | collective-permute-start | bytes 3145736 | tf_op jit(solution)/shard_map/ppermute | solution.py:919
  49.8 43.2 %all-to-all-start.1 = ((bf16[8,192,100]{2,1,0:T(8,128)(2,1)}), bf16[8,192,100]{2,1,0:T(8,128)(2,1)}, u32[]{:S(2)}, u32[]{:S(2)}) async-start(bf16[8,192,100]{2,1,0:T(8,128)(2,1)} %broadcast_in_dim.33), calls=%async_computation.1 | async-start | bytes 786432 | tf_op jit(solution)/shard_map/all_to_all | solution.py:937
  70.3 34.9 %collective-permute-start.11 = (bf16[96,3072]{1,0:T(8,128)(2,1)}, bf16[96,3072]{1,0:T(8,128)(2,1)}, u32[]{:S(2)}, u32[]{:S(2)}) collective-permute-start(bf16[96,3072]{1,0:T(8,128)(2,1)} %constant_dynamic-slice_fusion.27), channel_id=1, source_target_pairs={{0,16},{8,24},{16,0},{24,8},{1,17},{9,25},{17,1},{25,9},{2,18},{10... | collective-permute-start | bytes 1769480 | tf_op jit(solution)/shard_map/ppermute | solution.py:919
  71.6 39.6 %collective-permute-start.12 = (bf16[192,3072]{1,0:T(8,128)(2,1)}, bf16[192,3072]{1,0:T(8,128)(2,1)S(1)}, u32[]{:S(2)}, u32[]{:S(2)}) collective-permute-start(bf16[192,3072]{1,0:T(8,128)(2,1)} %get-tuple-element.92), channel_id=1, source_target_pairs={{0,24},{8,16},{16,8},{24,0},{1,25},{9,17},{17,9},{25,1},{2,26},{10... | collective-permute-start | bytes 3538952 | tf_op jit(solution)/shard_map/ppermute | solution.py:919
  93.0 27.2 %all-to-all-start.2 = ((bf16[8,48,768]{2,1,0:T(8,128)(2,1)}), bf16[8,48,768]{2,1,0:T(8,128)(2,1)}, u32[]{:S(2)}, u32[]{:S(2)}) async-start(bf16[8,48,768]{2,1,0:T(8,128)(2,1)} %bitcast.32), calls=%async_computation.2 | async-start | bytes 1179648 | tf_op jit(solution)/shard_map/all_to_all | solution.py:937
  129.4 34.3 %collective-permute-start.16 = (bf16[768,768]{1,0:T(8,128)(2,1)}, bf16[768,768]{1,0:T(8,128)(2,1)}, u32[]{:S(2)}, u32[]{:S(2)}) collective-permute-start(bf16[768,768]{1,0:T(8,128)(2,1)} %get-tuple-element.98), channel_id=1, source_target_pairs={{0,16},{8,24},{16,0},{24,8},{1,17},{9,25},{17,1},{25,9},{2,18},{10... | collective-permute-start | bytes 3538952 | tf_op jit(solution)/shard_map/ppermute | solution.py:919
  136.5 27.1 %all-to-all-start.3 = ((bf16[8,48,768]{2,1,0:T(8,128)(2,1)}), bf16[8,48,768]{2,1,0:T(8,128)(2,1)S(1)}, u32[]{:S(2)}, u32[]{:S(2)}) async-start(bf16[8,48,768]{2,1,0:T(8,128)(2,1)} %bitcast.38), calls=%async_computation.3 | async-start | bytes 1179648 | tf_op jit(solution)/shard_map/all_to_all | solution.py:937
  141.6 26.8 %collective-permute-start.18 = (bf16[192,3072]{1,0:T(8,128)(2,1)}, bf16[192,3072]{1,0:T(8,128)(2,1)}, u32[]{:S(2)}, u32[]{:S(2)}) collective-permute-start(bf16[192,3072]{1,0:T(8,128)(2,1)} %get-tuple-element.102), channel_id=1, source_target_pairs={{0,8},{8,0},{16,24},{24,16},{1,9},{9,1},{17,25},{25,17},{2,10},{10... | collective-permute-start | bytes 3538952 | tf_op jit(solution)/shard_map/ppermute | solution.py:919
  142.5 21.2 %collective-permute-start.17 = (bf16[192,768]{1,0:T(8,128)(2,1)S(1)}, bf16[192,768]{1,0:T(8,128)(2,1)S(1)}, u32[]{:S(2)}, u32[]{:S(2)}) collective-permute-start(bf16[192,768]{1,0:T(8,128)(2,1)S(1)} %copy-done.44), channel_id=1, source_target_pairs={{0,24},{8,16},{16,8},{24,0},{1,25},{9,17},{17,9},{25,1},{2,26},{10... | collective-permute-start | bytes 884744 | tf_op jit(solution)/shard_map/ppermute | solution.py:919
  163.7 21.6 %collective-permute-start.20 = (bf16[576,768]{1,0:T(8,128)(2,1)S(1)}, bf16[576,768]{1,0:T(8,128)(2,1)S(1)}, u32[]{:S(2)}, u32[]{:S(2)}) collective-permute-start(bf16[576,768]{1,0:T(8,128)(2,1)S(1)} %copy-done.36), channel_id=1, source_target_pairs={{0,24},{8,16},{16,8},{24,0},{1,25},{9,17},{17,9},{25,1},{2,26},{10... | collective-permute-start | bytes 2654216 | tf_op jit(solution)/shard_map/ppermute | solution.py:919
  183.1 21.3 %collective-permute-start.21 = (bf16[576,768]{1,0:T(8,128)(2,1)}, bf16[576,768]{1,0:T(8,128)(2,1)}, u32[]{:S(2)}, u32[]{:S(2)}) collective-permute-start(bf16[576,768]{1,0:T(8,128)(2,1)} %get-tuple-element.107), channel_id=1, source_target_pairs={{0,16},{8,24},{16,0},{24,8},{1,17},{9,25},{17,1},{25,9},{2,18},{10... | collective-permute-start | bytes 2654216 | tf_op jit(solution)/shard_map/ppermute | solution.py:919
  204.5 31.5 %all-to-all-start.4 = ((bf16[8,48,1536]{2,1,0:T(8,128)(2,1)}), bf16[8,48,1536]{2,1,0:T(8,128)(2,1)S(1)}, u32[]{:S(2)}, u32[]{:S(2)}) async-start(bf16[8,48,1536]{2,1,0:T(8,128)(2,1)} %bitcast.130), calls=%async_computation.4 | async-start | bytes 2359296 | tf_op jit(solution)/shard_map/all_to_all | solution.py:937
  210.7 35.4 %collective-permute-start.23 = (bf16[768,768]{1,0:T(8,128)(2,1)}, bf16[768,768]{1,0:T(8,128)(2,1)S(1)}, u32[]{:S(2)}, u32[]{:S(2)}) collective-permute-start(bf16[768,768]{1,0:T(8,128)(2,1)} %get-tuple-element.123), channel_id=1, source_target_pairs={{0,24},{8,16},{16,8},{24,0},{1,25},{9,17},{17,9},{25,1},{2,26},{10... | collective-permute-start | bytes 3538952 | tf_op jit(solution)/shard_map/ppermute | solution.py:919
  217.3 28.7 %collective-permute-start.22 = (bf16[192,768]{1,0:T(8,128)(2,1)}, bf16[192,768]{1,0:T(8,128)(2,1)}, u32[]{:S(2)}, u32[]{:S(2)}) collective-permute-start(bf16[192,768]{1,0:T(8,128)(2,1)} %get-tuple-element.122), channel_id=1, source_target_pairs={{0,16},{8,24},{16,0},{24,8},{1,17},{9,25},{17,1},{25,9},{2,18},{10... | collective-permute-start | bytes 884744 | tf_op jit(solution)/shard_map/ppermute | solution.py:919
  246.8 22.7 %collective-permute-start.26 = (bf16[384,640]{1,0:T(8,128)(2,1)S(1)}, bf16[384,640]{1,0:T(8,128)(2,1)S(1)}, u32[]{:S(2)}, u32[]{:S(2)}) collective-permute-start(bf16[384,640]{1,0:T(8,128)(2,1)S(1)} %get-tuple-element.127), channel_id=1, source_target_pairs={{0,24},{8,16},{16,8},{24,0},{1,25},{9,17},{17,9},{25,1},{2,26},{10... | collective-permute-start | bytes 1474568 | tf_op jit(solution)/shard_map/ppermute | solution.py:919
  269.6 40.7 %collective-permute-start.28 = (bf16[192,3072]{1,0:T(8,128)(2,1)}, bf16[192,3072]{1,0:T(8,128)(2,1)S(1)}, u32[]{:S(2)}, u32[]{:S(2)}) collective-permute-start(bf16[192,3072]{1,0:T(8,128)(2,1)} %get-tuple-element.138), channel_id=1, source_target_pairs={{0,16},{8,24},{16,0},{24,8},{1,17},{9,25},{17,1},{25,9},{2,18},{10... | collective-permute-start | bytes 3538952 | tf_op jit(solution)/shard_map/ppermute | solution.py:919
  271.5 38.7 %collective-permute-start.27 = (bf16[96,3072]{1,0:T(8,128)(2,1)}, bf16[96,3072]{1,0:T(8,128)(2,1)}, u32[]{:S(2)}, u32[]{:S(2)}) collective-permute-start(bf16[96,3072]{1,0:T(8,128)(2,1)} %get-tuple-element.136), channel_id=1, source_target_pairs={{0,24},{8,16},{16,8},{24,0},{1,25},{9,17},{17,9},{25,1},{2,26},{10... | collective-permute-start | bytes 1769480 | tf_op jit(solution)/shard_map/ppermute | solution.py:919
  310.2 37.5 %all-to-all-start.5 = ((bf16[8,112,768]{2,1,0:T(8,128)(2,1)}), bf16[8,112,768]{2,1,0:T(8,128)(2,1)}, u32[]{:S(2)}, u32[]{:S(2)}) async-start(bf16[8,112,768]{2,1,0:T(8,128)(2,1)} %get-tuple-element.143), calls=%async_computation.5 | async-start | bytes 2752512 | tf_op jit(solution)/shard_map/all_to_all | solution.py:937
  317.3 20.2 %collective-permute-start.31 = (bf16[208,1024]{1,0:T(8,128)(2,1)}, bf16[208,1024]{1,0:T(8,128)(2,1)}, u32[]{:S(2)}, u32[]{:S(2)}) collective-permute-start(bf16[208,1024]{1,0:T(8,128)(2,1)} %get-tuple-element.142), channel_id=1, source_target_pairs={{0,24},{8,16},{16,8},{24,0},{1,25},{9,17},{17,9},{25,1},{2,26},{10... | collective-permute-start | bytes 1277960 | tf_op jit(solution)/shard_map/ppermute | solution.py:919
  318.2 20.4 %collective-permute-start.29 = (bf16[208,1024]{1,0:T(8,128)(2,1)}, bf16[208,1024]{1,0:T(8,128)(2,1)}, u32[]{:S(2)}, u32[]{:S(2)}) collective-permute-start(bf16[208,1024]{1,0:T(8,128)(2,1)} %get-tuple-element.140), channel_id=1, source_target_pairs={{0,8},{8,0},{16,24},{24,16},{1,9},{9,1},{17,25},{25,17},{2,10},{10... | collective-permute-start | bytes 1277960 | tf_op jit(solution)/shard_map/ppermute | solution.py:919
  328.7 28.9 %collective-permute-start.37 = (bf16[192,3072]{1,0:T(8,128)(2,1)}, bf16[192,3072]{1,0:T(8,128)(2,1)S(1)}, u32[]{:S(2)}, u32[]{:S(2)}) collective-permute-start(bf16[192,3072]{1,0:T(8,128)(2,1)} %get-tuple-element.146), channel_id=1, source_target_pairs={{0,8},{8,0},{16,24},{24,16},{1,9},{9,1},{17,25},{25,17},{2,10},{10... | collective-permute-start | bytes 3538952 | tf_op jit(solution)/shard_map/ppermute | solution.py:919
  (87 other events, 910.7 us)
